TPU v7x, 256 devices: a whole 4x4x8 slice. The times are simulated.
256 devices in a mesh: lon: 64 (over z, y, x_hi), lat: 4 (over x_lo, core).
Axes of the slice: x: 4 (x_hi: 2, x_lo: 2; x = x_hi * 2 + x_lo), y: 4, z: 8, core: 2. Of those that a mesh axis runs over, the one named last changes fastest.
Arguments:
- block_input: bfloat16 [4, 24, 2304, 192], P(None, 'lat', 'lon'), may hold values from -200 to 200
- grad_out: bfloat16 [4, 24, 2304, 192], P(None, 'lat', 'lon'), may hold values from -30 to 30
- ln_gain: float32 [192], replicated, may hold values from 0.1 to 1.9
- w_qkv: bfloat16 [192, 576], replicated, may hold values from -0.4375 to 0.4375
- w_proj: bfloat16 [192, 192], replicated, may hold values from -0.4375 to 0.4375
- bias_table: float32 [4, 2, 6, 3312], P('lat'), may hold values from -305 to 305
Outputs:
- grad_x: bfloat16 [4, 24, 2304, 192], P(None, 'lat', 'lon')
- grad_gain: float32 [192], replicated
- grad_wqkv: float32 [192, 576], replicated
- grad_wproj: float32 [192, 192], replicated
- grad_bias: float32 [4, 2, 6, 3312], P('lat')
All inputs are finite; a program needn't handle non-finite values.
Results may differ from a plain program's by a relative error of at most 0.009.
Values may be sent and summed in bfloat16 or wider, within the bound.
No kernel may reach another device: no remote copies, remote signals or barrier semaphores. Data moves between devices by JAX's collectives and lax.ppermute only.
A program may use at most 64 MiB of HBM per device.

v0:
```python
import jax
import jax.numpy as jnp
from jax import lax
from jax.sharding import PartitionSpec as P

HEAD_DIM = 32
WZ = 2
WLAT = 6
WLON = 12
WIN = 144
TABLE = 3312


def swapped(value, axis, bit):
    mask = 2**bit
    pairs = [(source, source ^ mask) for source in range(lax.axis_size(axis))]
    return lax.ppermute(value, axis, pairs)


def from_behind(block, axis, distance):
    devices = range(lax.axis_size(axis))
    route = [((i - distance) % len(devices), i) for i in devices]
    return lax.ppermute(block, axis, route)


def relation_table():
    positions = jnp.arange(WLON * WLON)
    first = positions // WLON
    second = positions % WLON
    offsets = second - first + WLON - 1
    return (offsets[:, None] == jnp.arange(2 * WLON - 1)[None, :]).astype(jnp.float32)


def expand_bias(table):
    leading = table.shape[:-1]
    count = len(leading)
    pairs = table.reshape(leading + (WZ * WZ * WLAT * WLAT, 2 * WLON - 1))
    dense = jnp.einsum("...pr,qr->...pq", pairs, relation_table(), precision=lax.Precision.HIGHEST)
    dense = dense.reshape(leading + (WZ, WZ, WLAT, WLAT, WLON, WLON))
    order = tuple(range(count)) + (count, count + 2, count + 4, count + 1, count + 3, count + 5)
    return dense.transpose(order).reshape(leading + (WIN, WIN))


def reduce_bias(dense):
    leading = dense.shape[:-2]
    count = len(leading)
    split = dense.reshape(leading + (WZ, WLAT, WLON, WZ, WLAT, WLON))
    order = tuple(range(count)) + (count, count + 3, count + 1, count + 4, count + 2, count + 5)
    grouped = split.transpose(order).reshape(leading + (WZ * WZ * WLAT * WLAT, WLON * WLON))
    summed = jnp.einsum(
        "...pq,qr->...pr", grouped, relation_table(), precision=lax.Precision.HIGHEST
    )
    return summed.reshape(leading + (TABLE,))


def to_windows(grid):
    depth, height, breadth, features = grid.shape
    split = grid.reshape(depth // WZ, WZ, height // WLAT, WLAT, breadth // WLON, WLON, features)
    return split.transpose(0, 2, 4, 1, 3, 5, 6).reshape(
        depth // WZ, height // WLAT, breadth // WLON, WIN, features
    )


def from_windows(blocks):
    levels, bands, strips, window, features = blocks.shape
    split = blocks.reshape(levels, bands, strips, WZ, WLAT, WLON, features)
    return split.transpose(0, 3, 1, 4, 2, 5, 6).reshape(
        levels * WZ, bands * WLAT, strips * WLON, features
    )


def allowed_pairs(last_level, last_band):
    positions = jnp.arange(WIN)
    level = positions // (WLAT * WLON)
    band = positions // WLON % WLAT
    upper = (level >= WZ - WZ // 2).astype(jnp.int32)
    edge = (band >= WLAT - WLAT // 2).astype(jnp.int32)
    region = 2 * upper[None, :] * last_level[:, None] + edge[None, :] * last_band[:, None]
    return region[:, :, None] == region[:, None, :]


def window_grads(projected, grad_mixed, bias, allowed):
    bands, strips, window, triple = projected.shape
    width = triple // 3
    heads = bias.shape[1]
    size = width // heads
    scale = HEAD_DIM ** (-0.5)
    split = (bands, strips, window, heads, size)
    query = projected[..., :width].reshape(split)
    key_rows = projected[..., width : 2 * width].reshape(split)
    value_rows = projected[..., 2 * width :].reshape(split)
    grad_heads = grad_mixed.reshape(split)
    scores = (
        jnp.einsum("abihd,abjhd->abhij", query, key_rows, preferred_element_type=jnp.float32)
        * scale
        + bias[:, None]
    )
    scores = jnp.where(allowed[:, None, None], scores, -1e30)
    top = jnp.max(scores, axis=-1, keepdims=True)
    powers = jnp.exp(scores - top)
    attend = powers / jnp.sum(powers, axis=-1, keepdims=True)
    attend_half = attend.astype(jnp.bfloat16)
    outputs = jnp.einsum(
        "abhij,abjhd->abihd", attend_half, value_rows, preferred_element_type=jnp.float32
    ).astype(jnp.bfloat16)
    grad_value = jnp.einsum(
        "abhij,abihd->abjhd", attend_half, grad_heads, preferred_element_type=jnp.float32
    ).astype(jnp.bfloat16)
    grad_attend = jnp.einsum(
        "abihd,abjhd->abhij", grad_heads, value_rows, preferred_element_type=jnp.float32
    )
    total = jnp.sum(attend * grad_attend, axis=-1, keepdims=True)
    grad_scores = attend * (grad_attend - total)
    grad_half = grad_scores.astype(jnp.bfloat16)
    grad_query = (
        jnp.einsum("abhij,abjhd->abihd", grad_half, key_rows, preferred_element_type=jnp.float32)
        * scale
    ).astype(jnp.bfloat16)
    grad_key = (
        jnp.einsum("abhij,abihd->abjhd", grad_half, query, preferred_element_type=jnp.float32)
        * scale
    ).astype(jnp.bfloat16)
    shape = (bands, strips, window, width)
    grad_projected = jnp.concatenate(
        [grad_query.reshape(shape), grad_key.reshape(shape), grad_value.reshape(shape)], axis=-1
    )
    return (outputs.reshape(shape), grad_projected, jnp.sum(grad_scores, axis=1))


def lon_ahead(stacked):
    half = WLON // 2
    arriving = swapped(stacked[:, :, :, :half], "lon", 0)
    return jnp.concatenate([stacked[:, :, :, half:], arriving], axis=3)


def band_ahead(stacked):
    half = WLAT // 2
    arriving = from_behind(stacked[:, :, :half], "lat", -1)
    return jnp.concatenate([stacked[:, :, half:], arriving], axis=2)


def band_back(grid):
    half = WLAT // 2
    height = grid.shape[1]
    arriving = from_behind(grid[:, height - half :], "lat", 1)
    return jnp.concatenate([arriving, grid[:, : height - half]], axis=1)


def lon_back(grid):
    half = WLON // 2
    breadth = grid.shape[2]
    arriving = swapped(grid[:, :, breadth - half :], "lon", 0)
    return jnp.concatenate([arriving, grid[:, :, : breadth - half]], axis=2)


def across(left, right):
    return lax.dot_general(
        left, right, (((0,), (0,)), ((), ())), preferred_element_type=jnp.float32
    )


def on_device(block_input, grad_out, ln_gain, w_qkv, w_proj, bias_table):
    width = block_input.shape[-1]
    values = block_input.astype(jnp.float32)
    mean = jnp.mean(values, axis=-1, keepdims=True)
    centred = values - mean
    inverse = lax.rsqrt(jnp.mean(centred * centred, axis=-1, keepdims=True) + 1e-05)
    standard = centred * inverse
    normed = (standard * ln_gain).astype(jnp.bfloat16)
    stacked = jnp.stack([normed, grad_out])
    stacked = band_ahead(lon_ahead(stacked))
    stacked = jnp.roll(stacked, -(WZ // 2), axis=1)
    shifted = stacked[0]
    grad_shifted = stacked[1]
    grid = shifted.shape[:3]
    token_rows = shifted.reshape(-1, width)
    grad_rows = grad_shifted.reshape(-1, width)
    projected = jnp.dot(token_rows, w_qkv, preferred_element_type=jnp.float32).astype(jnp.bfloat16)
    grad_mixed = lax.dot_general(
        grad_rows, w_proj, (((1,), (1,)), ((), ())), preferred_element_type=jnp.float32
    ).astype(jnp.bfloat16)
    proj_windows = to_windows(projected.reshape(grid + (3 * width,)))
    mixed_windows = to_windows(grad_mixed.reshape(grid + (width,)))
    levels, bands, strips = proj_windows.shape[:3]
    band_index = lax.axis_index("lat") * bands + jnp.arange(bands)
    last_band = (band_index == lax.axis_size("lat") * bands - 1).astype(jnp.int32)
    tables = jnp.transpose(bias_table, (1, 0, 2, 3))
    out_list = []
    grad_list = []
    table_list = []
    for level in range(levels):
        level_flag = jnp.full((bands,), 1 if level == levels - 1 else 0, jnp.int32)
        allowed = allowed_pairs(level_flag, last_band)
        outputs, grad_projected, grad_scores = window_grads(
            proj_windows[level], mixed_windows[level], expand_bias(tables[level]), allowed
        )
        out_list.append(outputs)
        grad_list.append(grad_projected)
        table_list.append(reduce_bias(grad_scores))
    out_rows = from_windows(jnp.stack(out_list)).reshape(-1, width)
    grad_proj_rows = from_windows(jnp.stack(grad_list)).reshape(-1, 3 * width)
    table_part = jnp.stack(table_list, axis=1)
    wproj_part = across(out_rows, grad_rows)
    wqkv_part = across(token_rows, grad_proj_rows)
    grad_shift_rows = lax.dot_general(
        grad_proj_rows, w_qkv, (((1,), (1,)), ((), ())), preferred_element_type=jnp.float32
    ).astype(jnp.bfloat16)
    moved = grad_shift_rows.reshape(grid + (width,))
    moved = lon_back(band_back(moved))
    grad_normed = jnp.roll(moved, WZ // 2, axis=0).astype(jnp.float32)
    gain_part = jnp.sum(grad_normed * standard, axis=(0, 1, 2))
    scaled = grad_normed * ln_gain
    grad_local = inverse * (
        scaled
        - jnp.mean(scaled, axis=-1, keepdims=True)
        - standard * jnp.mean(scaled * standard, axis=-1, keepdims=True)
    )
    grad_x = (grad_out.astype(jnp.float32) + grad_local).astype(jnp.bfloat16)
    grad_bias = lax.psum(table_part, "lon")
    grad_gain, grad_wqkv, grad_wproj = lax.psum((gain_part, wqkv_part, wproj_part), ("lon", "lat"))
    return (grad_x, grad_gain, grad_wqkv, grad_wproj, grad_bias)


def solution(mesh):
    return jax.shard_map(
        on_device,
        mesh=mesh,
        in_specs=(
            P(None, "lat", "lon", None),
            P(None, "lat", "lon", None),
            P(),
            P(),
            P(),
            P("lat", None, None, None),
        ),
        out_specs=(P(None, "lat", "lon", None), P(), P(), P(), P("lat", None, None, None)),
        check_vma=False,
    )
```

profile of v0, /device:TPU:1, one launch (start us, length us, event | category | flops | bytes accessed | tf_op | source)
XLA Modules:
  0.0 1070.3 jit_solution(16629813528064885133)
XLA Ops:
  7.2 1.3 convert_reduce_fusion
  8.5 1.4 fusion.40
  9.9 1.1 copy.144
  11.0 1.4 fusion.51
  12.4 3.7 collective-permute-start
  16.1 0.7 broadcast_compare_fusion.1
  17.9 5.0 convolution_bitcast_fusion
  23.0 11.3 %copy.133 = f32[1,6,2,6,12,2,6,12]{4,3,2,7,6,5,1,0:T(8,128)} copy(f32[1,6,2,6,12,2,6,12]{7,6,3,5,2,1,4,0:T(8,128)} %convolution_bitcast_fusion) | data formatting | bytes 995328 | tf_op jit(solution)/shard_map/add | solution.py:94
  34.2 5.7 reshape.530
  40.0 5.0 convolution_bitcast_fusion.1
  45.0 11.3 %copy.132 = f32[1,6,2,6,12,2,6,12]{4,3,2,7,6,5,1,0:T(8,128)} copy(f32[1,6,2,6,12,2,6,12]{7,6,3,5,2,1,4,0:T(8,128)} %convolution_bitcast_fusion.1) | data formatting | bytes 995328 | tf_op jit(solution)/shard_map/add | solution.py:94
  56.3 5.7 reshape.528
  62.6 1.2 collective-permute-start.1
  63.8 0.7 broadcast_compare_fusion
  64.5 6.6 collective-permute-done.1
  73.3 1.2 copy.98
  75.0 1.1 copy.74
  76.4 1.0 fusion.87
  77.9 0.9 copy.97
  79.0 0.9 copy.92
  79.9 2.4 fusion.93
  82.3 2.5 fusion.24
  84.8 1.1 fusion.26
  85.9 0.6 multiply_reduce_fusion
  86.5 2.5 fusion.33
  89.0 1.2 fusion.19
  90.3 1.0 fusion.20
  93.2 3.9 fusion.94
  97.1 3.1 fusion.23
  100.3 1.0 fusion.25
  101.3 0.6 multiply_reduce_fusion.1
  101.9 1.6 fusion.31
  103.5 1.2 fusion.21
  104.8 1.0 fusion.22
  108.3 1.8 copy.100
  110.7 1.4 copy.102
  112.7 5.0 reshape.521
  117.7 7.7 copy.117
  125.4 5.0 reshape.522
  130.9 0.9 stack_reshape.9
  133.0 1.0 reshape_reshape.15
  134.0 1.4 copy.90
  136.0 1.4 copy.113
  137.4 1.4 copy.85
  142.6 0.7 fusion.92
  143.5 5.1 reshape.519
  148.6 7.6 copy.114
  156.2 5.7 reshape.520
  162.0 1.8 fusion.65
  163.8 0.9 stack_reshape.8
  164.7 1.7 pad_maximum_fusion.6
  166.4 1.3 fusion.95
  167.7 1.0 pad_maximum_fusion.8
  168.7 1.2 collective-permute-start.3
  169.9 1.0 fusion.96
  171.0 603.4 %all-reduce.4.cloned.1.call-done = f32[1,2,6,3312]{3,2,1,0:T(8,128)} async-done(((f32[1,2,6,3312]{3,2,1,0:T(8,128)}), f32[1,2,6,3312]{3,2,1,0:T(8,128)}) %all-reduce.4.cloned.1.call-update) | async-done | bytes 158992 | tf_op jit(solution)/shard_map/psum | solution.py:219
  774.3 1.7 copy.120
  776.0 1.8 fusion.42
  777.8 0.7 fusion.39
  778.5 1.0 copy.119
  779.5 104.3 %psum.28 = f32[192]{0:T(256)} all-reduce(f32[192]{0:T(256)S(1)} %get-tuple-element.15), channel_id=1, replica_groups=mesh['lon'=64,'lat'=4] {'lon','lat'}, use_global_device_ids=true, to_apply=%region_11.12 | all-reduce | flops 192 | bytes 1536 | tf_op jit(solution)/shard_map/psum | solution.py:220
  883.8 176.0 %all-reduce.6.cloned.1.call-done = (f32[192,576]{1,0:T(8,128)}, f32[192,192]{1,0:T(8,128)}) async-done(((f32[192,576]{1,0:T(8,128)}, f32[192,192]{1,0:T(8,128)}), (f32[192,576]{1,0:T(8,128)}, f32[192,192]{1,0:T(8,128)})) %all-reduce.6.cloned.1.call-update) | async-done | bytes 589840 | tf_op jit(solution)/shard_map/psum | solution.py:220
  1059.9 1.8 copy.148
  1061.7 1.6 copy.149
  (119 shorter events, 17.0 us)
Async XLA Ops:
  7.2 67.3 %copy-start = (bf16[192,576]{1,0:T(8,128)(2,1)S(1)}, bf16[192,576]{1,0:T(8,128)(2,1)}, u32[]{:S(2)}) copy-start(bf16[192,576]{1,0:T(8,128)(2,1)} %param.9) | copy-start | bytes 663556
  7.2 9.7 copy-start.21
  7.2 767.1 %all-reduce.4.cloned.1.call-start = ((), (), s32[]{:S(2)}) async-start(), calls=%async_computation | async-start | bytes 425984 | tf_op jit(solution)/shard_map/psum | solution.py:219
  12.4 49.9 %collective-permute-start = (bf16[2,4,6,6,192]{4,3,2,1,0:T(8,128)(2,1)S(1)}, bf16[2,4,6,6,192]{4,3,2,1,0:T(8,128)(2,1)S(1)}, u32[]{:S(2)}, u32[]{:S(2)}) collective-permute-start(bf16[2,4,6,6,192]{4,3,2,1,0:T(8,128)(2,1)S(1)} %pad_maximum_fusion.7), channel_id=1, source_target_pairs={{0,4},{4,0},{8,12},{12,8},{16,20},{20,16},{24,28},{28,24},{32,36},... | collective-permute-start | bytes 331784 | tf_op jit(solution)/shard_map/ppermute | solution.py:17
  62.6 8.5 collective-permute-start.1
  71.2 0.9 copy-start.22
  71.7 2.8 copy-start.4
  72.1 1.2 copy-start.2
  82.3 3.6 copy-start.9
  82.3 2.5 copy-start.16
  84.8 1.1 copy-start.20
  86.5 3.8 copy-start.13
  90.3 1.9 copy-start.8
  92.2 1.0 copy-start.23
  97.1 3.1 copy-start.10
  103.5 2.3 copy-start.18
  103.5 3.3 copy-start.17
  125.4 6.4 copy-start.19
  132.8 3.2 copy-start.7
  135.4 3.9 copy-start.14
  141.7 1.8 copy-start.6
  143.3 24.4 %collective-permute-start.2 = (bf16[4,3,36,192]{3,2,1,0:T(8,128)(2,1)}, bf16[4,3,36,192]{3,2,1,0:T(8,128)(2,1)}, u32[]{:S(2)}, u32[]{:S(2)}) collective-permute-start(bf16[4,3,36,192]{3,2,1,0:T(8,128)(2,1)} %get-tuple-element.41), channel_id=1, source_target_pairs={{3,0},{0,1},{1,2},{2,3},{7,4},{4,5},{5,6},{6,7},{11,8},{8,9},{9,10... | collective-permute-start | bytes 497672 | tf_op jit(solution)/shard_map/ppermute | solution.py:23
  156.2 8.4 copy-start.15
  162.0 4.4 copy-start.5
  162.0 7.9 copy-start.3
  162.0 7.9 copy-start.12
  164.7 611.3 %copy-start.1 = (bf16[4,6,36,192]{3,0,2,1:T(4,128)(2,1)S(1)}, bf16[4,6,36,192]{3,0,2,1:T(4,128)(2,1)}, u32[]{:S(2)}) copy-start(bf16[4,6,36,192]{3,0,2,1:T(4,128)(2,1)} %param.6) | copy-start | bytes 995332
  164.7 611.3 %copy-start.24 = (f32[192]{0:T(256)S(1)}, f32[192]{0:T(256)}, u32[]{:S(2)}) copy-start(f32[192]{0:T(256)} %param.8) | copy-start | bytes 2308
  166.4 893.5 %all-reduce.6.cloned.1.call-start = ((), (), s32[]{:S(2)}) async-start(), calls=%async_computation.1 | async-start | bytes 1376256 | tf_op jit(solution)/shard_map/psum | solution.py:220
  167.7 610.1 %copy-start.11 = (bf16[4,6,36,192]{3,0,2,1:T(4,128)(2,1)S(1)}, bf16[4,6,36,192]{3,0,2,1:T(4,128)(2,1)}, u32[]{:S(2)}) copy-start(bf16[4,6,36,192]{3,0,2,1:T(4,128)(2,1)} %param.7) | copy-start | bytes 995332
  168.7 607.3 %collective-permute-start.3 = (bf16[4,6,6,192]{3,2,1,0:T(8,128)(2,1)S(1)}, bf16[4,6,6,192]{3,2,1,0:T(8,128)(2,1)S(1)}, u32[]{:S(2)}, u32[]{:S(2)}) collective-permute-start(bf16[4,6,6,192]{3,2,1,0:T(8,128)(2,1)S(1)} %pad_maximum_fusion.8), channel_id=1, source_target_pairs={{0,4},{4,0},{8,12},{12,8},{16,20},{20,16},{24,28},{28,24},{32,36},... | collective-permute-start | bytes 165896 | tf_op jit(solution)/shard_map/ppermute | solution.py:17
Sparse Core Ops, SparseCore 0:
  166.5 607.7 all-reduce.3
  781.4 278.4 all-reduce.5
where the time goes:
time: 1080 us; the launch traced here: 1070 us
  waiting for transfers between devices  786 us (73%)
  local copies, waits for them, and re-layouts  107 us (10%)
  blocking collectives  104 us (10%)
  matrix products  35.8 us (3%)
  other arithmetic  16.4 us (2%)
  between operations  14.9 us (1%)
    psum x1, waiting for transfers between devices, on_device(): grad_bias = lax.psum(table_part, 'lon')  603 us
    psum x1, waiting for transfers between devices, on_device(): lax.psum((gain_part, wqkv_part, wproj_part), ('lon', 'lat'))  176 us
    psum x1, blocking collectives, on_device(): lax.psum((gain_part, wqkv_part, wproj_part), ('lon', 'lat'))  104 us
    add x4, local copies, waits for them, and re-layouts, window_grads(): jnp.einsum('abihd,abjhd->abhij', query, key_rows, preferred_element_type=...  34 us
  transfers between devices with their start and end apart: 6, of which 3 were waited for; matrix products, arithmetic and copies ran while one was open for 7% of the time, Pallas kernels for 0%

commit v1 on v0

v1 whole, which is shorter than its diff:
```python
import functools

import jax
import jax.numpy as jnp
from jax import lax
from jax.experimental import pallas as pl
from jax.experimental.pallas import tpu as pltpu
from jax.sharding import Mesh, PartitionSpec as P

C = 192
HEADS = 6
HEAD_DIM = 32
WLON = 12
WIN = 144
TABLE = 3312
PAIRS = 12
OFFSETS = 23
SCALE = HEAD_DIM**-0.5
STRIPS = 3
WINDOWS = 6
TYPES = 12
GROUP = ("y", "xl", "c")
REST = ("z", "xh")
PARTS = 16
PART_ROWS = C // PARTS
QKV_LANES = 640
PROJ_LANES = 256
W_LANES = QKV_LANES + PROJ_LANES
B_LANES = 256
B_PARTS = 13
SEND_LANES = W_LANES + B_LANES
LATS = 4
MIX_LANES = W_LANES + LATS * B_LANES
WIDE = 3584
f32 = jnp.float32
bf16 = jnp.bfloat16
VMEM_LIMIT = 56 * 1024 * 1024

NN = (((1,), (0,)), ((), ()))
NT = (((1,), (1,)), ((), ()))


def dot(a, b, dims=NN):
    return lax.dot_general(a, b, dims, preferred_element_type=f32)


def table_offset(zl_i, zl_j):
    zi, li = divmod(zl_i, 6)
    zj, lj = divmod(zl_j, 6)
    return (((zi * 2 + zj) * 6 + li) * 6 + lj) * OFFSETS


def offset_match(oj):
    row = lax.broadcasted_iota(jnp.int32, (PAIRS * 32, 256), 0)
    col = lax.broadcasted_iota(jnp.int32, (PAIRS * 32, 256), 1)
    zl = col // WLON
    target = zl * 32 + (oj + 11) - (col - zl * WLON)
    return jnp.where(row == target, 1.0, 0.0).astype(bf16)


def bias_kernel(table_ref, out_ref, wide, pairs):
    wide[...] = jnp.zeros_like(wide)
    for lz in range(2):
        wide[lz * HEADS : (lz + 1) * HEADS, :TABLE] = table_ref[0, lz]
    pairs[...] = jnp.zeros_like(pairs)
    lane = lax.broadcasted_iota(jnp.int32, (16, 128), 1)
    for zl_j in range(PAIRS):
        for v in range(3):
            total = jnp.zeros((16, 128), f32)
            for q in range(4):
                off = table_offset(4 * v + q, zl_j)
                base, rest = off // 128 * 128, off % 128
                width = 128 if rest + OFFSETS <= 128 else 256
                piece = wide[:, base : base + width]
                shift = (32 * q - rest) % width
                if shift:
                    piece = pltpu.roll(piece, shift, 1)
                inside = (lane >= 32 * q) & (lane < 32 * q + OFFSETS)
                total = jnp.where(inside, piece[:, :128], total)
            pairs[v, pl.ds(zl_j, TYPES, stride=16), :] = total[:TYPES]
    full = jnp.concatenate([pairs[v] for v in range(3)], axis=1)
    high = full.astype(bf16)
    left = full - high.astype(f32)
    middle = left.astype(bf16)
    low = (left - middle.astype(f32)).astype(bf16)
    for oj in range(WLON):
        match = offset_match(oj)
        dense = dot(high, match) + (dot(middle, match) + dot(low, match))
        for t in range(TYPES):
            block = dense[t * 16 : t * 16 + PAIRS]
            out_ref[t, 0, pl.ds(oj, PAIRS, stride=WLON), :] = block[:, :128]
            out_ref[t, 1, pl.ds(oj, PAIRS, stride=WLON), :] = block[:, 128:]
    lat = lax.axis_index("xl") * 2 + lax.axis_index("c")
    last_band = (lat == LATS - 1).astype(jnp.int32)
    j = lax.broadcasted_iota(jnp.int32, (WIN, 256), 0)
    i = lax.broadcasted_iota(jnp.int32, (WIN, 256), 1)

    def region(token, last_level):
        upper = jnp.where(token >= 72, 2 * last_level, 0)
        inner = jnp.where(token >= 72, token - 72, token)
        return upper + jnp.where(inner >= 36, last_band, 0)

    for lz in range(2):
        allowed = region(i, lz) == region(j, lz)
        for h in range(HEADS):
            t = lz * HEADS + h
            for n in range(2):
                kept = allowed[:, 128 * n : 128 * (n + 1)]
                out_ref[t, n] = jnp.where(kept, out_ref[t, n], -1e30)


def bias_dense(table):
    return pl.pallas_call(
        bias_kernel,
        out_shape=jax.ShapeDtypeStruct((TYPES, 2, WIN, 128), f32),
        in_specs=[pl.BlockSpec(memory_space=pltpu.VMEM)],
        out_specs=pl.BlockSpec(memory_space=pltpu.VMEM),
        scratch_shapes=[pltpu.VMEM((16, WIDE), f32), pltpu.VMEM((3, TYPES * 16, 128), f32)],
        compiler_params=pltpu.CompilerParams(vmem_limit_bytes=VMEM_LIMIT),
        cost_estimate=pl.CostEstimate(
            flops=20_000_000_000, bytes_accessed=1_200_000, transcendentals=0
        ),
        name="bias_dense",
    )(table)


def normalised(values):
    mean = jnp.mean(values, axis=-1, keepdims=True)
    centred = values - mean
    inverse = lax.rsqrt(jnp.mean(centred * centred, axis=-1, keepdims=True) + 1e-05)
    return centred * inverse, inverse


def main_kernel(
    x_ref, g_ref, lat_ref, lon_ref, corner_ref, gain_ref, w3_ref, w3t_ref, wqkv_ref, wproj_ref,
    bias_ref, own_out, lat_out, lon_out, corner_out, send_out,
    xw, gw, rows, dense, wsum, psum, gsum, spread, wide, grads,
):
    for level in range(4):
        source = (level + 1) % 4
        lz, zi = divmod(level, 2)
        for a in range(6):
            for k, (own, to) in enumerate(((x_ref, xw), (g_ref, gw))):
                if a < 3:
                    body = own[source, a + 3].astype(f32)[6:36]
                    tail = lon_ref[k, source, a].astype(f32)
                else:
                    body = lat_ref[k, source, a - 3].astype(f32)
                    tail = corner_ref[k, source, a - 3].astype(f32)
                line = jnp.concatenate([body, tail], axis=0)
                start = zi * 72 + a * WLON
                for s in range(STRIPS):
                    to[lz * STRIPS + s, start : start + WLON, :] = line[s * WLON : (s + 1) * WLON]
    dense[...] = jnp.zeros_like(dense)
    wsum[...] = jnp.zeros_like(wsum)
    psum[...] = jnp.zeros_like(psum)
    gsum[...] = jnp.zeros_like(gsum)
    gain = gain_ref[...]
    lane_head = lax.broadcasted_iota(jnp.int32, (WIN, C), 1) // HEAD_DIM

    def of_head(value, h):
        return jnp.where(lane_head == h, value, jnp.zeros_like(value))

    def window(w, carry):
        lz = w // STRIPS
        standard, _ = normalised(xw[w])
        tokens = (standard * gain).astype(bf16)
        cot = gw[w].astype(bf16)
        query = dot(tokens, w3_ref[0]).astype(bf16)
        key = dot(tokens, w3_ref[1]).astype(bf16)
        value = dot(tokens, w3_ref[2]).astype(bf16)
        key_t = dot(w3t_ref[1], tokens, NT).astype(bf16)
        value_t = dot(w3t_ref[2], tokens, NT).astype(bf16)
        mixed = dot(cot, wproj_ref[...], NT).astype(bf16)
        out_t = []
        grad_query_t = []
        grad_key = jnp.zeros((WIN, C), f32)
        grad_value = jnp.zeros((WIN, C), f32)
        for h in range(HEADS):
            part = slice(h * HEAD_DIM, (h + 1) * HEAD_DIM)
            bias = jnp.concatenate(
                [bias_ref[lz * HEADS + h, 0], bias_ref[lz * HEADS + h, 1][:, : WIN - 128]], axis=1
            )
            scores = dot(of_head(key, h), query, NT) * SCALE + bias
            top = jnp.max(scores, axis=0, keepdims=True)
            powers = jnp.exp(scores - top)
            attend = powers * (1.0 / jnp.sum(powers, axis=0, keepdims=True))
            half = attend.astype(bf16)
            grad_attend = dot(of_head(value, h), mixed, NT)
            total = jnp.sum(attend * grad_attend, axis=0, keepdims=True)
            grad_scores = attend * (grad_attend - total)
            grad_half = grad_scores.astype(bf16)
            dense[lz * HEADS + h, 0] += grad_scores[:, :128]
            dense[lz * HEADS + h, 1, :, : WIN - 128] += grad_scores[:, 128:]
            out_t.append(dot(value_t[part], half).astype(bf16))
            grad_query_t.append(dot(key_t[part], grad_half) * SCALE)
            grad_value += dot(half, of_head(mixed, h))
            grad_key += dot(grad_half, of_head(query, h))
        out_t = jnp.concatenate(out_t, axis=0)
        grad_query = jnp.concatenate(grad_query_t, axis=0).T
        psum[...] += dot(out_t, cot)
        spread[:, 0:C] = grad_query
        spread[:, C : 2 * C] = grad_key * SCALE
        spread[:, 2 * C : 3 * C] = grad_value
        grad_projected = spread[...].astype(bf16)
        tokens_t = (standard * gain).T.astype(bf16)
        wsum[...] += dot(tokens_t, grad_projected)
        back = dot(grad_projected, wqkv_ref[...], NT).astype(bf16).astype(f32)
        rows[w] = back
        gsum[0:1, :] += jnp.sum(back * standard, axis=0, keepdims=True)
        return carry

    lax.fori_loop(0, WINDOWS, window, 0)

    for level in range(4):
        source = (level + 1) % 4
        lz, zi = divmod(level, 2)
        for a in range(6):
            start = zi * 72 + a * WLON
            line = jnp.concatenate(
                [rows[lz * STRIPS + s, start : start + WLON, :] for s in range(STRIPS)], axis=0
            )
            body, tail = line[:30].astype(bf16), line[30:].astype(bf16)
            if a < 3:
                own_out[source, a] = body
                lon_out[source, a] = tail
            else:
                lat_out[source, a - 3] = body
                corner_out[source, a - 3] = tail

    grads[...] = jnp.zeros_like(grads)
    for oj in range(WLON):
        picked = jnp.concatenate(
            [
                jnp.concatenate(
                    [
                        jnp.concatenate(
                            [dense[t, n, pl.ds(oj, PAIRS, stride=WLON), :] for n in range(2)],
                            axis=1,
                        ),
                        jnp.zeros((4, 256), f32),
                    ],
                    axis=0,
                )
                for t in range(TYPES)
            ],
            axis=0,
        )
        high = picked.astype(bf16)
        low = (picked - high.astype(f32)).astype(bf16)
        match = offset_match(oj)
        added = dot(high, match, NT) + dot(low, match, NT)
        for v in range(3):
            grads[v] += added[:, 128 * v : 128 * (v + 1)]
    wide[...] = jnp.zeros_like(wide)
    lane = lax.broadcasted_iota(jnp.int32, (TYPES, 256), 1)
    for zl_j in range(PAIRS):
        for v in range(3):
            four = grads[v, pl.ds(zl_j, TYPES, stride=16), :]
            for q in range(4):
                off = table_offset(4 * v + q, zl_j)
                base, rest = off // 128 * 128, off % 128
                width = 128 if rest + OFFSETS <= 128 else 256
                piece = four
                if width == 256:
                    piece = jnp.concatenate([four, jnp.zeros_like(four)], axis=1)
                shift = (rest - 32 * q) % width
                if shift:
                    piece = pltpu.roll(piece, shift, 1)
                position = lane[:, :width]
                inside = (position >= rest) & (position < rest + OFFSETS)
                target = (slice(0, TYPES), slice(base, base + width))
                wide[target] = jnp.where(inside, piece, wide[target])

    tail = jnp.concatenate(
        [gsum[0:1, :], jnp.zeros((16 - PART_ROWS - 1, C), f32)], axis=0
    )
    for p in range(PARTS):
        lines = slice(p * PART_ROWS, (p + 1) * PART_ROWS)
        first = jnp.concatenate([wsum[lines, :], jnp.zeros((4, 3 * C), f32)], axis=0)
        send_out[p, :, 0 : 3 * C] = first.astype(bf16)
        send_out[p, :, 3 * C : QKV_LANES] = jnp.zeros((16, QKV_LANES - 3 * C), bf16)
        second = jnp.concatenate([psum[lines, :], tail], axis=0)
        send_out[p, :, QKV_LANES : QKV_LANES + C] = second.astype(bf16)
        send_out[p, :, QKV_LANES + C : W_LANES] = jnp.zeros((16, PROJ_LANES - C), bf16)
        if p < B_PARTS:
            third = wide[:, p * B_LANES : (p + 1) * B_LANES].astype(bf16)
        else:
            third = jnp.zeros((16, B_LANES), bf16)
        send_out[p, :, W_LANES:] = third


def main(x, g, lat_in, lon_in, corner_in, gain, w3, w3t, wqkv, wproj, bias):
    vmem = pl.BlockSpec(memory_space=pltpu.VMEM)
    return pl.pallas_call(
        main_kernel,
        out_shape=(
            jax.ShapeDtypeStruct((4, 3, 30, C), bf16),
            jax.ShapeDtypeStruct((4, 3, 30, C), bf16),
            jax.ShapeDtypeStruct((4, 3, 6, C), bf16),
            jax.ShapeDtypeStruct((4, 3, 6, C), bf16),
            jax.ShapeDtypeStruct((PARTS, 16, SEND_LANES), bf16),
        ),
        in_specs=[vmem] * 11,
        out_specs=(vmem,) * 5,
        scratch_shapes=[
            pltpu.VMEM((WINDOWS, WIN, C), f32),
            pltpu.VMEM((WINDOWS, WIN, C), f32),
            pltpu.VMEM((WINDOWS, WIN, C), f32),
            pltpu.VMEM((TYPES, 2, WIN, 128), f32),
            pltpu.VMEM((C, 3 * C), f32),
            pltpu.VMEM((C, C), f32),
            pltpu.VMEM((8, C), f32),
            pltpu.VMEM((WIN, 3 * C), f32),
            pltpu.VMEM((16, WIDE), f32),
            pltpu.VMEM((3, TYPES * 16, 128), f32),
        ],
        compiler_params=pltpu.CompilerParams(vmem_limit_bytes=VMEM_LIMIT),
        cost_estimate=pl.CostEstimate(
            flops=20_000_000_000, bytes_accessed=4_000_000, transcendentals=750_000
        ),
        name="window_grads",
    )(x, g, lat_in, lon_in, corner_in, gain, w3, w3t, wqkv, wproj, bias)


def norm_kernel(x_ref, g_ref, gain_ref, own_ref, lat_ref, lon_ref, corner_ref, out_ref):
    gain = gain_ref[...]
    for level in range(4):
        for a in range(6):
            if a < 3:
                head, body = corner_ref[level, a], lat_ref[level, a]
            else:
                head, body = lon_ref[level, a - 3], own_ref[level, a - 3]
            grad = jnp.concatenate([head.astype(f32), body.astype(f32)], axis=0)
            standard, inverse = normalised(x_ref[level, a].astype(f32))
            scaled = grad * gain
            local = inverse * (
                scaled
                - jnp.mean(scaled, axis=-1, keepdims=True)
                - standard * jnp.mean(scaled * standard, axis=-1, keepdims=True)
            )
            out_ref[level, a] = (g_ref[level, a].astype(f32) + local).astype(bf16)


def norm_grads(x, g, gain, own, lat_in, lon_in, corner_in):
    vmem = pl.BlockSpec(memory_space=pltpu.VMEM)
    return pl.pallas_call(
        norm_kernel,
        out_shape=jax.ShapeDtypeStruct(x.shape, bf16),
        in_specs=[vmem] * 7,
        out_specs=vmem,
        compiler_params=pltpu.CompilerParams(vmem_limit_bytes=VMEM_LIMIT),
        cost_estimate=pl.CostEstimate(
            flops=10_000_000, bytes_accessed=1_500_000, transcendentals=1000
        ),
        name="norm_grads",
    )(x, g, gain, own, lat_in, lon_in, corner_in)


def unpack_kernel(parts_ref, gain_out, wqkv_out, wproj_out, bias_out):
    gain_out[...] = parts_ref[0, :, QKV_LANES : QKV_LANES + C].astype(f32)[12:13]
    for p in range(PARTS):
        lines = slice(p * PART_ROWS, (p + 1) * PART_ROWS)
        wqkv_out[lines, :] = parts_ref[p, :, 0 : 3 * C].astype(f32)[:PART_ROWS]
        wproj_out[lines, :] = parts_ref[p, :, QKV_LANES : QKV_LANES + C].astype(f32)[:PART_ROWS]
        if p < B_PARTS:
            width = min(B_LANES, TABLE - p * B_LANES)
            block = parts_ref[p, :, W_LANES:].astype(f32)[:, :width]
            for lz in range(2):
                bias_out[0, lz, :, p * B_LANES : p * B_LANES + width] = block[
                    lz * HEADS : (lz + 1) * HEADS
                ]


def unpack(parts):
    vmem = pl.BlockSpec(memory_space=pltpu.VMEM)
    return pl.pallas_call(
        unpack_kernel,
        out_shape=(
            jax.ShapeDtypeStruct((1, C), f32),
            jax.ShapeDtypeStruct((C, 3 * C), f32),
            jax.ShapeDtypeStruct((C, C), f32),
            jax.ShapeDtypeStruct((1, 2, HEADS, TABLE), f32),
        ),
        in_specs=[vmem],
        out_specs=(vmem,) * 4,
        compiler_params=pltpu.CompilerParams(vmem_limit_bytes=VMEM_LIMIT),
        name="unpack",
    )(parts)


def summed(send):
    lats = LATS
    got = lax.all_to_all(send, GROUP, 0, 0, tiled=True)
    got = got.reshape((PARTS // lats, lats, 16, SEND_LANES)).astype(f32)
    weights = jnp.sum(got[..., :W_LANES], axis=(0, 1))
    bias = jnp.sum(got[..., W_LANES:], axis=0).transpose(1, 0, 2).reshape(16, lats * B_LANES)
    mixed = jnp.concatenate([weights, bias], axis=1).astype(bf16)
    count = lax.axis_size(REST)
    got = lax.all_to_all(
        jnp.broadcast_to(mixed[None], (count,) + mixed.shape), REST, 0, 0, tiled=True
    )
    total = jnp.sum(got.astype(f32), axis=0).astype(bf16)
    weights = jnp.broadcast_to(total[None, None, :, :W_LANES], (PARTS // lats, lats, 16, W_LANES))
    bias = total[:, W_LANES:].reshape(16, lats, B_LANES).transpose(1, 0, 2)
    bias = jnp.broadcast_to(bias[None], (PARTS // lats, lats, 16, B_LANES))
    spread = jnp.concatenate([weights, bias], axis=-1).reshape(send.shape)
    return lax.all_to_all(spread, GROUP, 0, 0, tiled=True)


def on_device(x, g, ln_gain, w_qkv, w_proj, bias_table):
    lon_axes, lat_axes = ("z", "y", "xh"), ("xl", "c")
    both = lon_axes + lat_axes
    lons, lats = lax.axis_size(lon_axes), lax.axis_size(lat_axes)
    lon_swap = [(i, i ^ 1) for i in range(lons)]
    lat_down = [(i, (i - 1) % lats) for i in range(lats)]
    lat_up = [(i, (i + 1) % lats) for i in range(lats)]
    corner_down = [(i * lats + a, (i ^ 1) * lats + b) for i in range(lons) for a, b in lat_down]
    corner_up = [(i * lats + a, (i ^ 1) * lats + b) for i in range(lons) for a, b in lat_up]

    corner_in = lax.ppermute(jnp.stack([x[:, :3, :6], g[:, :3, :6]]), both, corner_down)
    lon_in = lax.ppermute(jnp.stack([x[:, 3:, :6], g[:, 3:, :6]]), lon_axes, lon_swap)
    lat_in = lax.ppermute(jnp.stack([x[:, :3, 6:], g[:, :3, 6:]]), lat_axes, lat_down)
    bias = bias_dense(bias_table)
    w3 = w_qkv.reshape(C, 3, C).transpose(1, 0, 2)
    w3t = w_qkv.T.reshape(3, C, C)
    gain = ln_gain.reshape(1, C)
    own, to_lat, to_lon, to_corner, send = main(
        x, g, lat_in, lon_in, corner_in, gain, w3, w3t, w_qkv, w_proj, bias
    )
    back_corner = lax.ppermute(to_corner, both, corner_up)
    back_lon = lax.ppermute(to_lon, lon_axes, lon_swap)
    back_lat = lax.ppermute(to_lat, lat_axes, lat_up)
    grad_gain, grad_wqkv, grad_wproj, grad_bias = unpack(summed(send))
    grad_x = norm_grads(x, g, gain, own, back_lat, back_lon, back_corner)
    return grad_x, grad_gain.reshape(C), grad_wqkv, grad_wproj, grad_bias


def solution(mesh):
    shape = (mesh.shape["lon"] // 8, 4, 2, 2, 2)
    split = Mesh(mesh.devices.reshape(shape), ("z", "y", "xh", "xl", "c"))
    tokens = P(None, ("xl", "c"), ("z", "y", "xh"), None)
    table = P(("xl", "c"), None, None, None)
    return jax.shard_map(
        on_device,
        mesh=split,
        in_specs=(tokens, tokens, P(), P(), P(), table),
        out_specs=(tokens, P(), P(), P(), table),
        check_vma=False,
    )
```

time: 1080 us -> 124 us (0.11)
  waiting for transfers between devices: 786 us -> 7.3 us
  local copies, waits for them, and re-layouts: 107 us -> 10.2 us
  blocking collectives: 104 us -> 53.5 us
  matrix products: 35.8 us -> 0 us
  Pallas kernels: 0 us -> 33.8 us
  other arithmetic: 16.4 us -> 1.32 us
  between operations: 14.9 us -> 0.93 us
    psum x2 -> x0, waiting for transfers between devices: 779 us -> none  [the longest x1 603 us: on_device(): grad_bias = lax.psum(table_part, 'lon')]
    psum x1 -> x0, blocking collectives: 104 us -> none  [on_device(): lax.psum((gain_part, wqkv_part, wproj_part), ('lon', 'lat'))]
    all_to_all x0 -> x2, blocking collectives: none -> 53.5 us  [the longest x1 37.9 us: summed(): lax.all_to_all(jnp.broadcast_to(mixed[None], (count,) + mixed.shape), RES...]
    add x4 -> x0, local copies, waits for them, and re-layouts: 34 us -> none  [window_grads(): jnp.einsum('abihd,abjhd->abhij', query, key_rows, preferred_element_type=...]
    pallas_call x0 -> x4, Pallas kernels: none -> 33.8 us  [the longest x1 22.5 us: main(): pl.pallas_call(main_kernel, out_shape=(jax.ShapeDtypeStruct((4, 3, 30, C)...]
    dot_general x19 -> x0, matrix products: 29.5 us -> none  [the longest x2 10 us: expand_bias(): jnp.einsum('...pr,qr->...pq', pairs, relation_table(), precision=lax.Prec...]
    another operation x18 -> x2, local copies, waits for them, and re-layouts: 19 us -> 0.15 us  [the longest x1 0.13 us: on_device(): jnp.stack([x[:, :3, 6:], g[:, :3, 6:]])]
    transpose x4 -> x2, local copies, waits for them, and re-layouts: 15.5 us -> 0.89 us  [the longest x1 0.88 us: on_device(): w3t = w_qkv.T.reshape(3, C, C)]
  transfers between devices with their start and end apart: 6 -> 7, of which waited for: 3 -> 1; matrix products, arithmetic and copies ran while one was open for 7% -> 4% of each run, Pallas kernels for 0% -> 7%
where the time goes in v1:
time: 124 us
  blocking collectives  53.5 us (43%)
  Pallas kernels  33.8 us (27%)
  starting transfers between devices  16.9 us (14%)
  local copies, waits for them, and re-layouts  10.2 us (8%)
  waiting for transfers between devices  7.3 us (6%)
  other arithmetic  1.32 us (1%)
    all_to_all x1, blocking collectives, summed(): lax.all_to_all(jnp.broadcast_to(mixed[None], (count,) + mixed.shape), RES...  37.9 us
    pallas_call x1, Pallas kernels, main(): pl.pallas_call(main_kernel, out_shape=(jax.ShapeDtypeStruct((4, 3, 30, C)...  22.5 us
    all_to_all x1, blocking collectives, summed(): got = lax.all_to_all(send, GROUP, 0, 0, tiled=True)  15.6 us
    unnamed x36, local copies, waits for them, and re-layouts  8.1 us
    ppermute x1, waiting for transfers between devices, on_device(): back_lon = lax.ppermute(to_lon, lon_axes, lon_swap)  7.29 us
    all_to_all x1, starting transfers between devices, summed(): return lax.all_to_all(spread, GROUP, 0, 0, tiled=True)  5.73 us
    pallas_call x1, Pallas kernels, bias_dense(): pl.pallas_call(bias_kernel, out_shape=jax.ShapeDtypeStruct((TYPES, 2, WIN...  4.82 us
    pallas_call x1, Pallas kernels, norm_grads(): pl.pallas_call(norm_kernel, out_shape=jax.ShapeDtypeStruct(x.shape, bf16)...  4.47 us
  transfers between devices with their start and end apart: 7, of which 1 were waited for; matrix products, arithmetic and copies ran while one was open for 4% of the time, Pallas kernels for 7%

profile of v1, /device:TPU:1, one launch (start us, length us, event | category | flops | bytes accessed | tf_op | source)
XLA Modules:
  0.0 123.9 jit_solution(9224074356322208623)
XLA Ops:
  0.6 0.0 copy-start.4
  0.6 1.1 copy.72.x_ref
  1.8 0.0 copy-done.4
  1.8 0.0 copy-start
  1.8 0.1 copy.73.g_ref
  1.9 0.0 copy-start.1
  1.9 0.0 copy-start.6
  2.0 3.7 %collective-permute-start.1 = (bf16[2,4,3,6,192]{4,3,2,1,0:T(8,128)(2,1)S(1)}, bf16[2,4,3,6,192]{4,3,2,1,0:T(8,128)(2,1)S(1)}, u32[]{:S(2)}, u32[]{:S(2)}) collective-permute-start(bf16[2,4,3,6,192]{4,3,2,1,0:T(8,128)(2,1)S(1)} %pad_maximum_fusion.2), channel_id=1, source_target_pairs={{0,4},{4,0},{8,12},{12,8},{16,20},{20,16},{24,28},{28,24},{32,36},... | collective-permute-start | bytes 165896 | tf_op jit(solution)/shard_map/ppermute | solution.py:422
  5.7 2.9 %collective-permute-start.2 = (bf16[2,4,3,6,192]{4,3,2,1,0:T(8,128)(2,1)S(1)}, bf16[2,4,3,6,192]{4,3,2,1,0:T(8,128)(2,1)S(1)}, u32[]{:S(2)}, u32[]{:S(2)}) collective-permute-start(bf16[2,4,3,6,192]{4,3,2,1,0:T(8,128)(2,1)S(1)} %pad_maximum_fusion.3), channel_id=1, source_target_pairs={{0,7},{1,4},{2,5},{3,6},{4,3},{5,0},{6,1},{7,2},{8,15},{9,12},{10,... | collective-permute-start | bytes 165896 | tf_op jit(solution)/shard_map/ppermute | solution.py:421
  8.5 0.1 slice_bitcast_fusion
  8.7 0.0 copy-done
  8.7 0.1 pad_maximum_fusion.1
  8.8 0.0 copy-done.1
  8.8 0.1 collective-permute-start
  8.9 0.0 copy-done.6
  8.9 0.7 copy.69.table_ref
  9.6 0.0 copy-start.3
  9.6 4.8 %bias_dense.1.bias_ref = f32[12,2,144,128]{3,2,1,0:T(8,128)} custom-call(f32[1,2,6,3312]{3,2,1,0:T(8,128)} %copy.69.table_ref), custom_call_target="tpu_custom_call" | custom-call | flops 20000000000 | bytes 1200000 | tf_op jit(solution)/shard_map/bias_dense/pallas_call | solution.py:113
  14.4 0.0 copy-done.3
  14.4 0.2 copy.66
  14.6 0.9 copy.68
  15.5 0.9 copy.67
  16.3 0.0 collective-permute-done.1.lon_ref
  16.3 0.0 copy-start.11
  16.3 0.0 collective-permute-done.2.corner_ref
  16.4 0.0 copy-start.12
  16.4 0.0 collective-permute-done.lat_ref
  16.4 0.0 copy-start.9
  16.4 0.6 copy-done.11
  17.0 0.0 copy-done.12
  17.0 0.1 copy-done.9
  17.2 22.5 %window_grads.1 = (bf16[4,3,30,192]{3,2,1,0:T(8,128)(2,1)}, bf16[4,3,30,192]{3,2,1,0:T(8,128)(2,1)}, bf16[4,3,6,192]{3,2,1,0:T(8,128)(2,1)}, bf16[4,3,6,192]{3,2,1,0:T(8,128)(2,1)}, bf16[16,16,1152]{2,1,0:T(8,128)(2,1)}) custom-call(bf16[4,6,36,192]{3,2,1,0:T(8,128)(2,1)} %copy-done, bf16[4,6,36,192]{3,2,1,0:T(8,128)(2,1)} %copy-done.1, ...), custom_call_target="tpu_custom_call" | custom-call | flops 20000000000 | bytes 4000000 | tf_op jit(solution)/shard_map/window_grads/pallas_call | solution.py:295
  39.7 15.6 %all_to_all.15 = bf16[16,16,1152]{2,1,0:T(8,128)(2,1)S(1)} all-to-all(bf16[16,16,1152]{2,1,0:T(8,128)(2,1)} %get-tuple-element.18), channel_id=1, replica_groups=mesh['z'=8,'y'=4,'xh'=2,'xl'=2,'c'=2] {'y','xl','c'}, dimensions={0} | all-to-all | bytes 1179648 | tf_op jit(solution)/shard_map/all_to_all | solution.py:394
  55.2 0.1 bitcast_convert_fusion
  55.4 0.1 broadcast_in_dim.6
  55.5 37.9 %all_to_all.16 = bf16[16,16,1920]{2,1,0:T(8,128)(2,1)S(1)} all-to-all(bf16[16,16,1920]{2,1,0:T(8,128)(2,1)S(1)} %broadcast_in_dim.6), channel_id=1, replica_groups=mesh['z'=8,'y'=4,'xh'=2,'xl'=2,'c'=2] {'z','xh'}, dimensions={0} | all-to-all | bytes 1966080 | tf_op jit(solution)/shard_map/all_to_all | solution.py:400
  93.5 0.1 reduce_sum.32
  93.7 0.0 copy-start.10
  93.7 0.0 copy-start.14
  93.8 0.0 copy-start.13
  93.8 0.9 pad_maximum_fusion
  94.6 5.7 %all-to-all-start.2 = ((bf16[16,16,1152]{2,1,0:T(8,128)(2,1)}), bf16[16,16,1152]{2,1,0:T(8,128)(2,1)S(1)}, u32[]{:S(2)}, u32[]{:S(2)}) async-start(bf16[16,16,1152]{2,1,0:T(8,128)(2,1)} %bitcast.15), calls=%async_computation.2 | async-start | bytes 1179648 | tf_op jit(solution)/shard_map/all_to_all | solution.py:408
  100.4 0.0 copy-done.10
  100.4 1.7 %collective-permute-start.3 = (bf16[4,3,30,192]{3,2,1,0:T(8,128)(2,1)S(1)}, bf16[4,3,30,192]{3,2,1,0:T(8,128)(2,1)S(1)}, u32[]{:S(2)}, u32[]{:S(2)}) collective-permute-start(bf16[4,3,30,192]{3,2,1,0:T(8,128)(2,1)S(1)} %copy-done.10), channel_id=1, source_target_pairs={{0,1},{1,2},{2,3},{3,0},{4,5},{5,6},{6,7},{7,4},{8,9},{9,10},{10,1... | collective-permute-start | bytes 414728 | tf_op jit(solution)/shard_map/ppermute | solution.py:433
  102.1 0.0 copy-done.14
  102.1 0.3 collective-permute-start.4
  102.4 0.0 copy-done.13
  102.4 2.5 %collective-permute-start.5 = (bf16[4,3,6,192]{3,2,1,0:T(8,128)(2,1)S(1)}, bf16[4,3,6,192]{3,2,1,0:T(8,128)(2,1)S(1)}, u32[]{:S(2)}, u32[]{:S(2)}) collective-permute-start(bf16[4,3,6,192]{3,2,1,0:T(8,128)(2,1)S(1)} %copy-done.13), channel_id=1, source_target_pairs={{0,5},{1,6},{2,7},{3,4},{4,1},{5,2},{6,3},{7,0},{8,13},{9,14},{10,... | collective-permute-start | bytes 82952 | tf_op jit(solution)/shard_map/ppermute | solution.py:431
  104.9 7.3 %collective-permute-done.4.lon_ref = bf16[4,3,6,192]{3,2,1,0:T(8,128)(2,1)S(1)} collective-permute-done((bf16[4,3,6,192]{3,2,1,0:T(8,128)(2,1)S(1)}, bf16[4,3,6,192]{3,2,1,0:T(8,128)(2,1)S(1)}, u32[]{:S(2)}, u32[]{:S(2)}) %collective-permute-start.4) | collective-permute-done | bytes 27680 | tf_op jit(solution)/shard_map/ppermute | solution.py:432
  112.2 0.0 copy-start.7
  112.2 0.0 collective-permute-done.5.corner_ref
  112.2 0.0 copy-start.8
  112.2 0.0 collective-permute-done.3.lat_ref
  112.2 0.0 copy-start.5
  112.2 0.6 copy-done.7
  112.8 0.0 copy-done.8
  112.8 0.1 copy-done.5
  112.9 4.5 %norm_grads.1 = bf16[4,6,36,192]{3,2,1,0:T(8,128)(2,1)} custom-call(bf16[4,6,36,192]{3,2,1,0:T(8,128)(2,1)} %copy-done, bf16[4,6,36,192]{3,2,1,0:T(8,128)(2,1)} %copy-done.1, f32[1,192]{1,0:T(1,128)} %bitcast.36, bf16[4,3,30,192]{3,2,1,0:T(8,128)(2,1)} %get-tuple-element.14.own_ref, bf16[4,3,30,192]{3,2,1,0:T(8,128)(2,1)} %copy-done.5, ...), custom_call_target="tpu_custom_call" | custom-call | flops 10000000 | bytes 1500000 | tf_op jit(solution)/shard_map/norm_grads/pallas_call | solution.py:347
  117.4 2.0 %copy.76 = bf16[4,6,36,192]{3,0,2,1:T(4,128)(2,1)} copy(bf16[4,6,36,192]{3,2,1,0:T(8,128)(2,1)} %norm_grads.1) | data formatting | bytes 663552
  119.4 0.0 all-to-all-done.2.parts_ref
  119.4 0.0 copy-start.2
  119.4 0.8 copy-done.2
  120.2 2.0 %unpack.1 = (f32[1,192]{1,0:T(1,128)}, f32[192,576]{1,0:T(8,128)}, f32[192,192]{1,0:T(8,128)}, f32[1,2,6,3312]{3,2,1,0:T(8,128)}) custom-call(bf16[16,16,1152]{2,1,0:T(8,128)(2,1)} %copy-done.2), custom_call_target="tpu_custom_call" | custom-call | tf_op jit(solution)/shard_map/unpack/pallas_call | solution.py:377
  122.3 1.7 %copy.77 = f32[1,2,6,3312]{3,1,2,0:T(2,128)} copy(f32[1,2,6,3312]{3,2,1,0:T(8,128)} %get-tuple-element.42) | data formatting | bytes 317952
  (13 shorter events, 0.2 us)
Async XLA Ops:
  0.6 1.2 copy-start.4
  1.8 6.9 %copy-start = (bf16[4,6,36,192]{3,2,1,0:T(8,128)(2,1)}, bf16[4,6,36,192]{3,2,1,0:T(8,128)(2,1)S(1)}, u32[]{:S(2)}) copy-start(bf16[4,6,36,192]{3,2,1,0:T(8,128)(2,1)S(1)} %copy.72.x_ref) | copy-start | bytes 995332
  1.9 6.9 %copy-start.1 = (bf16[4,6,36,192]{3,2,1,0:T(8,128)(2,1)}, bf16[4,6,36,192]{3,2,1,0:T(8,128)(2,1)S(1)}, u32[]{:S(2)}) copy-start(bf16[4,6,36,192]{3,2,1,0:T(8,128)(2,1)S(1)} %copy.73.g_ref) | copy-start | bytes 995332
  1.9 7.0 %copy-start.6 = (f32[1,2,6,3312]{3,1,2,0:T(2,128)S(1)}, f32[1,2,6,3312]{3,1,2,0:T(2,128)}, u32[]{:S(2)}) copy-start(f32[1,2,6,3312]{3,1,2,0:T(2,128)} %param.11) | copy-start | bytes 476932
  2.0 14.4 %collective-permute-start.1 = (bf16[2,4,3,6,192]{4,3,2,1,0:T(8,128)(2,1)S(1)}, bf16[2,4,3,6,192]{4,3,2,1,0:T(8,128)(2,1)S(1)}, u32[]{:S(2)}, u32[]{:S(2)}) collective-permute-start(bf16[2,4,3,6,192]{4,3,2,1,0:T(8,128)(2,1)S(1)} %pad_maximum_fusion.2), channel_id=1, source_target_pairs={{0,4},{4,0},{8,12},{12,8},{16,20},{20,16},{24,28},{28,24},{32,36},... | collective-permute-start | bytes 165896 | tf_op jit(solution)/shard_map/ppermute | solution.py:422
  5.7 10.7 %collective-permute-start.2 = (bf16[2,4,3,6,192]{4,3,2,1,0:T(8,128)(2,1)S(1)}, bf16[2,4,3,6,192]{4,3,2,1,0:T(8,128)(2,1)S(1)}, u32[]{:S(2)}, u32[]{:S(2)}) collective-permute-start(bf16[2,4,3,6,192]{4,3,2,1,0:T(8,128)(2,1)S(1)} %pad_maximum_fusion.3), channel_id=1, source_target_pairs={{0,7},{1,4},{2,5},{3,6},{4,3},{5,0},{6,1},{7,2},{8,15},{9,12},{10,... | collective-permute-start | bytes 165896 | tf_op jit(solution)/shard_map/ppermute | solution.py:421
  8.8 7.6 %collective-permute-start = (bf16[2,4,3,30,192]{4,3,2,1,0:T(8,128)(2,1)S(1)}, bf16[2,4,3,30,192]{4,3,2,1,0:T(8,128)(2,1)S(1)}, u32[]{:S(2)}, u32[]{:S(2)}) collective-permute-start(bf16[2,4,3,30,192]{4,3,2,1,0:T(8,128)(2,1)S(1)} %pad_maximum_fusion.1), channel_id=1, source_target_pairs={{0,3},{1,0},{2,1},{3,2},{4,7},{5,4},{6,5},{7,6},{8,11},{9,8},{10,9... | collective-permute-start | bytes 829448 | tf_op jit(solution)/shard_map/ppermute | solution.py:423
  9.6 4.8 %copy-start.3 = (bf16[192,576]{1,0:T(8,128)(2,1)S(1)}, bf16[192,576]{1,0:T(8,128)(2,1)}, u32[]{:S(2)}) copy-start(bf16[192,576]{1,0:T(8,128)(2,1)} %wqkv_ref.1) | copy-start | bytes 663556
  16.3 0.6 copy-start.11
  16.4 0.7 copy-start.12
  16.4 0.8 copy-start.9
  93.7 6.6 %copy-start.10 = (bf16[4,3,30,192]{3,2,1,0:T(8,128)(2,1)S(1)}, bf16[4,3,30,192]{3,2,1,0:T(8,128)(2,1)}, u32[]{:S(2)}) copy-start(bf16[4,3,30,192]{3,2,1,0:T(8,128)(2,1)} %get-tuple-element.15) | copy-start | bytes 414724
  93.7 8.4 %copy-start.14 = (bf16[4,3,6,192]{3,2,1,0:T(8,128)(2,1)S(1)}, bf16[4,3,6,192]{3,2,1,0:T(8,128)(2,1)}, u32[]{:S(2)}) copy-start(bf16[4,3,6,192]{3,2,1,0:T(8,128)(2,1)} %get-tuple-element.16) | copy-start | bytes 82948
  93.8 8.7 %copy-start.13 = (bf16[4,3,6,192]{3,2,1,0:T(8,128)(2,1)S(1)}, bf16[4,3,6,192]{3,2,1,0:T(8,128)(2,1)}, u32[]{:S(2)}) copy-start(bf16[4,3,6,192]{3,2,1,0:T(8,128)(2,1)} %get-tuple-element.17) | copy-start | bytes 82948
  94.6 24.8 %all-to-all-start.2 = ((bf16[16,16,1152]{2,1,0:T(8,128)(2,1)}), bf16[16,16,1152]{2,1,0:T(8,128)(2,1)S(1)}, u32[]{:S(2)}, u32[]{:S(2)}) async-start(bf16[16,16,1152]{2,1,0:T(8,128)(2,1)} %bitcast.15), calls=%async_computation.2 | async-start | bytes 1179648 | tf_op jit(solution)/shard_map/all_to_all | solution.py:408
  100.4 11.8 %collective-permute-start.3 = (bf16[4,3,30,192]{3,2,1,0:T(8,128)(2,1)S(1)}, bf16[4,3,30,192]{3,2,1,0:T(8,128)(2,1)S(1)}, u32[]{:S(2)}, u32[]{:S(2)}) collective-permute-start(bf16[4,3,30,192]{3,2,1,0:T(8,128)(2,1)S(1)} %copy-done.10), channel_id=1, source_target_pairs={{0,1},{1,2},{2,3},{3,0},{4,5},{5,6},{6,7},{7,4},{8,9},{9,10},{10,1... | collective-permute-start | bytes 414728 | tf_op jit(solution)/shard_map/ppermute | solution.py:433
  102.1 10.1 %collective-permute-start.4 = (bf16[4,3,6,192]{3,2,1,0:T(8,128)(2,1)S(1)}, bf16[4,3,6,192]{3,2,1,0:T(8,128)(2,1)S(1)}, u32[]{:S(2)}, u32[]{:S(2)}) collective-permute-start(bf16[4,3,6,192]{3,2,1,0:T(8,128)(2,1)S(1)} %copy-done.14), channel_id=1, source_target_pairs={{0,4},{4,0},{8,12},{12,8},{16,20},{20,16},{24,28},{28,24},{32,36},... | collective-permute-start | bytes 82952 | tf_op jit(solution)/shard_map/ppermute | solution.py:432
  102.4 9.8 %collective-permute-start.5 = (bf16[4,3,6,192]{3,2,1,0:T(8,128)(2,1)S(1)}, bf16[4,3,6,192]{3,2,1,0:T(8,128)(2,1)S(1)}, u32[]{:S(2)}, u32[]{:S(2)}) collective-permute-start(bf16[4,3,6,192]{3,2,1,0:T(8,128)(2,1)S(1)} %copy-done.13), channel_id=1, source_target_pairs={{0,5},{1,6},{2,7},{3,4},{4,1},{5,2},{6,3},{7,0},{8,13},{9,14},{10,... | collective-permute-start | bytes 82952 | tf_op jit(solution)/shard_map/ppermute | solution.py:431
  112.2 0.6 copy-start.7
  112.2 0.6 copy-start.8
  112.2 0.7 copy-start.5
  119.4 0.8 copy-start.2

commit v2 on v1

--- a/solution.py
+++ b/solution.py
@@ -19,22 +19,20 @@
 STRIPS = 3
 WINDOWS = 6
 TYPES = 12
-GROUP = ("y", "xl", "c")
-REST = ("z", "xh")
-PARTS = 16
-PART_ROWS = C // PARTS
-QKV_LANES = 640
-PROJ_LANES = 256
-W_LANES = QKV_LANES + PROJ_LANES
-B_LANES = 256
-B_PARTS = 13
+GROUP = ("y", "xh", "xl", "c")
+REST = "z"
+PARTS = 32
+W_PARTS = 24
+W_LANES = 384
+B_PARTS = 26
+B_LANES = 128
+GAIN_PART = 24
 SEND_LANES = W_LANES + B_LANES
 LATS = 4
-MIX_LANES = W_LANES + LATS * B_LANES
 WIDE = 3584
 f32 = jnp.float32
 bf16 = jnp.bfloat16
-VMEM_LIMIT = 56 * 1024 * 1024
+VMEM_LIMIT = 24 * 1024 * 1024
 
 NN = (((1,), (0,)), ((), ()))
 NT = (((1,), (1,)), ((), ()))
@@ -58,10 +56,16 @@
     return jnp.where(row == target, 1.0, 0.0).astype(bf16)
 
 
-def bias_kernel(table_ref, out_ref, wide, pairs):
+def prepare_kernel(table_ref, wqkv_ref, out_ref, w3_ref, w3t_ref, wide, pairs):
+    for k in range(3):
+        part = wqkv_ref[:, k * C : (k + 1) * C]
+        w3_ref[k] = part
+        if k:
+            w3t_ref[k - 1] = part.T
     wide[...] = jnp.zeros_like(wide)
-    for lz in range(2):
-        wide[lz * HEADS : (lz + 1) * HEADS, :TABLE] = table_ref[0, lz]
+    for h in range(HEADS):
+        for lz in range(2):
+            wide[lz * HEADS + h : lz * HEADS + h + 1, :TABLE] = table_ref[h, lz : lz + 1]
     pairs[...] = jnp.zeros_like(pairs)
     lane = lax.broadcasted_iota(jnp.int32, (16, 128), 1)
     for zl_j in range(PAIRS):
@@ -109,19 +113,24 @@
                 out_ref[t, n] = jnp.where(kept, out_ref[t, n], -1e30)
 
 
-def bias_dense(table):
+def prepare(table, wqkv):
+    vmem = pl.BlockSpec(memory_space=pltpu.VMEM)
     return pl.pallas_call(
-        bias_kernel,
-        out_shape=jax.ShapeDtypeStruct((TYPES, 2, WIN, 128), f32),
-        in_specs=[pl.BlockSpec(memory_space=pltpu.VMEM)],
-        out_specs=pl.BlockSpec(memory_space=pltpu.VMEM),
+        prepare_kernel,
+        out_shape=(
+            jax.ShapeDtypeStruct((TYPES, 2, WIN, 128), f32),
+            jax.ShapeDtypeStruct((3, C, C), bf16),
+            jax.ShapeDtypeStruct((2, C, C), bf16),
+        ),
+        in_specs=[vmem] * 2,
+        out_specs=(vmem,) * 3,
         scratch_shapes=[pltpu.VMEM((16, WIDE), f32), pltpu.VMEM((3, TYPES * 16, 128), f32)],
         compiler_params=pltpu.CompilerParams(vmem_limit_bytes=VMEM_LIMIT),
         cost_estimate=pl.CostEstimate(
-            flops=20_000_000_000, bytes_accessed=1_200_000, transcendentals=0
-        ),
-        name="bias_dense",
-    )(table)
+            flops=4_000_000_000, bytes_accessed=4_000_000, transcendentals=0
+        ),
+        name="prepare",
+    )(table, wqkv)
 
 
 def normalised(values):
@@ -169,8 +178,8 @@
         query = dot(tokens, w3_ref[0]).astype(bf16)
         key = dot(tokens, w3_ref[1]).astype(bf16)
         value = dot(tokens, w3_ref[2]).astype(bf16)
-        key_t = dot(w3t_ref[1], tokens, NT).astype(bf16)
-        value_t = dot(w3t_ref[2], tokens, NT).astype(bf16)
+        key_t = dot(w3t_ref[0], tokens, NT).astype(bf16)
+        value_t = dot(w3t_ref[1], tokens, NT).astype(bf16)
         mixed = dot(cot, wproj_ref[...], NT).astype(bf16)
         out_t = []
         grad_query_t = []
@@ -272,22 +281,26 @@
                 target = (slice(0, TYPES), slice(base, base + width))
                 wide[target] = jnp.where(inside, piece, wide[target])
 
-    tail = jnp.concatenate(
-        [gsum[0:1, :], jnp.zeros((16 - PART_ROWS - 1, C), f32)], axis=0
-    )
+    halves = []
+    for n in range(2):
+        if n == 0:
+            halves.append(wsum[:, :W_LANES])
+        else:
+            halves.append(jnp.concatenate([wsum[:, W_LANES:], psum[...]], axis=1))
     for p in range(PARTS):
-        lines = slice(p * PART_ROWS, (p + 1) * PART_ROWS)
-        first = jnp.concatenate([wsum[lines, :], jnp.zeros((4, 3 * C), f32)], axis=0)
-        send_out[p, :, 0 : 3 * C] = first.astype(bf16)
-        send_out[p, :, 3 * C : QKV_LANES] = jnp.zeros((16, QKV_LANES - 3 * C), bf16)
-        second = jnp.concatenate([psum[lines, :], tail], axis=0)
-        send_out[p, :, QKV_LANES : QKV_LANES + C] = second.astype(bf16)
-        send_out[p, :, QKV_LANES + C : W_LANES] = jnp.zeros((16, PROJ_LANES - C), bf16)
+        if p < W_PARTS:
+            lines = slice(p // 2 * 16, p // 2 * 16 + 16)
+            send_out[p, :, :W_LANES] = halves[p % 2][lines].astype(bf16)
+        elif p == GAIN_PART:
+            gains = jnp.concatenate([gsum[...], jnp.zeros((8, C), f32)], axis=0)
+            gains = jnp.concatenate([gains, jnp.zeros((16, W_LANES - C), f32)], axis=1)
+            send_out[p, :, :W_LANES] = gains.astype(bf16)
+        else:
+            send_out[p, :, :W_LANES] = jnp.zeros((16, W_LANES), bf16)
         if p < B_PARTS:
-            third = wide[:, p * B_LANES : (p + 1) * B_LANES].astype(bf16)
+            send_out[p, :, W_LANES:] = wide[:, p * B_LANES : (p + 1) * B_LANES].astype(bf16)
         else:
-            third = jnp.zeros((16, B_LANES), bf16)
-        send_out[p, :, W_LANES:] = third
+            send_out[p, :, W_LANES:] = jnp.zeros((16, B_LANES), bf16)
 
 
 def main(x, g, lat_in, lon_in, corner_in, gain, w3, w3t, wqkv, wproj, bias):
@@ -358,18 +371,22 @@
 
 
 def unpack_kernel(parts_ref, gain_out, wqkv_out, wproj_out, bias_out):
-    gain_out[...] = parts_ref[0, :, QKV_LANES : QKV_LANES + C].astype(f32)[12:13]
-    for p in range(PARTS):
-        lines = slice(p * PART_ROWS, (p + 1) * PART_ROWS)
-        wqkv_out[lines, :] = parts_ref[p, :, 0 : 3 * C].astype(f32)[:PART_ROWS]
-        wproj_out[lines, :] = parts_ref[p, :, QKV_LANES : QKV_LANES + C].astype(f32)[:PART_ROWS]
-        if p < B_PARTS:
-            width = min(B_LANES, TABLE - p * B_LANES)
-            block = parts_ref[p, :, W_LANES:].astype(f32)[:, :width]
+    gain_out[...] = parts_ref[GAIN_PART, :, :C].astype(f32)[:1]
+    for p in range(W_PARTS):
+        lines = slice(p // 2 * 16, p // 2 * 16 + 16)
+        block = parts_ref[p, :, :W_LANES].astype(f32)
+        if p % 2 == 0:
+            wqkv_out[lines, :W_LANES] = block
+        else:
+            wqkv_out[lines, W_LANES:] = block[:, :C]
+            wproj_out[lines, :] = block[:, C:]
+    for p in range(B_PARTS):
+        width = min(B_LANES, TABLE - p * B_LANES)
+        block = parts_ref[p, :, W_LANES:].astype(f32)[:, :width]
+        for h in range(HEADS):
             for lz in range(2):
-                bias_out[0, lz, :, p * B_LANES : p * B_LANES + width] = block[
-                    lz * HEADS : (lz + 1) * HEADS
-                ]
+                t = lz * HEADS + h
+                bias_out[h, lz : lz + 1, p * B_LANES : p * B_LANES + width] = block[t : t + 1]
 
 
 def unpack(parts):
@@ -380,7 +397,7 @@
             jax.ShapeDtypeStruct((1, C), f32),
             jax.ShapeDtypeStruct((C, 3 * C), f32),
             jax.ShapeDtypeStruct((C, C), f32),
-            jax.ShapeDtypeStruct((1, 2, HEADS, TABLE), f32),
+            jax.ShapeDtypeStruct((HEADS, 2, TABLE), f32),
         ),
         in_specs=[vmem],
         out_specs=(vmem,) * 4,
@@ -389,23 +406,26 @@
     )(parts)
 
 
-def summed(send):
-    lats = LATS
+def summed(send, ready):
+    others = PARTS // LATS
     got = lax.all_to_all(send, GROUP, 0, 0, tiled=True)
-    got = got.reshape((PARTS // lats, lats, 16, SEND_LANES)).astype(f32)
+    got = got.reshape((others, LATS, 16, SEND_LANES)).astype(f32)
     weights = jnp.sum(got[..., :W_LANES], axis=(0, 1))
-    bias = jnp.sum(got[..., W_LANES:], axis=0).transpose(1, 0, 2).reshape(16, lats * B_LANES)
-    mixed = jnp.concatenate([weights, bias], axis=1).astype(bf16)
+    bias = jnp.sum(got[..., W_LANES:], axis=0)
+    mixed = jnp.concatenate([weights] + [bias[n] for n in range(LATS)], axis=1).astype(bf16)
+    mixed, ready = lax.optimization_barrier((mixed, ready))
     count = lax.axis_size(REST)
     got = lax.all_to_all(
         jnp.broadcast_to(mixed[None], (count,) + mixed.shape), REST, 0, 0, tiled=True
     )
     total = jnp.sum(got.astype(f32), axis=0).astype(bf16)
-    weights = jnp.broadcast_to(total[None, None, :, :W_LANES], (PARTS // lats, lats, 16, W_LANES))
-    bias = total[:, W_LANES:].reshape(16, lats, B_LANES).transpose(1, 0, 2)
-    bias = jnp.broadcast_to(bias[None], (PARTS // lats, lats, 16, B_LANES))
-    spread = jnp.concatenate([weights, bias], axis=-1).reshape(send.shape)
-    return lax.all_to_all(spread, GROUP, 0, 0, tiled=True)
+    weights = total[:, :W_LANES]
+    rows = [
+        jnp.concatenate([weights, total[:, W_LANES + n * B_LANES : W_LANES + (n + 1) * B_LANES]], 1)
+        for n in range(LATS)
+    ]
+    spread = jnp.broadcast_to(jnp.stack(rows)[None], (others, LATS, 16, SEND_LANES))
+    return lax.all_to_all(spread.reshape(send.shape), GROUP, 0, 0, tiled=True), ready
 
 
 def on_device(x, g, ln_gain, w_qkv, w_proj, bias_table):
@@ -421,9 +441,7 @@
     corner_in = lax.ppermute(jnp.stack([x[:, :3, :6], g[:, :3, :6]]), both, corner_down)
     lon_in = lax.ppermute(jnp.stack([x[:, 3:, :6], g[:, 3:, :6]]), lon_axes, lon_swap)
     lat_in = lax.ppermute(jnp.stack([x[:, :3, 6:], g[:, :3, 6:]]), lat_axes, lat_down)
-    bias = bias_dense(bias_table)
-    w3 = w_qkv.reshape(C, 3, C).transpose(1, 0, 2)
-    w3t = w_qkv.T.reshape(3, C, C)
+    bias, w3, w3t = prepare(bias_table[0].transpose(1, 0, 2), w_qkv)
     gain = ln_gain.reshape(1, C)
     own, to_lat, to_lon, to_corner, send = main(
         x, g, lat_in, lon_in, corner_in, gain, w3, w3t, w_qkv, w_proj, bias
@@ -431,8 +449,10 @@
     back_corner = lax.ppermute(to_corner, both, corner_up)
     back_lon = lax.ppermute(to_lon, lon_axes, lon_swap)
     back_lat = lax.ppermute(to_lat, lat_axes, lat_up)
-    grad_gain, grad_wqkv, grad_wproj, grad_bias = unpack(summed(send))
+    parts, (back_lat, back_lon, back_corner) = summed(send, (back_lat, back_lon, back_corner))
+    grad_gain, grad_wqkv, grad_wproj, grad_bias = unpack(parts)
     grad_x = norm_grads(x, g, gain, own, back_lat, back_lon, back_corner)
+    grad_bias = grad_bias.transpose(1, 0, 2)[None]
     return grad_x, grad_gain.reshape(C), grad_wqkv, grad_wproj, grad_bias
 
 

time: 124 us -> 93.8 us (0.76)
  blocking collectives: 53.5 us -> 19.7 us
  waiting for transfers between devices: 7.3 us -> 20.3 us
  Pallas kernels: 33.8 us -> 26.1 us
  local copies, waits for them, and re-layouts: 10.2 us -> 4.31 us
  starting transfers between devices: 16.9 us -> 21.8 us
    all_to_all x1, blocking collectives: 37.9 us -> 19.7 us  [summed(): lax.all_to_all(jnp.broadcast_to(mixed[None], (count,) + mixed.shape), RES...]
    all_to_all x1 -> x2, waiting for transfers between devices: 0.01 us -> 15.8 us  [the longest x1 8.12 us: summed(): lax.all_to_all(spread.reshape(send.shape), GROUP, 0, 0, tiled=True)]
    all_to_all x1 -> x0, blocking collectives: 15.6 us -> none  [summed(): got = lax.all_to_all(send, GROUP, 0, 0, tiled=True)]
    ppermute x1, waiting for transfers between devices: 7.29 us -> 0.01 us  [on_device(): back_lon = lax.ppermute(to_lon, lon_axes, lon_swap)]
    unnamed x36 -> x15, local copies, waits for them, and re-layouts: 8.1 us -> 3.27 us
    all_to_all x1 -> x2, starting transfers between devices: 5.73 us -> 10.5 us  [the longest x1 5.47 us: summed(): got = lax.all_to_all(send, GROUP, 0, 0, tiled=True)]
    ppermute x1, waiting for transfers between devices: 0.01 us -> 3.21 us  [on_device(): lax.ppermute(jnp.stack([x[:, :3, 6:], g[:, :3, 6:]]), lat_axes, lat_down)]
    ppermute x1, starting transfers between devices: 0.34 us -> 2.98 us  [on_device(): back_lon = lax.ppermute(to_lon, lon_axes, lon_swap)]
  transfers between devices with their start and end apart: 7 -> 8, of which waited for: 1 -> 4; matrix products, arithmetic and copies ran while one was open for 4% -> 2% of each run, Pallas kernels for 7% -> 5%
where the time goes in v2:
time: 93.8 us; the launch traced here: 93.5 us
  Pallas kernels  26.1 us (28%)
  starting transfers between devices  21.8 us (23%)
  waiting for transfers between devices  20.3 us (22%)
  blocking collectives  19.7 us (21%)
  local copies, waits for them, and re-layouts  4.31 us (5%)
    pallas_call x1, Pallas kernels, main(): pl.pallas_call(main_kernel, out_shape=(jax.ShapeDtypeStruct((4, 3, 30, C)...  20.1 us
    all_to_all x1, blocking collectives, summed(): lax.all_to_all(jnp.broadcast_to(mixed[None], (count,) + mixed.shape), RES...  19.7 us
    all_to_all x1, waiting for transfers between devices, summed(): lax.all_to_all(spread.reshape(send.shape), GROUP, 0, 0, tiled=True)  8.12 us
    all_to_all x1, waiting for transfers between devices, summed(): got = lax.all_to_all(send, GROUP, 0, 0, tiled=True)  7.64 us
    all_to_all x1, starting transfers between devices, summed(): got = lax.all_to_all(send, GROUP, 0, 0, tiled=True)  5.47 us
    all_to_all x1, starting transfers between devices, summed(): lax.all_to_all(spread.reshape(send.shape), GROUP, 0, 0, tiled=True)  4.98 us
    ppermute x1, starting transfers between devices, on_device(): lax.ppermute(jnp.stack([x[:, 3:, :6], g[:, 3:, :6]]), lon_axes, lon_swap)  3.66 us
    unnamed x15, local copies, waits for them, and re-layouts  3.27 us
  transfers between devices with their start and end apart: 8, of which 4 were waited for; matrix products, arithmetic and copies ran while one was open for 2% of the time, Pallas kernels for 5%

profile of v2, /device:TPU:1, one launch (start us, length us, event | category | flops | bytes accessed | tf_op | source)
XLA Modules:
  0.0 93.5 jit_solution(13882757090613088831)
XLA Ops:
  0.6 1.1 %copy.30.x_ref = bf16[4,6,36,192]{3,2,1,0:T(8,128)(2,1)S(1)} copy(bf16[4,6,36,192]{3,0,2,1:T(4,128)(2,1)} %param.6) | data formatting | bytes 663552 | tf_op args[0]
  1.7 0.0 copy-start.1
  1.7 0.0 copy-start.2
  1.7 1.1 %copy.31.g_ref = bf16[4,6,36,192]{3,2,1,0:T(8,128)(2,1)S(1)} copy(bf16[4,6,36,192]{3,0,2,1:T(4,128)(2,1)} %param.7) | data formatting | bytes 663552 | tf_op args[1]
  2.9 3.7 %collective-permute-start.1 = (bf16[2,4,3,6,192]{4,3,2,1,0:T(8,128)(2,1)S(1)}, bf16[2,4,3,6,192]{4,3,2,1,0:T(8,128)(2,1)S(1)}, u32[]{:S(2)}, u32[]{:S(2)}) collective-permute-start(bf16[2,4,3,6,192]{4,3,2,1,0:T(8,128)(2,1)S(1)} %pad_maximum_fusion.1), channel_id=1, source_target_pairs={{0,4},{4,0},{8,12},{12,8},{16,20},{20,16},{24,28},{28,24},{32,36},... | collective-permute-start | bytes 165896 | tf_op jit(solution)/shard_map/ppermute | solution.py:442
  6.6 2.9 %collective-permute-start.2 = (bf16[2,4,3,6,192]{4,3,2,1,0:T(8,128)(2,1)S(1)}, bf16[2,4,3,6,192]{4,3,2,1,0:T(8,128)(2,1)S(1)}, u32[]{:S(2)}, u32[]{:S(2)}) collective-permute-start(bf16[2,4,3,6,192]{4,3,2,1,0:T(8,128)(2,1)S(1)} %pad_maximum_fusion.2), channel_id=1, source_target_pairs={{0,7},{1,4},{2,5},{3,6},{4,3},{5,0},{6,1},{7,2},{8,15},{9,12},{10,... | collective-permute-start | bytes 165896 | tf_op jit(solution)/shard_map/ppermute | solution.py:441
  9.5 0.1 slice_bitcast_fusion
  9.6 0.1 pad_maximum_fusion
  9.7 0.1 collective-permute-start
  9.8 0.0 copy-done.1
  9.8 0.0 copy-done.2
  9.8 0.0 copy-start
  9.9 0.0 copy-start.3
  9.9 2.6 %prepare.1 = (f32[12,2,144,128]{3,2,1,0:T(8,128)S(1)}, bf16[3,192,192]{2,1,0:T(8,128)(2,1)S(1)}, bf16[2,192,192]{2,1,0:T(8,128)(2,1)S(1)}) custom-call(f32[6,2,3312]{2,1,0:T(2,128)S(1)} %bitcast.50, bf16[192,576]{1,0:T(8,128)(2,1)S(1)} %copy-done.1), custom_call_target="tpu_custom_call" | custom-call | flops 4000000000 | bytes 4000000 | tf_op jit(solution)/shard_map/prepare/pallas_call | solution.py:118
  12.4 0.0 collective-permute-done.1.lon_ref
  12.5 1.4 %collective-permute-done.2.corner_ref = bf16[2,4,3,6,192]{4,3,2,1,0:T(8,128)(2,1)S(1)} collective-permute-done((bf16[2,4,3,6,192]{4,3,2,1,0:T(8,128)(2,1)S(1)}, bf16[2,4,3,6,192]{4,3,2,1,0:T(8,128)(2,1)S(1)}, u32[]{:S(2)}, u32[]{:S(2)}) %collective-permute-start.2) | collective-permute-done | bytes 55328 | tf_op jit(solution)/shard_map/ppermute | solution.py:441
  13.8 3.2 %collective-permute-done.lat_ref = bf16[2,4,3,30,192]{4,3,2,1,0:T(8,128)(2,1)S(1)} collective-permute-done((bf16[2,4,3,30,192]{4,3,2,1,0:T(8,128)(2,1)S(1)}, bf16[2,4,3,30,192]{4,3,2,1,0:T(8,128)(2,1)S(1)}, u32[]{:S(2)}, u32[]{:S(2)}) %collective-permute-start) | collective-permute-done | bytes 276512 | tf_op jit(solution)/shard_map/ppermute | solution.py:443
  17.0 0.0 copy-done
  17.0 0.0 copy-done.3
  17.0 20.1 %window_grads.1 = (bf16[4,3,30,192]{3,2,1,0:T(8,128)(2,1)S(1)}, bf16[4,3,30,192]{3,2,1,0:T(8,128)(2,1)S(1)}, bf16[4,3,6,192]{3,2,1,0:T(8,128)(2,1)S(1)}, bf16[4,...) custom-call(bf16[4,6,36,192]{3,2,1,0:T(8,128)(2,1)S(1)} %copy.30.x_ref, bf16[4,6,36,192]{3,2,1,0:T(8,128)(2,1)S(1)} %copy.31.g_ref, ...), custom_call_target="tpu_custom_call" | custom-call | flops 20000000000 | bytes 4000000 | tf_op jit(solution)/shard_map/window_grads/pallas_call | solution.py:308
  37.1 5.5 %all-to-all-start = ((bf16[32,16,512]{2,1,0:T(8,128)(2,1)}), bf16[32,16,512]{2,1,0:T(8,128)(2,1)S(1)}, u32[]{:S(2)}, u32[]{:S(2)}) async-start(bf16[32,16,512]{2,1,0:T(8,128)(2,1)} %get-tuple-element.25), calls=%async_computation | async-start | bytes 1048576 | tf_op jit(solution)/shard_map/all_to_all | solution.py:411
  42.6 3.0 %collective-permute-start.4 = (bf16[4,3,6,192]{3,2,1,0:T(8,128)(2,1)S(1)}, bf16[4,3,6,192]{3,2,1,0:T(8,128)(2,1)S(1)}, u32[]{:S(2)}, u32[]{:S(2)}) collective-permute-start(bf16[4,3,6,192]{3,2,1,0:T(8,128)(2,1)S(1)} %get-tuple-element.27), channel_id=1, source_target_pairs={{0,4},{4,0},{8,12},{12,8},{16,20},{20,16},{24,28},{28,24},{32,36},... | collective-permute-start | bytes 82952 | tf_op jit(solution)/shard_map/ppermute | solution.py:450
  45.6 1.4 %collective-permute-start.5 = (bf16[4,3,6,192]{3,2,1,0:T(8,128)(2,1)S(1)}, bf16[4,3,6,192]{3,2,1,0:T(8,128)(2,1)S(1)}, u32[]{:S(2)}, u32[]{:S(2)}) collective-permute-start(bf16[4,3,6,192]{3,2,1,0:T(8,128)(2,1)S(1)} %get-tuple-element.28), channel_id=1, source_target_pairs={{0,5},{1,6},{2,7},{3,4},{4,1},{5,2},{6,3},{7,0},{8,13},{9,14},{10,... | collective-permute-start | bytes 82952 | tf_op jit(solution)/shard_map/ppermute | solution.py:449
  47.0 0.3 collective-permute-start.3
  47.3 7.6 %all-to-all-done = bf16[32,16,512]{2,1,0:T(8,128)(2,1)S(1)} async-done(((bf16[32,16,512]{2,1,0:T(8,128)(2,1)}), bf16[32,16,512]{2,1,0:T(8,128)(2,1)S(1)}, u32[]{:S(2)}, u32[]{:S(2)}) %all-to-all-start) | async-done | bytes 524320 | tf_op jit(solution)/shard_map/all_to_all | solution.py:411
  55.0 0.1 bitcast_convert_fusion
  55.1 0.1 slice_reduce_fusion
  55.3 0.0 collective-permute-done.4.lon_ref
  55.3 0.0 collective-permute-done.5.corner_ref
  55.3 0.0 collective-permute-done.3.lat_ref
  55.3 19.7 %all_to_all.15 = bf16[8,16,896]{2,1,0:T(8,128)(2,1)S(1)} all-to-all(bf16[8,16,896]{2,1,0:T(8,128)(2,1)S(1)} %broadcast_in_dim.6), channel_id=1, replica_groups=mesh['z'=8,'y'=4,'xh'=2,'xl'=2,'c'=2] {'z'}, dimensions={0} | all-to-all | bytes 458752 | tf_op jit(solution)/shard_map/all_to_all | solution.py:418
  75.1 0.9 broadcast_in_dim.7
  76.0 5.0 %all-to-all-start.2 = ((bf16[32,16,512]{2,1,0:T(8,128)(2,1)}), bf16[32,16,512]{2,1,0:T(8,128)(2,1)S(1)}, u32[]{:S(2)}, u32[]{:S(2)}) async-start(bf16[32,16,512]{2,1,0:T(8,128)(2,1)} %bitcast.19), calls=%async_computation.2 | async-start | bytes 1048576 | tf_op jit(solution)/shard_map/all_to_all | solution.py:428
  81.0 2.4 %norm_grads.1 = bf16[4,6,36,192]{3,2,1,0:T(8,128)(2,1)S(1)} custom-call(bf16[4,6,36,192]{3,2,1,0:T(8,128)(2,1)S(1)} %copy.30.x_ref, bf16[4,6,36,192]{3,2,1,0:T(8,128)(2,1)S(1)} %copy.31.g_ref, f32[1,192]{1,0:T(1,128)S(1)} %bitcast.49, bf16[4,3,30,192]{3,2,1,0:T(8,128)(2,1)S(1)} %get-tuple-element.24.own_ref, ...), custom_call_target="tpu_custom_call" | custom-call | flops 10000000 | bytes 1500000 | tf_op jit(solution)/shard_map/norm_grads/pallas_call | solution.py:360
  83.4 1.0 %copy.32 = bf16[4,6,36,192]{3,0,2,1:T(4,128)(2,1)} copy(bf16[4,6,36,192]{3,2,1,0:T(8,128)(2,1)S(1)} %norm_grads.1) | data formatting | bytes 663552
  84.4 8.1 %all-to-all-done.2.parts_ref = bf16[32,16,512]{2,1,0:T(8,128)(2,1)S(1)} async-done(((bf16[32,16,512]{2,1,0:T(8,128)(2,1)}), bf16[32,16,512]{2,1,0:T(8,128)(2,1)S(1)}, u32[]{:S(2)}, u32[]{:S(2)}) %all-to-all-start.2) | async-done | bytes 524320 | tf_op jit(solution)/shard_map/all_to_all | solution.py:428
  92.5 0.9 unpack.1
  (16 shorter events, 0.2 us)
Async XLA Ops:
  1.7 8.1 %copy-start.1 = (bf16[192,576]{1,0:T(8,128)(2,1)S(1)}, bf16[192,576]{1,0:T(8,128)(2,1)}, u32[]{:S(2)}) copy-start(bf16[192,576]{1,0:T(8,128)(2,1)} %wqkv_ref.3) | copy-start | bytes 663556
  1.7 8.1 %copy-start.2 = (f32[1,2,6,3312]{3,1,2,0:T(2,128)S(1)}, f32[1,2,6,3312]{3,1,2,0:T(2,128)}, u32[]{:S(2)}) copy-start(f32[1,2,6,3312]{3,1,2,0:T(2,128)} %param.11) | copy-start | bytes 476932
  2.9 9.5 %collective-permute-start.1 = (bf16[2,4,3,6,192]{4,3,2,1,0:T(8,128)(2,1)S(1)}, bf16[2,4,3,6,192]{4,3,2,1,0:T(8,128)(2,1)S(1)}, u32[]{:S(2)}, u32[]{:S(2)}) collective-permute-start(bf16[2,4,3,6,192]{4,3,2,1,0:T(8,128)(2,1)S(1)} %pad_maximum_fusion.1), channel_id=1, source_target_pairs={{0,4},{4,0},{8,12},{12,8},{16,20},{20,16},{24,28},{28,24},{32,36},... | collective-permute-start | bytes 165896 | tf_op jit(solution)/shard_map/ppermute | solution.py:442
  6.6 7.2 %collective-permute-start.2 = (bf16[2,4,3,6,192]{4,3,2,1,0:T(8,128)(2,1)S(1)}, bf16[2,4,3,6,192]{4,3,2,1,0:T(8,128)(2,1)S(1)}, u32[]{:S(2)}, u32[]{:S(2)}) collective-permute-start(bf16[2,4,3,6,192]{4,3,2,1,0:T(8,128)(2,1)S(1)} %pad_maximum_fusion.2), channel_id=1, source_target_pairs={{0,7},{1,4},{2,5},{3,6},{4,3},{5,0},{6,1},{7,2},{8,15},{9,12},{10,... | collective-permute-start | bytes 165896 | tf_op jit(solution)/shard_map/ppermute | solution.py:441
  9.7 7.3 %collective-permute-start = (bf16[2,4,3,30,192]{4,3,2,1,0:T(8,128)(2,1)S(1)}, bf16[2,4,3,30,192]{4,3,2,1,0:T(8,128)(2,1)S(1)}, u32[]{:S(2)}, u32[]{:S(2)}) collective-permute-start(bf16[2,4,3,30,192]{4,3,2,1,0:T(8,128)(2,1)S(1)} %pad_maximum_fusion), channel_id=1, source_target_pairs={{0,3},{1,0},{2,1},{3,2},{4,7},{5,4},{6,5},{7,6},{8,11},{9,8},{10,9... | collective-permute-start | bytes 829448 | tf_op jit(solution)/shard_map/ppermute | solution.py:443
  9.8 7.2 %copy-start = (f32[192]{0:T(256)S(1)}, f32[192]{0:T(256)}, u32[]{:S(2)}) copy-start(f32[192]{0:T(256)} %param.8) | copy-start | bytes 2308
  9.9 7.2 %copy-start.3 = (bf16[192,192]{1,0:T(8,128)(2,1)S(1)}, bf16[192,192]{1,0:T(8,128)(2,1)}, u32[]{:S(2)}) copy-start(bf16[192,192]{1,0:T(8,128)(2,1)} %wproj_ref.1) | copy-start | bytes 221188
  37.1 17.8 %all-to-all-start = ((bf16[32,16,512]{2,1,0:T(8,128)(2,1)}), bf16[32,16,512]{2,1,0:T(8,128)(2,1)S(1)}, u32[]{:S(2)}, u32[]{:S(2)}) async-start(bf16[32,16,512]{2,1,0:T(8,128)(2,1)} %get-tuple-element.25), calls=%async_computation | async-start | bytes 1048576 | tf_op jit(solution)/shard_map/all_to_all | solution.py:411
  42.6 12.7 %collective-permute-start.4 = (bf16[4,3,6,192]{3,2,1,0:T(8,128)(2,1)S(1)}, bf16[4,3,6,192]{3,2,1,0:T(8,128)(2,1)S(1)}, u32[]{:S(2)}, u32[]{:S(2)}) collective-permute-start(bf16[4,3,6,192]{3,2,1,0:T(8,128)(2,1)S(1)} %get-tuple-element.27), channel_id=1, source_target_pairs={{0,4},{4,0},{8,12},{12,8},{16,20},{20,16},{24,28},{28,24},{32,36},... | collective-permute-start | bytes 82952 | tf_op jit(solution)/shard_map/ppermute | solution.py:450
  45.6 9.7 %collective-permute-start.5 = (bf16[4,3,6,192]{3,2,1,0:T(8,128)(2,1)S(1)}, bf16[4,3,6,192]{3,2,1,0:T(8,128)(2,1)S(1)}, u32[]{:S(2)}, u32[]{:S(2)}) collective-permute-start(bf16[4,3,6,192]{3,2,1,0:T(8,128)(2,1)S(1)} %get-tuple-element.28), channel_id=1, source_target_pairs={{0,5},{1,6},{2,7},{3,4},{4,1},{5,2},{6,3},{7,0},{8,13},{9,14},{10,... | collective-permute-start | bytes 82952 | tf_op jit(solution)/shard_map/ppermute | solution.py:449
  47.0 8.3 %collective-permute-start.3 = (bf16[4,3,30,192]{3,2,1,0:T(8,128)(2,1)S(1)}, bf16[4,3,30,192]{3,2,1,0:T(8,128)(2,1)S(1)}, u32[]{:S(2)}, u32[]{:S(2)}) collective-permute-start(bf16[4,3,30,192]{3,2,1,0:T(8,128)(2,1)S(1)} %get-tuple-element.26), channel_id=1, source_target_pairs={{0,1},{1,2},{2,3},{3,0},{4,5},{5,6},{6,7},{7,4},{8,9},{9,10},{10,1... | collective-permute-start | bytes 414728 | tf_op jit(solution)/shard_map/ppermute | solution.py:451
  76.0 16.5 %all-to-all-start.2 = ((bf16[32,16,512]{2,1,0:T(8,128)(2,1)}), bf16[32,16,512]{2,1,0:T(8,128)(2,1)S(1)}, u32[]{:S(2)}, u32[]{:S(2)}) async-start(bf16[32,16,512]{2,1,0:T(8,128)(2,1)} %bitcast.19), calls=%async_computation.2 | async-start | bytes 1048576 | tf_op jit(solution)/shard_map/all_to_all | solution.py:428

commit v3 on v2

v3 whole, which is shorter than its diff:
```python
import functools

import jax
import jax.numpy as jnp
from jax import lax
from jax.experimental import pallas as pl
from jax.experimental.pallas import tpu as pltpu
from jax.sharding import Mesh, PartitionSpec as P

C = 192
HEADS = 6
HEAD_DIM = 32
WLON = 12
WIN = 144
TABLE = 3312
PAIRS = 12
OFFSETS = 23
LOG2E = 1.4426950408889634
SCALE = HEAD_DIM**-0.5
BODY = 120
TAIL = 24
MAIN = 128
LEFT = 16
SHARED = HEADS * LEFT
STRIPS = 3
WINDOWS = 6
TYPES = 12
GROUP = ("y", "xh", "xl", "c")
REST = "z"
PARTS = 32
W_PARTS = 24
W_LANES = 384
B_PARTS = 26
B_LANES = 128
GAIN_PART = 24
SEND_LANES = W_LANES + B_LANES
LATS = 4
WIDE = 3584
f32 = jnp.float32
bf16 = jnp.bfloat16
VMEM_LIMIT = 40 * 1024 * 1024

NN = (((1,), (0,)), ((), ()))
NT = (((1,), (1,)), ((), ()))


def dot(a, b, dims=NN):
    return lax.dot_general(a, b, dims, preferred_element_type=f32)


def table_offset(zl_i, zl_j):
    li, zi = divmod(zl_i, 2)
    lj, zj = divmod(zl_j, 2)
    return (((zi * 2 + zj) * 6 + li) * 6 + lj) * OFFSETS


def iota(shape, dim):
    return lax.broadcasted_iota(jnp.int32, shape, dim)


def ones_where(condition):
    return jnp.where(condition, 1.0, 0.0).astype(bf16)


def query_index(column):
    return jnp.where(column < MAIN, column, MAIN + column % LEFT)


def offset_match(oj, transposed):
    shape = (2 * MAIN, PAIRS * 32) if transposed else (PAIRS * 32, 2 * MAIN)
    row, col = iota(shape, 1 if transposed else 0), iota(shape, 0 if transposed else 1)
    token = query_index(col)
    zl = token // WLON
    target = zl * 32 + (oj + 11) - (token - zl * WLON)
    return ones_where((row == target) & (col < MAIN + SHARED))


def window_order(transposed):
    dest, source = iota((WIN, WIN), 1 if transposed else 0), iota((WIN, WIN), 0 if transposed else 1)
    window = dest // 24
    lz = window // STRIPS
    strip = window - lz * STRIPS
    inside = dest - window * 24
    zi = inside // WLON
    longitude = strip * WLON + inside - zi * WLON
    level = (2 * lz + zi + 1) % 4
    return ones_where(source == 4 * longitude + level)


def prepare_kernel(
    table_ref, wqkv_ref, wproj_ref, x_ref, g_ref,
    main_ref, left_ref, w3_ref, w3t_ref, wprojt_ref, own_ref, wide, pairs,
):
    for k in range(3):
        part = wqkv_ref[:, k * C : (k + 1) * C]
        w3_ref[k] = part
        w3t_ref[k * C : (k + 1) * C] = part.T
    wprojt_ref[...] = wproj_ref[...].T
    for a in range(3):
        own_ref[0, a] = x_ref[a + 3, 6:36].reshape(BODY, C)
        own_ref[1, a] = g_ref[a + 3, 6:36].reshape(BODY, C)
    wide[...] = jnp.zeros_like(wide)
    for h in range(HEADS):
        for lz in range(2):
            wide[lz * HEADS + h : lz * HEADS + h + 1, :TABLE] = table_ref[h, lz : lz + 1] * LOG2E
    pairs[...] = jnp.zeros_like(pairs)
    lane = iota((16, 128), 1)
    for zl_j in range(PAIRS):
        for v in range(3):
            total = jnp.zeros((16, 128), f32)
            for q in range(4):
                off = table_offset(4 * v + q, zl_j)
                base, rest = off // 128 * 128, off % 128
                width = 128 if rest + OFFSETS <= 128 else 256
                piece = wide[:, base : base + width]
                shift = (32 * q - rest) % width
                if shift:
                    piece = pltpu.roll(piece, shift, 1)
                inside = (lane >= 32 * q) & (lane < 32 * q + OFFSETS)
                total = jnp.where(inside, piece[:, :128], total)
            pairs[v, pl.ds(zl_j, TYPES, stride=16), :] = total[:TYPES]
    full = jnp.concatenate([pairs[v] for v in range(3)], axis=1)
    high = full.astype(bf16)
    rest = full - high.astype(f32)
    middle = rest.astype(bf16)
    low = (rest - middle.astype(f32)).astype(bf16)
    lane_head = iota((PAIRS, MAIN), 1) // LEFT
    for oj in range(WLON):
        match = offset_match(oj, False)
        dense = dot(high, match) + (dot(middle, match) + dot(low, match))
        for lz in range(2):
            left = jnp.zeros((PAIRS, MAIN), f32)
            for h in range(HEADS):
                t = lz * HEADS + h
                block = dense[t * 16 : t * 16 + PAIRS]
                main_ref[t, pl.ds(oj, PAIRS, stride=WLON), :] = block[:, :MAIN]
                left = jnp.where(lane_head == h, block[:, MAIN:], left)
            left_ref[lz, pl.ds(oj, PAIRS, stride=WLON), :] = left
    lat = lax.axis_index("xl") * 2 + lax.axis_index("c")
    last_band = (lat == LATS - 1).astype(jnp.int32)

    def region(token, last_level):
        upper = (token // WLON) % 2 * (2 * last_level)
        return upper + jnp.where(token >= 72, last_band, 0)

    j = iota((WIN, MAIN), 0)
    column = iota((WIN, MAIN), 1)
    for lz in range(2):
        allowed = region(column, lz) == region(j, lz)
        for h in range(HEADS):
            t = lz * HEADS + h
            main_ref[t] = jnp.where(allowed, main_ref[t], -1e30)
        allowed = region(query_index(column + MAIN), lz) == region(j, lz)
        left_ref[lz] = jnp.where(allowed, left_ref[lz], -1e30)


def prepare(table, wqkv, wproj, x, g):
    vmem = pl.BlockSpec(memory_space=pltpu.VMEM)
    return pl.pallas_call(
        prepare_kernel,
        out_shape=(
            jax.ShapeDtypeStruct((TYPES, WIN, MAIN), f32),
            jax.ShapeDtypeStruct((2, WIN, MAIN), f32),
            jax.ShapeDtypeStruct((3, C, C), bf16),
            jax.ShapeDtypeStruct((3 * C, C), bf16),
            jax.ShapeDtypeStruct((C, C), bf16),
            jax.ShapeDtypeStruct((2, 3, BODY, C), bf16),
        ),
        in_specs=[vmem] * 5,
        out_specs=(vmem,) * 6,
        scratch_shapes=[pltpu.VMEM((16, WIDE), f32), pltpu.VMEM((3, TYPES * 16, 128), f32)],
        compiler_params=pltpu.CompilerParams(vmem_limit_bytes=VMEM_LIMIT),
        cost_estimate=pl.CostEstimate(
            flops=4_000_000_000, bytes_accessed=4_000_000, transcendentals=0
        ),
        name="prepare",
    )(table, wqkv, wproj, x, g)


def normalised(values):
    mean = jnp.mean(values, axis=-1, keepdims=True)
    centred = values - mean
    inverse = lax.rsqrt(jnp.mean(centred * centred, axis=-1, keepdims=True) + 1e-05)
    return centred * inverse, inverse


def main_kernel(
    own_ref, lat_ref, lon_ref, corner_ref, gain_ref, w3_ref, w3t_ref, wproj_ref, wprojt_ref,
    bias_ref, left_ref, own_out, lat_out, lon_out, corner_out, send_out,
    xw, gw, rows, standard_ref, cot_ref, query_ref, key_ref, value_ref, mixed_ref, tokens_t_ref,
    qkv_t_ref, mixed_t_ref, scores_ref, grad_attend_ref, half_ref, grad_half_ref, dense, dense_left,
    wsum, psum, gsum, spread, wide, grads,
):
    order = window_order(False)
    for a in range(6):
        for k, to in enumerate((xw, gw)):
            if a < 3:
                body, tail = own_ref[k, a], lon_ref[k, a].reshape(TAIL, C)
            else:
                body = lat_ref[k, a - 3].reshape(BODY, C)
                tail = corner_ref[k, a - 3].reshape(TAIL, C)
            line = dot(order[:, :BODY], body) + dot(order[:, BODY:], tail)
            for w in range(WINDOWS):
                to[w, 24 * a : 24 * a + 24, :] = line[24 * w : 24 * w + 24]
    dense[...] = jnp.zeros_like(dense)
    dense_left[...] = jnp.zeros_like(dense_left)
    wsum[...] = jnp.zeros_like(wsum)
    psum[...] = jnp.zeros_like(psum)
    gsum[...] = jnp.zeros_like(gsum)
    gain = gain_ref[...]
    lane_head = iota((WIN, C), 1) // HEAD_DIM
    shape = (WIN, MAIN)
    repeat = ones_where((iota(shape, 0) == MAIN + iota(shape, 1) % LEFT) & (iota(shape, 1) < SHARED))
    shape = (MAIN, WIN)
    repeat_t = ones_where((iota(shape, 1) == MAIN + iota(shape, 0) % LEFT) & (iota(shape, 0) < SHARED))
    shape = (LEFT, MAIN)
    gather = ones_where((iota(shape, 0) == iota(shape, 1) % LEFT) & (iota(shape, 1) < SHARED))
    own_head_t = iota((C, MAIN), 0) // HEAD_DIM == iota((C, MAIN), 1) // LEFT
    own_head = iota((MAIN, C), 1) // HEAD_DIM == iota((MAIN, C), 0) // LEFT

    def of_head(value, h):
        return jnp.where(lane_head[: value.shape[0]] == h, value, jnp.zeros_like(value))

    def stacked(value):
        return jnp.concatenate([of_head(value, h) for h in range(HEADS)], axis=0)

    def only_head(mask, value):
        return jnp.where(mask, value, jnp.zeros_like(value)).astype(bf16)

    standard, _ = normalised(xw[...].reshape(WINDOWS * WIN, C))
    standard_ref[...] = standard
    scaled = standard * gain
    tokens = scaled.astype(bf16)
    cots = gw[...].reshape(WINDOWS * WIN, C).astype(bf16)
    cot_ref[...] = cots
    query_ref[...] = dot(tokens, w3_ref[0]).astype(bf16)
    key_ref[...] = dot(tokens, w3_ref[1]).astype(bf16)
    value_ref[...] = dot(tokens, w3_ref[2]).astype(bf16)
    mixed_ref[...] = dot(cots, wprojt_ref[...]).astype(bf16)
    for w in range(WINDOWS):
        tokens_t = scaled[w * WIN : (w + 1) * WIN].T.astype(bf16)
        tokens_t_ref[w] = tokens_t
        qkv_t_ref[w] = dot(w3t_ref[...], tokens_t).astype(bf16)
        mixed_t_ref[w] = dot(wproj_ref[...], gw[w].T.astype(bf16)).astype(bf16)

    for w in range(WINDOWS):
        lz = w // STRIPS
        span = slice(w * WIN, (w + 1) * WIN)
        query_t, mixed_t = qkv_t_ref[w, 0:C], mixed_t_ref[w]
        key, value = key_ref[span], value_ref[span]
        scores_ref[w, : HEADS * WIN] = dot(stacked(key), query_t[:, :MAIN])
        scores_ref[w, HEADS * WIN :] = dot(key, only_head(own_head_t, dot(query_t, repeat)))
        grad_attend_ref[w, : HEADS * WIN] = dot(stacked(value), mixed_t[:, :MAIN])
        grad_attend_ref[w, HEADS * WIN :] = dot(value, only_head(own_head_t, dot(mixed_t, repeat)))
        for t in range(HEADS + 1):
            lines = slice(t * WIN, (t + 1) * WIN)
            columns = slice(t * MAIN, (t + 1) * MAIN)
            bias = bias_ref[lz * HEADS + t] if t < HEADS else left_ref[lz]
            scores = scores_ref[w, lines] * (SCALE * LOG2E) + bias
            top = jnp.max(scores, axis=0, keepdims=True)
            powers = jnp.exp2(scores - top)
            attend = powers * (1.0 / jnp.sum(powers, axis=0, keepdims=True))
            half_ref[w, :, columns] = attend.astype(bf16)
            grad_attend = grad_attend_ref[w, lines]
            total = jnp.sum(attend * grad_attend, axis=0, keepdims=True)
            grad_scores = attend * (grad_attend - total)
            grad_half_ref[w, :, columns] = grad_scores.astype(bf16)
            if t < HEADS:
                dense[lz * HEADS + t] += grad_scores
            else:
                dense_left[lz] += grad_scores

    for w in range(WINDOWS):
        span = slice(w * WIN, (w + 1) * WIN)

        def per_query(left, right_ref):
            parts = [
                dot(
                    left[h * HEAD_DIM : (h + 1) * HEAD_DIM],
                    right_ref[w, :, h * MAIN : (h + 1) * MAIN],
                )
                for h in range(HEADS)
            ]
            shared = dot(left, right_ref[w, :, HEADS * MAIN :])
            return jnp.concatenate(parts, axis=0), jnp.where(own_head_t, shared, 0.0)

        def per_key(left_ref, right):
            parts = [of_head(right[:MAIN], h) for h in range(HEADS)]
            parts.append(only_head(own_head, dot(repeat_t, right)))
            return dot(left_ref[w], jnp.concatenate(parts, axis=0))

        cot = cot_ref[span]
        out_t, out_left = per_query(qkv_t_ref[w, 2 * C :], half_ref)
        psum[...] += dot(out_t.astype(bf16), cot[:MAIN]) + dot(
            out_left.astype(bf16), dot(repeat_t, cot).astype(bf16)
        )
        query_grad, query_left = per_query(qkv_t_ref[w, C : 2 * C], grad_half_ref)
        first = slice(w * WIN, w * WIN + MAIN)
        last = slice(w * WIN + MAIN, (w + 1) * WIN)
        spread[first, 0:C] = (query_grad * SCALE).T
        spread[last, 0:C] = dot(gather, (query_left * SCALE).T.astype(bf16))
        spread[span, C : 2 * C] = per_key(grad_half_ref, query_ref[span]) * SCALE
        spread[span, 2 * C :] = per_key(half_ref, mixed_ref[span])

    grad_projected = spread[...].astype(bf16)
    back = dot(grad_projected, w3t_ref[...]).astype(bf16).astype(f32)
    rows[...] = back.reshape(WINDOWS, WIN, C)
    gsum[0:1, :] = jnp.sum(back * standard_ref[...], axis=0, keepdims=True)
    for w in range(WINDOWS):
        wsum[...] += dot(tokens_t_ref[w], grad_projected[w * WIN : (w + 1) * WIN])

    order_t = window_order(True)
    for a in range(6):
        line = jnp.concatenate([rows[w, 24 * a : 24 * a + 24, :] for w in range(WINDOWS)], axis=0)
        line = dot(order_t, line.astype(bf16))
        body, tail = line[:BODY].astype(bf16), line[BODY:].astype(bf16)
        if a < 3:
            own_out[a], lon_out[a] = body, tail
        else:
            lat_out[a - 3], corner_out[a - 3] = body, tail

    total = jnp.zeros((TYPES * 16, PAIRS * 32), f32)
    lane_left = iota((PAIRS, MAIN), 1) // LEFT
    for oj in range(WLON):
        picked = []
        for lz in range(2):
            left = dense_left[lz, pl.ds(oj, PAIRS, stride=WLON), :]
            for h in range(HEADS):
                first = dense[lz * HEADS + h, pl.ds(oj, PAIRS, stride=WLON), :]
                both = jnp.concatenate([first, jnp.where(lane_left == h, left, 0.0)], axis=1)
                picked += [both, jnp.zeros((4, 2 * MAIN), f32)]
        picked = jnp.concatenate(picked, axis=0)
        high = picked.astype(bf16)
        low = (picked - high.astype(f32)).astype(bf16)
        match = offset_match(oj, True)
        total += dot(high, match) + dot(low, match)
    for v in range(3):
        grads[v] = total[:, 128 * v : 128 * (v + 1)]
    wide[...] = jnp.zeros_like(wide)
    lane = iota((TYPES, 256), 1)
    for zl_j in range(PAIRS):
        for v in range(3):
            four = grads[v, pl.ds(zl_j, TYPES, stride=16), :]
            for q in range(4):
                off = table_offset(4 * v + q, zl_j)
                base, rest = off // 128 * 128, off % 128
                width = 128 if rest + OFFSETS <= 128 else 256
                piece = four
                if width == 256:
                    piece = jnp.concatenate([four, jnp.zeros_like(four)], axis=1)
                shift = (rest - 32 * q) % width
                if shift:
                    piece = pltpu.roll(piece, shift, 1)
                position = lane[:, :width]
                inside = (position >= rest) & (position < rest + OFFSETS)
                target = (slice(0, TYPES), slice(base, base + width))
                wide[target] = jnp.where(inside, piece, wide[target])

    halves = []
    for n in range(2):
        if n == 0:
            halves.append(wsum[:, :W_LANES])
        else:
            halves.append(jnp.concatenate([wsum[:, W_LANES:], psum[...]], axis=1))
    for p in range(PARTS):
        if p < W_PARTS:
            lines = slice(p // 2 * 16, p // 2 * 16 + 16)
            send_out[p, :, :W_LANES] = halves[p % 2][lines].astype(bf16)
        elif p == GAIN_PART:
            gains = jnp.concatenate([gsum[...], jnp.zeros((8, C), f32)], axis=0)
            gains = jnp.concatenate([gains, jnp.zeros((16, W_LANES - C), f32)], axis=1)
            send_out[p, :, :W_LANES] = gains.astype(bf16)
        else:
            send_out[p, :, :W_LANES] = jnp.zeros((16, W_LANES), bf16)
        if p < B_PARTS:
            send_out[p, :, W_LANES:] = wide[:, p * B_LANES : (p + 1) * B_LANES].astype(bf16)
        else:
            send_out[p, :, W_LANES:] = jnp.zeros((16, B_LANES), bf16)


def main(own, lat_in, lon_in, corner_in, gain, w3, w3t, wproj, wproj_t, bias, bias_left):
    vmem = pl.BlockSpec(memory_space=pltpu.VMEM)
    return pl.pallas_call(
        main_kernel,
        out_shape=(
            jax.ShapeDtypeStruct((3, BODY, C), bf16),
            jax.ShapeDtypeStruct((3, BODY, C), bf16),
            jax.ShapeDtypeStruct((3, TAIL, C), bf16),
            jax.ShapeDtypeStruct((3, TAIL, C), bf16),
            jax.ShapeDtypeStruct((PARTS, 16, SEND_LANES), bf16),
        ),
        in_specs=[vmem] * 11,
        out_specs=(vmem,) * 5,
        scratch_shapes=[
            pltpu.VMEM((WINDOWS, WIN, C), f32),
            pltpu.VMEM((WINDOWS, WIN, C), f32),
            pltpu.VMEM((WINDOWS, WIN, C), f32),
            pltpu.VMEM((WINDOWS * WIN, C), f32),
            pltpu.VMEM((WINDOWS * WIN, C), bf16),
            pltpu.VMEM((WINDOWS * WIN, C), bf16),
            pltpu.VMEM((WINDOWS * WIN, C), bf16),
            pltpu.VMEM((WINDOWS * WIN, C), bf16),
            pltpu.VMEM((WINDOWS * WIN, C), bf16),
            pltpu.VMEM((WINDOWS, C, WIN), bf16),
            pltpu.VMEM((WINDOWS, 3 * C, WIN), bf16),
            pltpu.VMEM((WINDOWS, C, WIN), bf16),
            pltpu.VMEM((WINDOWS, (HEADS + 1) * WIN, MAIN), f32),
            pltpu.VMEM((WINDOWS, (HEADS + 1) * WIN, MAIN), f32),
            pltpu.VMEM((WINDOWS, WIN, (HEADS + 1) * MAIN), bf16),
            pltpu.VMEM((WINDOWS, WIN, (HEADS + 1) * MAIN), bf16),
            pltpu.VMEM((TYPES, WIN, MAIN), f32),
            pltpu.VMEM((2, WIN, MAIN), f32),
            pltpu.VMEM((C, 3 * C), f32),
            pltpu.VMEM((C, C), f32),
            pltpu.VMEM((8, C), f32),
            pltpu.VMEM((WINDOWS * WIN, 3 * C), f32),
            pltpu.VMEM((16, WIDE), f32),
            pltpu.VMEM((3, TYPES * 16, 128), f32),
        ],
        compiler_params=pltpu.CompilerParams(vmem_limit_bytes=VMEM_LIMIT),
        cost_estimate=pl.CostEstimate(
            flops=20_000_000_000, bytes_accessed=4_000_000, transcendentals=750_000
        ),
        name="window_grads",
    )(own, lat_in, lon_in, corner_in, gain, w3, w3t, wproj, wproj_t, bias, bias_left)


def norm_kernel(x_ref, g_ref, gain_ref, own_ref, lat_ref, lon_ref, corner_ref, out_ref):
    gain = gain_ref[...]
    for a in range(6):
        if a < 3:
            head, body = corner_ref[a], lat_ref[a]
        else:
            head, body = lon_ref[a - 3], own_ref[a - 3]
        grad = jnp.concatenate([head.astype(f32), body.astype(f32)], axis=0)
        standard, inverse = normalised(x_ref[a].reshape(WIN, C).astype(f32))
        scaled = grad * gain
        local = inverse * (
            scaled
            - jnp.mean(scaled, axis=-1, keepdims=True)
            - standard * jnp.mean(scaled * standard, axis=-1, keepdims=True)
        )
        total = (g_ref[a].reshape(WIN, C).astype(f32) + local).astype(bf16)
        out_ref[a] = total.reshape(36, 4, C)


def norm_grads(x, g, gain, own, lat_in, lon_in, corner_in):
    vmem = pl.BlockSpec(memory_space=pltpu.VMEM)
    return pl.pallas_call(
        norm_kernel,
        out_shape=jax.ShapeDtypeStruct(x.shape, bf16),
        in_specs=[vmem] * 7,
        out_specs=vmem,
        compiler_params=pltpu.CompilerParams(vmem_limit_bytes=VMEM_LIMIT),
        cost_estimate=pl.CostEstimate(
            flops=10_000_000, bytes_accessed=1_500_000, transcendentals=1000
        ),
        name="norm_grads",
    )(x, g, gain, own, lat_in, lon_in, corner_in)


def unpack_kernel(parts_ref, gain_out, wqkv_out, wproj_out, bias_out):
    gain_out[...] = parts_ref[GAIN_PART, :, :C].astype(f32)[:1]
    for p in range(W_PARTS):
        lines = slice(p // 2 * 16, p // 2 * 16 + 16)
        block = parts_ref[p, :, :W_LANES].astype(f32)
        if p % 2 == 0:
            wqkv_out[lines, :W_LANES] = block
        else:
            wqkv_out[lines, W_LANES:] = block[:, :C]
            wproj_out[lines, :] = block[:, C:]
    for p in range(B_PARTS):
        width = min(B_LANES, TABLE - p * B_LANES)
        block = parts_ref[p, :, W_LANES:].astype(f32)[:, :width]
        for h in range(HEADS):
            for lz in range(2):
                t = lz * HEADS + h
                bias_out[h, lz : lz + 1, p * B_LANES : p * B_LANES + width] = block[t : t + 1]


def unpack(parts):
    vmem = pl.BlockSpec(memory_space=pltpu.VMEM)
    return pl.pallas_call(
        unpack_kernel,
        out_shape=(
            jax.ShapeDtypeStruct((1, C), f32),
            jax.ShapeDtypeStruct((C, 3 * C), f32),
            jax.ShapeDtypeStruct((C, C), f32),
            jax.ShapeDtypeStruct((HEADS, 2, TABLE), f32),
        ),
        in_specs=[vmem],
        out_specs=(vmem,) * 4,
        compiler_params=pltpu.CompilerParams(vmem_limit_bytes=VMEM_LIMIT),
        name="unpack",
    )(parts)


def summed(send, ready):
    others = PARTS // LATS
    got = lax.all_to_all(send, GROUP, 0, 0, tiled=True)
    got = got.reshape((others, LATS, 16, SEND_LANES)).astype(f32)
    weights = jnp.sum(got[..., :W_LANES], axis=(0, 1))
    bias = jnp.sum(got[..., W_LANES:], axis=0)
    mixed = jnp.concatenate([weights] + [bias[n] for n in range(LATS)], axis=1).astype(bf16)
    mixed, ready = lax.optimization_barrier((mixed, ready))
    count = lax.axis_size(REST)
    got = lax.all_to_all(
        jnp.broadcast_to(mixed[None], (count,) + mixed.shape), REST, 0, 0, tiled=True
    )
    total = jnp.sum(got.astype(f32), axis=0).astype(bf16)
    weights = total[:, :W_LANES]
    rows = [
        jnp.concatenate([weights, total[:, W_LANES + n * B_LANES : W_LANES + (n + 1) * B_LANES]], 1)
        for n in range(LATS)
    ]
    spread = jnp.broadcast_to(jnp.stack(rows)[None], (others, LATS, 16, SEND_LANES))
    return lax.all_to_all(spread.reshape(send.shape), GROUP, 0, 0, tiled=True), ready


def on_device(x, g, ln_gain, w_qkv, w_proj, bias_table):
    lon_axes, lat_axes = ("z", "y", "xh"), ("xl", "c")
    both = lon_axes + lat_axes
    lons, lats = lax.axis_size(lon_axes), lax.axis_size(lat_axes)
    lon_swap = [(i, i ^ 1) for i in range(lons)]
    lat_down = [(i, (i - 1) % lats) for i in range(lats)]
    lat_up = [(i, (i + 1) % lats) for i in range(lats)]
    corner_down = [(i * lats + a, (i ^ 1) * lats + b) for i in range(lons) for a, b in lat_down]
    corner_up = [(i * lats + a, (i ^ 1) * lats + b) for i in range(lons) for a, b in lat_up]

    x, g = x.transpose(1, 2, 0, 3), g.transpose(1, 2, 0, 3)
    corner_in = lax.ppermute(jnp.stack([x[:3, :6], g[:3, :6]]), both, corner_down)
    lon_in = lax.ppermute(jnp.stack([x[3:, :6], g[3:, :6]]), lon_axes, lon_swap)
    lat_in = lax.ppermute(jnp.stack([x[:3, 6:], g[:3, 6:]]), lat_axes, lat_down)
    bias, bias_left, w3, w3t, wproj_t, own = prepare(
        bias_table[0].transpose(1, 0, 2), w_qkv, w_proj, x, g
    )
    gain = ln_gain.reshape(1, C)
    own, to_lat, to_lon, to_corner, send = main(
        own, lat_in, lon_in, corner_in, gain, w3, w3t, w_proj, wproj_t, bias, bias_left
    )
    back_corner = lax.ppermute(to_corner, both, corner_up)
    back_lon = lax.ppermute(to_lon, lon_axes, lon_swap)
    back_lat = lax.ppermute(to_lat, lat_axes, lat_up)
    parts, (back_lat, back_lon, back_corner) = summed(send, (back_lat, back_lon, back_corner))
    grad_gain, grad_wqkv, grad_wproj, grad_bias = unpack(parts)
    grad_x = norm_grads(x, g, gain, own, back_lat, back_lon, back_corner)
    grad_x = grad_x.transpose(2, 0, 1, 3)
    grad_bias = grad_bias.transpose(1, 0, 2)[None]
    return grad_x, grad_gain.reshape(C), grad_wqkv, grad_wproj, grad_bias


def solution(mesh):
    shape = (mesh.shape["lon"] // 8, 4, 2, 2, 2)
    split = Mesh(mesh.devices.reshape(shape), ("z", "y", "xh", "xl", "c"))
    tokens = P(None, ("xl", "c"), ("z", "y", "xh"), None)
    table = P(("xl", "c"), None, None, None)
    return jax.shard_map(
        on_device,
        mesh=split,
        in_specs=(tokens, tokens, P(), P(), P(), table),
        out_specs=(tokens, P(), P(), P(), table),
        check_vma=False,
    )
```

time: 93.8 us -> 87.5 us (0.933)
  Pallas kernels: 26.1 us -> 19.2 us
    pallas_call x2, Pallas kernels: 22.7 us -> 16.4 us  [the longest x1 13.8 us: main(): pl.pallas_call(main_kernel, out_shape=(jax.ShapeDtypeStruct((3, BODY, C),...]
    unnamed x15 -> x16, local copies, waits for them, and re-layouts: 3.27 us -> 1.19 us
    another operation x2, local copies, waits for them, and re-layouts: 0.14 us -> 2.03 us  [the longest x1 1.09 us: on_device(): lat_in = lax.ppermute(jnp.stack([x[:3, 6:], g[:3, 6:]]), lat_axes, lat_down)]
    all_to_all x1, waiting for transfers between devices: 8.12 us -> 9.69 us  [summed(): lax.all_to_all(spread.reshape(send.shape), GROUP, 0, 0, tiled=True)]
  transfers between devices with their start and end apart: 8 -> 8, of which waited for: 4 -> 3; matrix products, arithmetic and copies ran while one was open for 2% -> 2% of each run, Pallas kernels for 5% -> 5%
where the time goes in v3:
time: 87.5 us; the launch traced here: 87.1 us
  starting transfers between devices  21.6 us (25%)
  waiting for transfers between devices  20.9 us (24%)
  blocking collectives  19.7 us (23%)
  Pallas kernels  19.2 us (22%)
  local copies, waits for them, and re-layouts  4.11 us (5%)
    all_to_all x1, blocking collectives, summed(): lax.all_to_all(jnp.broadcast_to(mixed[None], (count,) + mixed.shape), RES...  19.7 us
    pallas_call x1, Pallas kernels, main(): pl.pallas_call(main_kernel, out_shape=(jax.ShapeDtypeStruct((3, BODY, C),...  13.8 us
    all_to_all x1, waiting for transfers between devices, summed(): lax.all_to_all(spread.reshape(send.shape), GROUP, 0, 0, tiled=True)  9.69 us
    all_to_all x1, waiting for transfers between devices, summed(): got = lax.all_to_all(send, GROUP, 0, 0, tiled=True)  7.43 us
    all_to_all x1, starting transfers between devices, summed(): got = lax.all_to_all(send, GROUP, 0, 0, tiled=True)  5.46 us
    all_to_all x1, starting transfers between devices, summed(): lax.all_to_all(spread.reshape(send.shape), GROUP, 0, 0, tiled=True)  4.66 us
    ppermute x1, waiting for transfers between devices, on_device(): lat_in = lax.ppermute(jnp.stack([x[:3, 6:], g[:3, 6:]]), lat_axes, lat_down)  3.79 us
    ppermute x1, starting transfers between devices, on_device(): lon_in = lax.ppermute(jnp.stack([x[3:, :6], g[3:, :6]]), lon_axes, lon_swap)  3.66 us
  transfers between devices with their start and end apart: 8, of which 3 were waited for; matrix products, arithmetic and copies ran while one was open for 2% of the time, Pallas kernels for 5%

profile of v3, /device:TPU:1, one launch (start us, length us, event | category | flops | bytes accessed | tf_op | source)
XLA Modules:
  0.0 87.1 jit_solution(645099369495581686)
XLA Ops:
  0.6 0.0 copy-start
  0.6 0.9 %slice_bitcast_fusion.2 = (bf16[1,3,6,4,192]{4,3,2,1,0:T(4,128)(2,1)S(1)}, bf16[1,3,6,4,192]{4,3,2,1,0:T(4,128)(2,1)S(1)}, bf16[1,3,6,4,192]{4,3,2,1,0:T(4,128)(2,1)S(1)}, bf16[1,3,6,4,192]{4,3,2,1,0:T(4,128)(2,1)S(1)}) fusion(bf16[6,36,4,192]{3,2,1,0:T(4,128)(2,1)} %bitcast.55, bf16[6,36,4,192]{3,2,1,0:T(4,128)(2,1)} %bitcast.51), kind=kLoop, calls=%fused_computation.8 | loop fusion | bytes 221184 | tf_op jit(solution)/shard_map/stack | solution.py:531
  1.6 0.1 pad_maximum_fusion.1
  1.6 3.7 %collective-permute-start.1 = (bf16[2,3,6,4,192]{4,3,2,1,0:T(4,128)(2,1)S(1)}, bf16[2,3,6,4,192]{4,3,2,1,0:T(4,128)(2,1)S(1)}, u32[]{:S(2)}, u32[]{:S(2)}) collective-permute-start(bf16[2,3,6,4,192]{4,3,2,1,0:T(4,128)(2,1)S(1)} %pad_maximum_fusion.1), channel_id=1, source_target_pairs={{0,4},{4,0},{8,12},{12,8},{16,20},{20,16},{24,28},{28,24},{32,36},... | collective-permute-start | bytes 165896 | tf_op jit(solution)/shard_map/ppermute | solution.py:532
  5.3 0.1 pad_maximum_fusion.2
  5.4 2.9 %collective-permute-start.2 = (bf16[2,3,6,4,192]{4,3,2,1,0:T(4,128)(2,1)S(1)}, bf16[2,3,6,4,192]{4,3,2,1,0:T(4,128)(2,1)S(1)}, u32[]{:S(2)}, u32[]{:S(2)}) collective-permute-start(bf16[2,3,6,4,192]{4,3,2,1,0:T(4,128)(2,1)S(1)} %pad_maximum_fusion.2), channel_id=1, source_target_pairs={{0,7},{1,4},{2,5},{3,6},{4,3},{5,0},{6,1},{7,2},{8,15},{9,12},{10,... | collective-permute-start | bytes 165896 | tf_op jit(solution)/shard_map/ppermute | solution.py:531
  8.2 0.0 copy-done
  8.2 0.0 copy-start.4
  8.2 0.0 copy-start.5
  8.2 1.1 %slice_bitcast_fusion = (bf16[1,3,30,4,192]{4,3,2,1,0:T(4,128)(2,1)S(1)}, bf16[1,3,30,4,192]{4,3,2,1,0:T(4,128)(2,1)S(1)}) fusion(bf16[6,36,4,192]{3,2,1,0:T(4,128)(2,1)} %bitcast.56, bf16[6,36,4,192]{3,2,1,0:T(4,128)(2,1)S(1)} %bitcast.52), kind=kLoop, calls=%fused_computation.3 | loop fusion | bytes 552960 | tf_op jit(solution)/shard_map/stack | solution.py:533
  9.3 0.0 copy-start.1
  9.4 0.0 copy-start.3
  9.4 0.3 pad_maximum_fusion
  9.7 0.3 collective-permute-start
  9.9 0.0 copy-done.4
  10.0 0.0 copy-done.5
  10.0 0.4 copy-done.1
  10.4 0.1 copy-done.3
  10.4 2.6 %prepare.1 = (f32[12,144,128]{2,1,0:T(8,128)S(1)}, f32[2,144,128]{2,1,0:T(8,128)S(1)}, bf16[3,192,192]{2,1,0:T(8,128)(2,1)S(1)}, bf16[576,192]{1,0:T(8,128)(2,1)...) custom-call(f32[6,2,3312]{2,1,0:T(2,128)S(1)} %bitcast.61, bf16[192,576]{1,0:T(8,128)(2,1)S(1)} %copy-done.3, ...), custom_call_target="tpu_custom_call" | custom-call | flops 4000000000 | bytes 4000000 | tf_op jit(solution)/shard_map/prepare/pallas_call | solution.py:159
  13.1 0.0 collective-permute-done.1.lon_ref
  13.1 0.0 collective-permute-done.2.corner_ref
  13.1 3.8 %collective-permute-done.lat_ref = bf16[2,3,30,4,192]{4,3,2,1,0:T(4,128)(2,1)S(1)} collective-permute-done((bf16[2,3,30,4,192]{4,3,2,1,0:T(4,128)(2,1)S(1)}, bf16[2,3,30,4,192]{4,3,2,1,0:T(4,128)(2,1)S(1)}, u32[]{:S(2)}, u32[]{:S(2)}) %collective-permute-start) | collective-permute-done | bytes 276512 | tf_op jit(solution)/shard_map/ppermute | solution.py:533
  16.9 0.0 copy-start.2
  16.9 0.7 copy-done.2
  17.5 13.8 %window_grads.1 = (bf16[3,120,192]{2,1,0:T(8,128)(2,1)S(1)}, bf16[3,120,192]{2,1,0:T(8,128)(2,1)S(1)}, bf16[3,24,192]{2,1,0:T(8,128)(2,1)S(1)}, bf16[3,24,192]{2,1,0:T(8,128)(2,1)S(1)}, bf16[32,16,512]{2,1,0:T(8,128)(2,1)}) custom-call(bf16[2,3,120,192]{3,2,1,0:T(8,128)(2,1)S(1)} %get-tuple-element.24.own_ref, ...), custom_call_target="tpu_custom_call" | custom-call | flops 20000000000 | bytes 4000000 | tf_op jit(solution)/shard_map/window_grads/pallas_call | solution.py:383
  31.4 5.5 %all-to-all-start = ((bf16[32,16,512]{2,1,0:T(8,128)(2,1)}), bf16[32,16,512]{2,1,0:T(8,128)(2,1)S(1)}, u32[]{:S(2)}, u32[]{:S(2)}) async-start(bf16[32,16,512]{2,1,0:T(8,128)(2,1)} %get-tuple-element.31), calls=%async_computation | async-start | bytes 1048576 | tf_op jit(solution)/shard_map/all_to_all | solution.py:500
  36.8 3.0 %collective-permute-start.4 = (bf16[3,24,192]{2,1,0:T(8,128)(2,1)S(1)}, bf16[3,24,192]{2,1,0:T(8,128)(2,1)S(1)}, u32[]{:S(2)}, u32[]{:S(2)}) collective-permute-start(bf16[3,24,192]{2,1,0:T(8,128)(2,1)S(1)} %get-tuple-element.33), channel_id=1, source_target_pairs={{0,4},{4,0},{8,12},{12,8},{16,20},{20,16},{24,28},{28,24},{32,36},... | collective-permute-start | bytes 82952 | tf_op jit(solution)/shard_map/ppermute | solution.py:542
  39.8 1.4 %collective-permute-start.5 = (bf16[3,24,192]{2,1,0:T(8,128)(2,1)S(1)}, bf16[3,24,192]{2,1,0:T(8,128)(2,1)S(1)}, u32[]{:S(2)}, u32[]{:S(2)}) collective-permute-start(bf16[3,24,192]{2,1,0:T(8,128)(2,1)S(1)} %get-tuple-element.34), channel_id=1, source_target_pairs={{0,5},{1,6},{2,7},{3,4},{4,1},{5,2},{6,3},{7,0},{8,13},{9,14},{10,... | collective-permute-start | bytes 82952 | tf_op jit(solution)/shard_map/ppermute | solution.py:541
  41.2 0.3 collective-permute-start.3
  41.5 7.4 %all-to-all-done = bf16[32,16,512]{2,1,0:T(8,128)(2,1)S(1)} async-done(((bf16[32,16,512]{2,1,0:T(8,128)(2,1)}), bf16[32,16,512]{2,1,0:T(8,128)(2,1)S(1)}, u32[]{:S(2)}, u32[]{:S(2)}) %all-to-all-start) | async-done | bytes 524320 | tf_op jit(solution)/shard_map/all_to_all | solution.py:500
  49.0 0.1 bitcast_convert_fusion
  49.1 0.1 slice_reduce_fusion
  49.3 0.0 collective-permute-done.4.lon_ref
  49.3 0.0 collective-permute-done.5.corner_ref
  49.3 0.0 collective-permute-done.3.lat_ref
  49.3 19.7 %all_to_all.15 = bf16[8,16,896]{2,1,0:T(8,128)(2,1)S(1)} all-to-all(bf16[8,16,896]{2,1,0:T(8,128)(2,1)S(1)} %broadcast_in_dim.6), channel_id=1, replica_groups=mesh['z'=8,'y'=4,'xh'=2,'xl'=2,'c'=2] {'z'}, dimensions={0} | all-to-all | bytes 458752 | tf_op jit(solution)/shard_map/all_to_all | solution.py:507
  69.1 0.9 broadcast_in_dim.7
  70.0 4.7 %all-to-all-start.2 = ((bf16[32,16,512]{2,1,0:T(8,128)(2,1)}), bf16[32,16,512]{2,1,0:T(8,128)(2,1)S(1)}, u32[]{:S(2)}, u32[]{:S(2)}) async-start(bf16[32,16,512]{2,1,0:T(8,128)(2,1)} %bitcast.22), calls=%async_computation.2 | async-start | bytes 1048576 | tf_op jit(solution)/shard_map/all_to_all | solution.py:517
  74.6 1.9 %norm_grads.1 = bf16[6,36,4,192]{3,2,1,0:T(4,128)(2,1)} custom-call(bf16[6,36,4,192]{3,2,1,0:T(4,128)(2,1)S(1)} %bitcast.54, bf16[6,36,4,192]{3,2,1,0:T(4,128)(2,1)S(1)} %bitcast.58, f32[1,192]{1,0:T(1,128)S(1)} %bitcast.60, bf16[3,120,192]{2,1,0:T(8,128)(2,1)S(1)} %get-tuple-element.30.own_ref, bf16[3,120,192]{2,1,0:T(8,128)(2,1)S(1)} %collective-permute-done.3.lat_ref, ...), custom_call_target="tpu_custom_call" | custom-call | flops 10000000 | bytes 1500000 | tf_op jit(solution)/shard_map/norm_grads/pallas_call | solution.py:449
  76.5 9.7 %all-to-all-done.2.parts_ref = bf16[32,16,512]{2,1,0:T(8,128)(2,1)S(1)} async-done(((bf16[32,16,512]{2,1,0:T(8,128)(2,1)}), bf16[32,16,512]{2,1,0:T(8,128)(2,1)S(1)}, u32[]{:S(2)}, u32[]{:S(2)}) %all-to-all-start.2) | async-done | bytes 524320 | tf_op jit(solution)/shard_map/all_to_all | solution.py:517
  86.2 0.9 %unpack.1 = (f32[1,192]{1,0:T(1,128)}, f32[192,576]{1,0:T(8,128)}, f32[192,192]{1,0:T(8,128)}, f32[6,2,3312]{2,1,0:T(2,128)}) custom-call(bf16[32,16,512]{2,1,0:T(8,128)(2,1)S(1)} %all-to-all-done.2.parts_ref), custom_call_target="tpu_custom_call" | custom-call | tf_op jit(solution)/shard_map/unpack/pallas_call | solution.py:483
  (13 shorter events, 0.2 us)
Async XLA Ops:
  0.6 7.6 %copy-start = (bf16[4,6,36,192]{3,0,2,1:T(4,128)(2,1)S(1)}, bf16[4,6,36,192]{3,0,2,1:T(4,128)(2,1)}, u32[]{:S(2)}) copy-start(bf16[4,6,36,192]{3,0,2,1:T(4,128)(2,1)} %param.6) | copy-start | bytes 995332
  1.6 11.4 %collective-permute-start.1 = (bf16[2,3,6,4,192]{4,3,2,1,0:T(4,128)(2,1)S(1)}, bf16[2,3,6,4,192]{4,3,2,1,0:T(4,128)(2,1)S(1)}, u32[]{:S(2)}, u32[]{:S(2)}) collective-permute-start(bf16[2,3,6,4,192]{4,3,2,1,0:T(4,128)(2,1)S(1)} %pad_maximum_fusion.1), channel_id=1, source_target_pairs={{0,4},{4,0},{8,12},{12,8},{16,20},{20,16},{24,28},{28,24},{32,36},... | collective-permute-start | bytes 165896 | tf_op jit(solution)/shard_map/ppermute | solution.py:532
  5.4 7.7 %collective-permute-start.2 = (bf16[2,3,6,4,192]{4,3,2,1,0:T(4,128)(2,1)S(1)}, bf16[2,3,6,4,192]{4,3,2,1,0:T(4,128)(2,1)S(1)}, u32[]{:S(2)}, u32[]{:S(2)}) collective-permute-start(bf16[2,3,6,4,192]{4,3,2,1,0:T(4,128)(2,1)S(1)} %pad_maximum_fusion.2), channel_id=1, source_target_pairs={{0,7},{1,4},{2,5},{3,6},{4,3},{5,0},{6,1},{7,2},{8,15},{9,12},{10,... | collective-permute-start | bytes 165896 | tf_op jit(solution)/shard_map/ppermute | solution.py:531
  8.2 1.7 %copy-start.4 = (f32[1,2,6,3312]{3,1,2,0:T(2,128)S(1)}, f32[1,2,6,3312]{3,1,2,0:T(2,128)}, u32[]{:S(2)}) copy-start(f32[1,2,6,3312]{3,1,2,0:T(2,128)} %param.11) | copy-start | bytes 476932
  8.2 1.7 %copy-start.5 = (bf16[192,192]{1,0:T(8,128)(2,1)S(1)}, bf16[192,192]{1,0:T(8,128)(2,1)}, u32[]{:S(2)}) copy-start(bf16[192,192]{1,0:T(8,128)(2,1)} %wproj_ref.3) | copy-start | bytes 221188
  9.3 1.0 %copy-start.1 = (bf16[4,6,36,192]{3,0,2,1:T(4,128)(2,1)S(1)}, bf16[4,6,36,192]{3,0,2,1:T(4,128)(2,1)}, u32[]{:S(2)}) copy-start(bf16[4,6,36,192]{3,0,2,1:T(4,128)(2,1)} %param.7) | copy-start | bytes 995332
  9.4 1.1 %copy-start.3 = (bf16[192,576]{1,0:T(8,128)(2,1)S(1)}, bf16[192,576]{1,0:T(8,128)(2,1)}, u32[]{:S(2)}) copy-start(bf16[192,576]{1,0:T(8,128)(2,1)} %wqkv_ref.1) | copy-start | bytes 663556
  9.7 7.2 %collective-permute-start = (bf16[2,3,30,4,192]{4,3,2,1,0:T(4,128)(2,1)S(1)}, bf16[2,3,30,4,192]{4,3,2,1,0:T(4,128)(2,1)S(1)}, u32[]{:S(2)}, u32[]{:S(2)}) collective-permute-start(bf16[2,3,30,4,192]{4,3,2,1,0:T(4,128)(2,1)S(1)} %pad_maximum_fusion), channel_id=1, source_target_pairs={{0,3},{1,0},{2,1},{3,2},{4,7},{5,4},{6,5},{7,6},{8,11},{9,8},{10,9... | collective-permute-start | bytes 829448 | tf_op jit(solution)/shard_map/ppermute | solution.py:533
  16.9 0.7 copy-start.2
  31.4 17.6 %all-to-all-start = ((bf16[32,16,512]{2,1,0:T(8,128)(2,1)}), bf16[32,16,512]{2,1,0:T(8,128)(2,1)S(1)}, u32[]{:S(2)}, u32[]{:S(2)}) async-start(bf16[32,16,512]{2,1,0:T(8,128)(2,1)} %get-tuple-element.31), calls=%async_computation | async-start | bytes 1048576 | tf_op jit(solution)/shard_map/all_to_all | solution.py:500
  36.8 12.5 %collective-permute-start.4 = (bf16[3,24,192]{2,1,0:T(8,128)(2,1)S(1)}, bf16[3,24,192]{2,1,0:T(8,128)(2,1)S(1)}, u32[]{:S(2)}, u32[]{:S(2)}) collective-permute-start(bf16[3,24,192]{2,1,0:T(8,128)(2,1)S(1)} %get-tuple-element.33), channel_id=1, source_target_pairs={{0,4},{4,0},{8,12},{12,8},{16,20},{20,16},{24,28},{28,24},{32,36},... | collective-permute-start | bytes 82952 | tf_op jit(solution)/shard_map/ppermute | solution.py:542
  39.8 9.5 %collective-permute-start.5 = (bf16[3,24,192]{2,1,0:T(8,128)(2,1)S(1)}, bf16[3,24,192]{2,1,0:T(8,128)(2,1)S(1)}, u32[]{:S(2)}, u32[]{:S(2)}) collective-permute-start(bf16[3,24,192]{2,1,0:T(8,128)(2,1)S(1)} %get-tuple-element.34), channel_id=1, source_target_pairs={{0,5},{1,6},{2,7},{3,4},{4,1},{5,2},{6,3},{7,0},{8,13},{9,14},{10,... | collective-permute-start | bytes 82952 | tf_op jit(solution)/shard_map/ppermute | solution.py:541
  41.2 8.1 %collective-permute-start.3 = (bf16[3,120,192]{2,1,0:T(8,128)(2,1)S(1)}, bf16[3,120,192]{2,1,0:T(8,128)(2,1)S(1)}, u32[]{:S(2)}, u32[]{:S(2)}) collective-permute-start(bf16[3,120,192]{2,1,0:T(8,128)(2,1)S(1)} %get-tuple-element.32), channel_id=1, source_target_pairs={{0,1},{1,2},{2,3},{3,0},{4,5},{5,6},{6,7},{7,4},{8,9},{9,10},{10,1... | collective-permute-start | bytes 414728 | tf_op jit(solution)/shard_map/ppermute | solution.py:543
  70.0 16.2 %all-to-all-start.2 = ((bf16[32,16,512]{2,1,0:T(8,128)(2,1)}), bf16[32,16,512]{2,1,0:T(8,128)(2,1)S(1)}, u32[]{:S(2)}, u32[]{:S(2)}) async-start(bf16[32,16,512]{2,1,0:T(8,128)(2,1)} %bitcast.22), calls=%async_computation.2 | async-start | bytes 1048576 | tf_op jit(solution)/shard_map/all_to_all | solution.py:517

commit v4 on v3

--- a/solution.py
+++ b/solution.py
@@ -28,12 +28,14 @@
 GROUP = ("y", "xh", "xl", "c")
 REST = "z"
 PARTS = 32
-W_PARTS = 24
-W_LANES = 384
-B_PARTS = 26
-B_LANES = 128
-GAIN_PART = 24
-SEND_LANES = W_LANES + B_LANES
+SLOTS = 3
+W_TILES = 72
+W_SLOTS = 2
+B_COLUMNS = 26
+B_TILES = 20
+B_FIRST = 8
+GAIN_PART = B_FIRST + B_TILES
+WIDTH = 256
 LATS = 4
 WIDE = 3584
 f32 = jnp.float32
@@ -88,13 +90,15 @@
 
 
 def prepare_kernel(
-    table_ref, wqkv_ref, wproj_ref, x_ref, g_ref,
-    main_ref, left_ref, w3_ref, w3t_ref, wprojt_ref, own_ref, wide, pairs,
+    table_ref, wqkv_ref, wproj_ref, gain_ref, x_ref, g_ref,
+    main_ref, left_ref, w3_ref, w3t_ref, wprojt_ref, own_ref, match_ref, gain_out, wide, pairs,
 ):
+    gain_out[...] = gain_ref[...]
     for k in range(3):
         part = wqkv_ref[:, k * C : (k + 1) * C]
         w3_ref[k] = part
-        w3t_ref[k * C : (k + 1) * C] = part.T
+        w3t_ref[k * WIDTH : k * WIDTH + C] = part.T
+        w3t_ref[k * WIDTH + C : (k + 1) * WIDTH] = jnp.zeros((WIDTH - C, C), bf16)
     wprojt_ref[...] = wproj_ref[...].T
     for a in range(3):
         own_ref[0, a] = x_ref[a + 3, 6:36].reshape(BODY, C)
@@ -126,6 +130,7 @@
     low = (rest - middle.astype(f32)).astype(bf16)
     lane_head = iota((PAIRS, MAIN), 1) // LEFT
     for oj in range(WLON):
+        match_ref[oj] = offset_match(oj, True)
         match = offset_match(oj, False)
         dense = dot(high, match) + (dot(middle, match) + dot(low, match))
         for lz in range(2):
@@ -154,7 +159,7 @@
         left_ref[lz] = jnp.where(allowed, left_ref[lz], -1e30)
 
 
-def prepare(table, wqkv, wproj, x, g):
+def prepare(table, wqkv, wproj, gain, x, g):
     vmem = pl.BlockSpec(memory_space=pltpu.VMEM)
     return pl.pallas_call(
         prepare_kernel,
@@ -162,19 +167,21 @@
             jax.ShapeDtypeStruct((TYPES, WIN, MAIN), f32),
             jax.ShapeDtypeStruct((2, WIN, MAIN), f32),
             jax.ShapeDtypeStruct((3, C, C), bf16),
-            jax.ShapeDtypeStruct((3 * C, C), bf16),
+            jax.ShapeDtypeStruct((3 * WIDTH, C), bf16),
             jax.ShapeDtypeStruct((C, C), bf16),
             jax.ShapeDtypeStruct((2, 3, BODY, C), bf16),
-        ),
-        in_specs=[vmem] * 5,
-        out_specs=(vmem,) * 6,
+            jax.ShapeDtypeStruct((WLON, 2 * MAIN, PAIRS * 32), bf16),
+            jax.ShapeDtypeStruct((1, C), f32),
+        ),
+        in_specs=[vmem] * 6,
+        out_specs=(vmem,) * 8,
         scratch_shapes=[pltpu.VMEM((16, WIDE), f32), pltpu.VMEM((3, TYPES * 16, 128), f32)],
         compiler_params=pltpu.CompilerParams(vmem_limit_bytes=VMEM_LIMIT),
         cost_estimate=pl.CostEstimate(
             flops=4_000_000_000, bytes_accessed=4_000_000, transcendentals=0
         ),
         name="prepare",
-    )(table, wqkv, wproj, x, g)
+    )(table, wqkv, wproj, gain, x, g)
 
 
 def normalised(values):
@@ -184,12 +191,18 @@
     return centred * inverse, inverse
 
 
+def w_place(t):
+    if t < W_SLOTS * PARTS:
+        return t // W_SLOTS, t % W_SLOTS
+    return t - W_SLOTS * PARTS, W_SLOTS
+
+
 def main_kernel(
     own_ref, lat_ref, lon_ref, corner_ref, gain_ref, w3_ref, w3t_ref, wproj_ref, wprojt_ref,
-    bias_ref, left_ref, own_out, lat_out, lon_out, corner_out, send_out,
-    xw, gw, rows, standard_ref, cot_ref, query_ref, key_ref, value_ref, mixed_ref, tokens_t_ref,
+    bias_ref, left_ref, match_ref, rows_out, send_out,
+    xw, gw, standard_ref, cot_ref, query_ref, key_ref, value_ref, mixed_ref, tokens_t_ref,
     qkv_t_ref, mixed_t_ref, scores_ref, grad_attend_ref, half_ref, grad_half_ref, dense, dense_left,
-    wsum, psum, gsum, spread, wide, grads,
+    wsum, psum, gsum, spread, wide, grads, stack,
 ):
     order = window_order(False)
     for a in range(6):
@@ -204,9 +217,8 @@
                 to[w, 24 * a : 24 * a + 24, :] = line[24 * w : 24 * w + 24]
     dense[...] = jnp.zeros_like(dense)
     dense_left[...] = jnp.zeros_like(dense_left)
-    wsum[...] = jnp.zeros_like(wsum)
-    psum[...] = jnp.zeros_like(psum)
     gsum[...] = jnp.zeros_like(gsum)
+    spread[...] = jnp.zeros_like(spread)
     gain = gain_ref[...]
     lane_head = iota((WIN, C), 1) // HEAD_DIM
     shape = (WIN, MAIN)
@@ -240,7 +252,9 @@
     for w in range(WINDOWS):
         tokens_t = scaled[w * WIN : (w + 1) * WIN].T.astype(bf16)
         tokens_t_ref[w] = tokens_t
-        qkv_t_ref[w] = dot(w3t_ref[...], tokens_t).astype(bf16)
+        for k in range(3):
+            part = dot(w3t_ref[k * WIDTH : k * WIDTH + C], tokens_t)
+            qkv_t_ref[w, k * C : (k + 1) * C] = part.astype(bf16)
         mixed_t_ref[w] = dot(wproj_ref[...], gw[w].T.astype(bf16)).astype(bf16)
 
     for w in range(WINDOWS):
@@ -274,13 +288,13 @@
         span = slice(w * WIN, (w + 1) * WIN)
 
         def per_query(left, right_ref):
-            parts = [
-                dot(
-                    left[h * HEAD_DIM : (h + 1) * HEAD_DIM],
-                    right_ref[w, :, h * MAIN : (h + 1) * MAIN],
+            parts = []
+            for h in range(0, HEADS, 2):
+                two = dot(
+                    left[h * HEAD_DIM : (h + 2) * HEAD_DIM],
+                    right_ref[w, :, h * MAIN : (h + 2) * MAIN],
                 )
-                for h in range(HEADS)
-            ]
+                parts += [two[:HEAD_DIM, :MAIN], two[HEAD_DIM:, MAIN:]]
             shared = dot(left, right_ref[w, :, HEADS * MAIN :])
             return jnp.concatenate(parts, axis=0), jnp.where(own_head_t, shared, 0.0)
 
@@ -291,33 +305,25 @@
 
         cot = cot_ref[span]
         out_t, out_left = per_query(qkv_t_ref[w, 2 * C :], half_ref)
-        psum[...] += dot(out_t.astype(bf16), cot[:MAIN]) + dot(
-            out_left.astype(bf16), dot(repeat_t, cot).astype(bf16)
-        )
+        both = jnp.concatenate([out_t.astype(bf16), out_left.astype(bf16)], axis=1)
+        added = dot(both, jnp.concatenate([cot[:MAIN], dot(repeat_t, cot).astype(bf16)], axis=0))
+        psum[...] = added if w == 0 else psum[...] + added
         query_grad, query_left = per_query(qkv_t_ref[w, C : 2 * C], grad_half_ref)
         first = slice(w * WIN, w * WIN + MAIN)
         last = slice(w * WIN + MAIN, (w + 1) * WIN)
-        spread[first, 0:C] = (query_grad * SCALE).T
-        spread[last, 0:C] = dot(gather, (query_left * SCALE).T.astype(bf16))
-        spread[span, C : 2 * C] = per_key(grad_half_ref, query_ref[span]) * SCALE
-        spread[span, 2 * C :] = per_key(half_ref, mixed_ref[span])
-
-    grad_projected = spread[...].astype(bf16)
-    back = dot(grad_projected, w3t_ref[...]).astype(bf16).astype(f32)
-    rows[...] = back.reshape(WINDOWS, WIN, C)
-    gsum[0:1, :] = jnp.sum(back * standard_ref[...], axis=0, keepdims=True)
+        spread[first, 0:C] = (query_grad * SCALE).astype(bf16).T
+        spread[last, 0:C] = dot(gather, (query_left * SCALE).astype(bf16).T).astype(bf16)
+        grad_key = per_key(grad_half_ref, query_ref[span]) * SCALE
+        spread[span, WIDTH : WIDTH + C] = grad_key.astype(bf16)
+        spread[span, 2 * WIDTH : 2 * WIDTH + C] = per_key(half_ref, mixed_ref[span]).astype(bf16)
+
+    grad_projected = spread[...]
+    back = dot(grad_projected, w3t_ref[...]).astype(bf16)
+    rows_out[...] = back
+    gsum[0:1, :] = jnp.sum(back.astype(f32) * standard_ref[...], axis=0, keepdims=True)
     for w in range(WINDOWS):
-        wsum[...] += dot(tokens_t_ref[w], grad_projected[w * WIN : (w + 1) * WIN])
-
-    order_t = window_order(True)
-    for a in range(6):
-        line = jnp.concatenate([rows[w, 24 * a : 24 * a + 24, :] for w in range(WINDOWS)], axis=0)
-        line = dot(order_t, line.astype(bf16))
-        body, tail = line[:BODY].astype(bf16), line[BODY:].astype(bf16)
-        if a < 3:
-            own_out[a], lon_out[a] = body, tail
-        else:
-            lat_out[a - 3], corner_out[a - 3] = body, tail
+        added = dot(tokens_t_ref[w], spread[w * WIN : (w + 1) * WIN])
+        wsum[...] = added if w == 0 else wsum[...] + added
 
     total = jnp.zeros((TYPES * 16, PAIRS * 32), f32)
     lane_left = iota((PAIRS, MAIN), 1) // LEFT
@@ -332,7 +338,7 @@
         picked = jnp.concatenate(picked, axis=0)
         high = picked.astype(bf16)
         low = (picked - high.astype(f32)).astype(bf16)
-        match = offset_match(oj, True)
+        match = match_ref[oj]
         total += dot(high, match) + dot(low, match)
     for v in range(3):
         grads[v] = total[:, 128 * v : 128 * (v + 1)]
@@ -356,43 +362,42 @@
                 target = (slice(0, TYPES), slice(base, base + width))
                 wide[target] = jnp.where(inside, piece, wide[target])
 
-    halves = []
-    for n in range(2):
-        if n == 0:
-            halves.append(wsum[:, :W_LANES])
+    weights = jnp.concatenate(
+        [wsum[:, k * WIDTH : k * WIDTH + C] for k in range(3)] + [psum[...]], axis=1
+    )
+    for t in range(W_TILES):
+        row, column = divmod(t, 6)
+        tile = weights[16 * row : 16 * row + 16, 128 * column : 128 * column + 128]
+        p, slot = w_place(t)
+        send_out[p, :, 128 * slot : 128 * slot + 128] = tile.astype(bf16)
+    stack[...] = jnp.zeros_like(stack)
+    for n in range(B_COLUMNS):
+        stack[TYPES * n : TYPES * (n + 1), :] = wide[:TYPES, 128 * n : 128 * (n + 1)]
+    last = slice(128 * W_SLOTS, 128 * SLOTS)
+    for n in range(B_TILES):
+        send_out[B_FIRST + n, :, last] = stack[16 * n : 16 * n + 16, :].astype(bf16)
+    for p in range(GAIN_PART, PARTS):
+        if p == GAIN_PART:
+            line = gsum[0:1, :]
+            gains = jnp.concatenate([line[:, :128], jnp.zeros((7, 128), f32)], axis=0)
+            more = jnp.concatenate([line[:, 128:], jnp.zeros((1, 256 - C), f32)], axis=1)
+            more = jnp.concatenate([more, jnp.zeros((7, 128), f32)], axis=0)
+            send_out[p, :, last] = jnp.concatenate([gains, more], axis=0).astype(bf16)
         else:
-            halves.append(jnp.concatenate([wsum[:, W_LANES:], psum[...]], axis=1))
-    for p in range(PARTS):
-        if p < W_PARTS:
-            lines = slice(p // 2 * 16, p // 2 * 16 + 16)
-            send_out[p, :, :W_LANES] = halves[p % 2][lines].astype(bf16)
-        elif p == GAIN_PART:
-            gains = jnp.concatenate([gsum[...], jnp.zeros((8, C), f32)], axis=0)
-            gains = jnp.concatenate([gains, jnp.zeros((16, W_LANES - C), f32)], axis=1)
-            send_out[p, :, :W_LANES] = gains.astype(bf16)
-        else:
-            send_out[p, :, :W_LANES] = jnp.zeros((16, W_LANES), bf16)
-        if p < B_PARTS:
-            send_out[p, :, W_LANES:] = wide[:, p * B_LANES : (p + 1) * B_LANES].astype(bf16)
-        else:
-            send_out[p, :, W_LANES:] = jnp.zeros((16, B_LANES), bf16)
-
-
-def main(own, lat_in, lon_in, corner_in, gain, w3, w3t, wproj, wproj_t, bias, bias_left):
+            send_out[p, :, last] = jnp.zeros((16, 128), bf16)
+
+
+def main(own, lat_in, lon_in, corner_in, gain, w3, w3t, wproj, wproj_t, bias, bias_left, match):
     vmem = pl.BlockSpec(memory_space=pltpu.VMEM)
     return pl.pallas_call(
         main_kernel,
         out_shape=(
-            jax.ShapeDtypeStruct((3, BODY, C), bf16),
-            jax.ShapeDtypeStruct((3, BODY, C), bf16),
-            jax.ShapeDtypeStruct((3, TAIL, C), bf16),
-            jax.ShapeDtypeStruct((3, TAIL, C), bf16),
-            jax.ShapeDtypeStruct((PARTS, 16, SEND_LANES), bf16),
-        ),
-        in_specs=[vmem] * 11,
-        out_specs=(vmem,) * 5,
+            jax.ShapeDtypeStruct((WINDOWS * WIN, C), bf16),
+            jax.ShapeDtypeStruct((PARTS, 16, SLOTS * 128), bf16),
+        ),
+        in_specs=[vmem] * 12,
+        out_specs=(vmem,) * 2,
         scratch_shapes=[
-            pltpu.VMEM((WINDOWS, WIN, C), f32),
             pltpu.VMEM((WINDOWS, WIN, C), f32),
             pltpu.VMEM((WINDOWS, WIN, C), f32),
             pltpu.VMEM((WINDOWS * WIN, C), f32),
@@ -410,29 +415,59 @@
             pltpu.VMEM((WINDOWS, WIN, (HEADS + 1) * MAIN), bf16),
             pltpu.VMEM((TYPES, WIN, MAIN), f32),
             pltpu.VMEM((2, WIN, MAIN), f32),
-            pltpu.VMEM((C, 3 * C), f32),
+            pltpu.VMEM((C, 3 * WIDTH), f32),
             pltpu.VMEM((C, C), f32),
             pltpu.VMEM((8, C), f32),
-            pltpu.VMEM((WINDOWS * WIN, 3 * C), f32),
+            pltpu.VMEM((WINDOWS * WIN, 3 * WIDTH), bf16),
             pltpu.VMEM((16, WIDE), f32),
             pltpu.VMEM((3, TYPES * 16, 128), f32),
+            pltpu.VMEM((B_TILES * 16, 128), f32),
         ],
         compiler_params=pltpu.CompilerParams(vmem_limit_bytes=VMEM_LIMIT),
         cost_estimate=pl.CostEstimate(
             flops=20_000_000_000, bytes_accessed=4_000_000, transcendentals=750_000
         ),
         name="window_grads",
-    )(own, lat_in, lon_in, corner_in, gain, w3, w3t, wproj, wproj_t, bias, bias_left)
-
-
-def norm_kernel(x_ref, g_ref, gain_ref, own_ref, lat_ref, lon_ref, corner_ref, out_ref):
+    )(own, lat_in, lon_in, corner_in, gain, w3, w3t, wproj, wproj_t, bias, bias_left, match)
+
+
+def pieces_kernel(rows_ref, body_out, tail_out):
+    order_t = window_order(True)
+    for a in range(6):
+        line = jnp.concatenate(
+            [rows_ref[WIN * w + 24 * a : WIN * w + 24 * a + 24, :] for w in range(WINDOWS)], axis=0
+        )
+        line = dot(order_t, line)
+        body_out[a] = line[:BODY].astype(bf16)
+        tail_out[a] = line[BODY:].astype(bf16)
+
+
+def pieces(rows):
+    vmem = pl.BlockSpec(memory_space=pltpu.VMEM)
+    return pl.pallas_call(
+        pieces_kernel,
+        out_shape=(
+            jax.ShapeDtypeStruct((6, BODY, C), bf16),
+            jax.ShapeDtypeStruct((6, TAIL, C), bf16),
+        ),
+        in_specs=[vmem],
+        out_specs=(vmem,) * 2,
+        compiler_params=pltpu.CompilerParams(vmem_limit_bytes=VMEM_LIMIT),
+        cost_estimate=pl.CostEstimate(
+            flops=500_000_000, bytes_accessed=700_000, transcendentals=0
+        ),
+        name="pieces",
+    )(rows)
+
+
+def norm_kernel(x_ref, g_ref, gain_ref, body_ref, tail_ref, lat_ref, out_ref):
     gain = gain_ref[...]
     for a in range(6):
         if a < 3:
-            head, body = corner_ref[a], lat_ref[a]
+            grad = lat_ref[a].astype(f32)
         else:
-            head, body = lon_ref[a - 3], own_ref[a - 3]
-        grad = jnp.concatenate([head.astype(f32), body.astype(f32)], axis=0)
+            grad = [tail_ref[a - 3].astype(f32), body_ref[a - 3].astype(f32)]
+            grad = jnp.concatenate(grad, axis=0)
         standard, inverse = normalised(x_ref[a].reshape(WIN, C).astype(f32))
         scaled = grad * gain
         local = inverse * (
@@ -444,38 +479,46 @@
         out_ref[a] = total.reshape(36, 4, C)
 
 
-def norm_grads(x, g, gain, own, lat_in, lon_in, corner_in):
+def norm_grads(x, g, gain, body, tail, lat_in):
     vmem = pl.BlockSpec(memory_space=pltpu.VMEM)
     return pl.pallas_call(
         norm_kernel,
         out_shape=jax.ShapeDtypeStruct(x.shape, bf16),
-        in_specs=[vmem] * 7,
+        in_specs=[vmem] * 6,
         out_specs=vmem,
         compiler_params=pltpu.CompilerParams(vmem_limit_bytes=VMEM_LIMIT),
         cost_estimate=pl.CostEstimate(
             flops=10_000_000, bytes_accessed=1_500_000, transcendentals=1000
         ),
         name="norm_grads",
-    )(x, g, gain, own, lat_in, lon_in, corner_in)
-
-
-def unpack_kernel(parts_ref, gain_out, wqkv_out, wproj_out, bias_out):
-    gain_out[...] = parts_ref[GAIN_PART, :, :C].astype(f32)[:1]
-    for p in range(W_PARTS):
-        lines = slice(p // 2 * 16, p // 2 * 16 + 16)
-        block = parts_ref[p, :, :W_LANES].astype(f32)
-        if p % 2 == 0:
-            wqkv_out[lines, :W_LANES] = block
-        else:
-            wqkv_out[lines, W_LANES:] = block[:, :C]
-            wproj_out[lines, :] = block[:, C:]
-    for p in range(B_PARTS):
-        width = min(B_LANES, TABLE - p * B_LANES)
-        block = parts_ref[p, :, W_LANES:].astype(f32)[:, :width]
+    )(x, g, gain, body, tail, lat_in)
+
+
+def unpack_kernel(parts_ref, gain_out, wqkv_out, wproj_out, bias_out, stack):
+    last = slice(128 * W_SLOTS, 128 * SLOTS)
+    gains = parts_ref[GAIN_PART, :, last].astype(f32)
+    gain_out[:, :128] = gains[0:1]
+    gain_out[:, 128:] = gains[8:9, : C - 128]
+
+    def tile(t):
+        p, slot = w_place(t)
+        return parts_ref[p, :, 128 * slot : 128 * slot + 128].astype(f32)
+
+    for row in range(C // 16):
+        lines = slice(16 * row, 16 * row + 16)
+        for column in range(4):
+            wqkv_out[lines, 128 * column : 128 * column + 128] = tile(6 * row + column)
+        mixed = tile(6 * row + 4)
+        wqkv_out[lines, 512:] = mixed[:, :64]
+        wproj_out[lines, :] = jnp.concatenate([mixed[:, 64:], tile(6 * row + 5)], axis=1)
+    for n in range(B_TILES):
+        stack[16 * n : 16 * n + 16, :] = parts_ref[B_FIRST + n, :, last].astype(f32)
+    for n in range(B_COLUMNS):
+        width = min(128, TABLE - 128 * n)
         for h in range(HEADS):
             for lz in range(2):
-                t = lz * HEADS + h
-                bias_out[h, lz : lz + 1, p * B_LANES : p * B_LANES + width] = block[t : t + 1]
+                t = TYPES * n + lz * HEADS + h
+                bias_out[h, lz : lz + 1, 128 * n : 128 * n + width] = stack[t : t + 1, :width]
 
 
 def unpack(parts):
@@ -490,31 +533,71 @@
         ),
         in_specs=[vmem],
         out_specs=(vmem,) * 4,
+        scratch_shapes=[pltpu.VMEM((B_TILES * 16, 128), f32)],
         compiler_params=pltpu.CompilerParams(vmem_limit_bytes=VMEM_LIMIT),
         name="unpack",
     )(parts)
 
 
-def summed(send, ready):
-    others = PARTS // LATS
+def scattered(send):
     got = lax.all_to_all(send, GROUP, 0, 0, tiled=True)
-    got = got.reshape((others, LATS, 16, SEND_LANES)).astype(f32)
-    weights = jnp.sum(got[..., :W_LANES], axis=(0, 1))
-    bias = jnp.sum(got[..., W_LANES:], axis=0)
-    mixed = jnp.concatenate([weights] + [bias[n] for n in range(LATS)], axis=1).astype(bf16)
-    mixed, ready = lax.optimization_barrier((mixed, ready))
+    got = got.reshape((PARTS // LATS, LATS, 16, SLOTS * 128)).astype(f32)
+    shared = jnp.sum(got[..., : 128 * W_SLOTS], axis=(0, 1))
+    last = jnp.sum(got[..., 128 * W_SLOTS :], axis=0)
+    return jnp.concatenate([shared] + [last[n] for n in range(LATS)], axis=1).astype(bf16)
+
+
+def exchanged(mixed):
     count = lax.axis_size(REST)
     got = lax.all_to_all(
         jnp.broadcast_to(mixed[None], (count,) + mixed.shape), REST, 0, 0, tiled=True
     )
-    total = jnp.sum(got.astype(f32), axis=0).astype(bf16)
-    weights = total[:, :W_LANES]
+    total = jnp.sum(got.astype(f32), axis=0)
+    shared = total[:, : 128 * W_SLOTS]
+    last = [total[:, 128 * (W_SLOTS + n) : 128 * (W_SLOTS + n + 1)] for n in range(LATS)]
+    everywhere = last[0] + last[1] + last[2] + last[3]
+    part = lax.axis_index(GROUP)
+    per_lat = (part >= B_FIRST) & (part < GAIN_PART)
     rows = [
-        jnp.concatenate([weights, total[:, W_LANES + n * B_LANES : W_LANES + (n + 1) * B_LANES]], 1)
+        jnp.concatenate([shared, jnp.where(per_lat, last[n], everywhere)], axis=1).astype(bf16)
         for n in range(LATS)
     ]
-    spread = jnp.broadcast_to(jnp.stack(rows)[None], (others, LATS, 16, SEND_LANES))
-    return lax.all_to_all(spread.reshape(send.shape), GROUP, 0, 0, tiled=True), ready
+    spread = jnp.broadcast_to(jnp.stack(rows)[None], (PARTS // LATS, LATS, 16, SLOTS * 128))
+    return spread.reshape(PARTS, 16, SLOTS * 128)
+
+
+def pack_kernel(x_ref, g_ref, corner_out, lon_out, lat_out, sems):
+    copies = []
+    for k, ref in enumerate((x_ref, g_ref)):
+        for n, (source, to) in enumerate(
+            (
+                (ref.at[pl.ds(0, 3), pl.ds(0, 6)], corner_out),
+                (ref.at[pl.ds(3, 3), pl.ds(0, 6)], lon_out),
+                (ref.at[pl.ds(0, 3), pl.ds(6, 30)], lat_out),
+            )
+        ):
+            copies.append(pltpu.make_async_copy(source, to.at[k], sems.at[3 * k + n]))
+    for copy in copies:
+        copy.start()
+    for copy in copies:
+        copy.wait()
+
+
+def pack(x, g):
+    vmem = pl.BlockSpec(memory_space=pltpu.VMEM)
+    return pl.pallas_call(
+        pack_kernel,
+        out_shape=(
+            jax.ShapeDtypeStruct((2, 3, 6, 4, C), bf16),
+            jax.ShapeDtypeStruct((2, 3, 6, 4, C), bf16),
+            jax.ShapeDtypeStruct((2, 3, 30, 4, C), bf16),
+        ),
+        in_specs=[pl.BlockSpec(memory_space=pltpu.HBM)] * 2,
+        out_specs=(vmem,) * 3,
+        scratch_shapes=[pltpu.SemaphoreType.DMA((6,))],
+        compiler_params=pltpu.CompilerParams(vmem_limit_bytes=VMEM_LIMIT),
+        name="pack",
+    )(x, g)
 
 
 def on_device(x, g, ln_gain, w_qkv, w_proj, bias_table):
@@ -525,25 +608,26 @@
     lat_down = [(i, (i - 1) % lats) for i in range(lats)]
     lat_up = [(i, (i + 1) % lats) for i in range(lats)]
     corner_down = [(i * lats + a, (i ^ 1) * lats + b) for i in range(lons) for a, b in lat_down]
-    corner_up = [(i * lats + a, (i ^ 1) * lats + b) for i in range(lons) for a, b in lat_up]
 
     x, g = x.transpose(1, 2, 0, 3), g.transpose(1, 2, 0, 3)
-    corner_in = lax.ppermute(jnp.stack([x[:3, :6], g[:3, :6]]), both, corner_down)
-    lon_in = lax.ppermute(jnp.stack([x[3:, :6], g[3:, :6]]), lon_axes, lon_swap)
-    lat_in = lax.ppermute(jnp.stack([x[:3, 6:], g[:3, 6:]]), lat_axes, lat_down)
-    bias, bias_left, w3, w3t, wproj_t, own = prepare(
-        bias_table[0].transpose(1, 0, 2), w_qkv, w_proj, x, g
+    to_corner, to_lon, to_lat = pack(x, g)
+    corner_in = lax.ppermute(to_corner, both, corner_down)
+    lon_in = lax.ppermute(to_lon, lon_axes, lon_swap)
+    lat_in = lax.ppermute(to_lat, lat_axes, lat_down)
+    bias, bias_left, w3, w3t, wproj_t, own, match, gain = prepare(
+        bias_table[0].transpose(1, 0, 2), w_qkv, w_proj, ln_gain.reshape(1, C), x, g
     )
-    gain = ln_gain.reshape(1, C)
-    own, to_lat, to_lon, to_corner, send = main(
-        own, lat_in, lon_in, corner_in, gain, w3, w3t, w_proj, wproj_t, bias, bias_left
+    rows, send = main(
+        own, lat_in, lon_in, corner_in, gain, w3, w3t, w_proj, wproj_t, bias, bias_left, match
     )
-    back_corner = lax.ppermute(to_corner, both, corner_up)
-    back_lon = lax.ppermute(to_lon, lon_axes, lon_swap)
-    back_lat = lax.ppermute(to_lat, lat_axes, lat_up)
-    parts, (back_lat, back_lon, back_corner) = summed(send, (back_lat, back_lon, back_corner))
+    body, tail = pieces(rows)
+    tail = lax.ppermute(tail, lon_axes, lon_swap)
+    mixed, tail = lax.optimization_barrier((scattered(send), tail))
+    lat_rows = lax.ppermute(jnp.concatenate([tail[3:], body[3:]], axis=1), lat_axes, lat_up)
+    spread, lat_rows = lax.optimization_barrier((exchanged(mixed), lat_rows))
+    parts = lax.all_to_all(spread, GROUP, 0, 0, tiled=True)
     grad_gain, grad_wqkv, grad_wproj, grad_bias = unpack(parts)
-    grad_x = norm_grads(x, g, gain, own, back_lat, back_lon, back_corner)
+    grad_x = norm_grads(x, g, gain, body, tail, lat_rows)
     grad_x = grad_x.transpose(2, 0, 1, 3)
     grad_bias = grad_bias.transpose(1, 0, 2)[None]
     return grad_x, grad_gain.reshape(C), grad_wqkv, grad_wproj, grad_bias

time: 87.5 us -> 84.1 us (0.961)
  blocking collectives: 19.7 us -> 0 us
  starting transfers between devices: 21.6 us -> 30.5 us
  local copies, waits for them, and re-layouts: 4.11 us -> 9.03 us
  waiting for transfers between devices: 20.9 us -> 23.9 us
    all_to_all x1 -> x0, blocking collectives: 19.7 us -> none  [summed(): lax.all_to_all(jnp.broadcast_to(mixed[None], (count,) + mixed.shape), RES...]
    all_to_all x2 -> x3, starting transfers between devices: 10.1 us -> 20.1 us  [the longest x1 8.18 us: exchanged(): lax.all_to_all(jnp.broadcast_to(mixed[None], (count,) + mixed.shape), RES...]
    all_to_all x2 -> x3, waiting for transfers between devices: 17.1 us -> 23.9 us  [the longest x1 8.65 us: exchanged(): lax.all_to_all(jnp.broadcast_to(mixed[None], (count,) + mixed.shape), RES...]
    unnamed x16 -> x26, local copies, waits for them, and re-layouts: 1.19 us -> 7.52 us
    ppermute x6 -> x5, waiting for transfers between devices: 3.81 us -> 0.01 us  [the longest x1 0.01 us: on_device(): lon_in = lax.ppermute(to_lon, lon_axes, lon_swap)]
    another operation x3 -> x1, local copies, waits for them, and re-layouts: 2.03 us -> 0.01 us  [the longest x1 1.09 us: on_device(): lat_in = lax.ppermute(jnp.stack([x[:3, 6:], g[:3, 6:]]), lat_axes, lat_down)]
    ppermute x6 -> x5, starting transfers between devices: 11.5 us -> 10.4 us  [the longest x1 3.32 us: on_device(): lat_in = lax.ppermute(to_lat, lat_axes, lat_down)]
    pallas_call x1 -> x3, Pallas kernels: 13.8 us -> 13.1 us  [the longest x1 12.5 us: main(): pl.pallas_call(main_kernel, out_shape=(jax.ShapeDtypeStruct((WINDOWS * WI...]
  transfers between devices with their start and end apart: 8 -> 8, of which waited for: 3 -> 3; matrix products, arithmetic and copies ran while one was open for 2% -> 0% of each run, Pallas kernels for 5% -> 6%
where the time goes in v4:
time: 84.1 us; the launch traced here: 83.4 us
  starting transfers between devices  30.5 us (36%)
  waiting for transfers between devices  23.9 us (28%)
  Pallas kernels  18.9 us (22%)
  local copies, waits for them, and re-layouts  9.03 us (11%)
  between operations  0.85 us (1%)
    pallas_call x1, Pallas kernels, main(): pl.pallas_call(main_kernel, out_shape=(jax.ShapeDtypeStruct((WINDOWS * WI...  12.5 us
    all_to_all x1, waiting for transfers between devices, exchanged(): lax.all_to_all(jnp.broadcast_to(mixed[None], (count,) + mixed.shape), RES...  8.65 us
    all_to_all x1, waiting for transfers between devices, on_device(): parts = lax.all_to_all(spread, GROUP, 0, 0, tiled=True)  8.29 us
    all_to_all x1, starting transfers between devices, exchanged(): lax.all_to_all(jnp.broadcast_to(mixed[None], (count,) + mixed.shape), RES...  8.18 us
    unnamed x26, local copies, waits for them, and re-layouts  7.52 us
    all_to_all x1, waiting for transfers between devices, scattered(): got = lax.all_to_all(send, GROUP, 0, 0, tiled=True)  6.97 us
    all_to_all x1, starting transfers between devices, scattered(): got = lax.all_to_all(send, GROUP, 0, 0, tiled=True)  6 us
    all_to_all x1, starting transfers between devices, on_device(): parts = lax.all_to_all(spread, GROUP, 0, 0, tiled=True)  5.96 us
  transfers between devices with their start and end apart: 8, of which 3 were waited for; matrix products, arithmetic and copies ran while one was open for 0% of the time, Pallas kernels for 6%

profile of v4, /device:TPU:1, one launch (start us, length us, event | category | flops | bytes accessed | tf_op | source)
XLA Modules:
  0.0 83.4 jit_solution(6736920858619444595)
XLA Ops:
  0.6 0.0 copy-start
  0.6 1.0 %copy-done = bf16[4,6,36,192]{3,0,2,1:T(4,128)(2,1)S(1)} copy-done((bf16[4,6,36,192]{3,0,2,1:T(4,128)(2,1)S(1)}, bf16[4,6,36,192]{3,0,2,1:T(4,128)(2,1)}, u32[]{:S(2)}) %copy-start) | copy-done | bytes 331800
  1.6 0.0 copy-start.3
  1.6 1.0 %copy-done.3 = bf16[4,6,36,192]{3,0,2,1:T(4,128)(2,1)S(1)} copy-done((bf16[4,6,36,192]{3,0,2,1:T(4,128)(2,1)S(1)}, bf16[4,6,36,192]{3,0,2,1:T(4,128)(2,1)}, u32[]{:S(2)}) %copy-start.3) | copy-done | bytes 331800
  2.7 0.3 pack.1
  2.9 3.3 %collective-permute-start = (bf16[2,3,30,4,192]{4,3,2,1,0:T(4,128)(2,1)S(1)}, bf16[2,3,30,4,192]{4,3,2,1,0:T(4,128)(2,1)S(1)}, u32[]{:S(2)}, u32[]{:S(2)}) collective-permute-start(bf16[2,3,30,4,192]{4,3,2,1,0:T(4,128)(2,1)S(1)} %get-tuple-element.30), channel_id=1, source_target_pairs={{0,3},{1,0},{2,1},{3,2},{4,7},{5,4},{6,5},{7,6},{8,11},{9,8},{10,9... | collective-permute-start | bytes 829448 | tf_op jit(solution)/shard_map/ppermute | solution.py:616
  6.3 1.0 %collective-permute-start.1 = (bf16[2,3,6,4,192]{4,3,2,1,0:T(4,128)(2,1)S(1)}, bf16[2,3,6,4,192]{4,3,2,1,0:T(4,128)(2,1)S(1)}, u32[]{:S(2)}, u32[]{:S(2)}) collective-permute-start(bf16[2,3,6,4,192]{4,3,2,1,0:T(4,128)(2,1)S(1)} %get-tuple-element.31), channel_id=1, source_target_pairs={{0,4},{4,0},{8,12},{12,8},{16,20},{20,16},{24,28},{28,24},{32,36},... | collective-permute-start | bytes 165896 | tf_op jit(solution)/shard_map/ppermute | solution.py:615
  7.3 2.2 %collective-permute-start.2 = (bf16[2,3,6,4,192]{4,3,2,1,0:T(4,128)(2,1)S(1)}, bf16[2,3,6,4,192]{4,3,2,1,0:T(4,128)(2,1)S(1)}, u32[]{:S(2)}, u32[]{:S(2)}) collective-permute-start(bf16[2,3,6,4,192]{4,3,2,1,0:T(4,128)(2,1)S(1)} %get-tuple-element.32), channel_id=1, source_target_pairs={{0,7},{1,4},{2,5},{3,6},{4,3},{5,0},{6,1},{7,2},{8,15},{9,12},{10,... | collective-permute-start | bytes 165896 | tf_op jit(solution)/shard_map/ppermute | solution.py:614
  9.5 0.0 copy-start.1
  9.5 1.0 %copy-done.1 = bf16[4,6,36,192]{3,0,2,1:T(4,128)(2,1)S(1)} copy-done((bf16[4,6,36,192]{3,0,2,1:T(4,128)(2,1)S(1)}, bf16[4,6,36,192]{3,0,2,1:T(4,128)(2,1)}, u32[]{:S(2)}) %copy-start.1) | copy-done | bytes 331800
  10.5 0.0 copy-start.4
  10.5 1.0 %copy-done.4 = bf16[4,6,36,192]{3,0,2,1:T(4,128)(2,1)S(1)} copy-done((bf16[4,6,36,192]{3,0,2,1:T(4,128)(2,1)S(1)}, bf16[4,6,36,192]{3,0,2,1:T(4,128)(2,1)}, u32[]{:S(2)}) %copy-start.4) | copy-done | bytes 331800
  11.5 0.0 copy-start.6
  11.5 0.9 %copy-done.6 = bf16[192,576]{1,0:T(8,128)(2,1)S(1)} copy-done((bf16[192,576]{1,0:T(8,128)(2,1)S(1)}, bf16[192,576]{1,0:T(8,128)(2,1)}, u32[]{:S(2)}) %copy-start.6) | copy-done | bytes 221208
  12.5 0.0 copy-start.7
  12.5 0.9 %copy-done.7 = f32[1,2,6,3312]{3,1,2,0:T(2,128)S(1)} copy-done((f32[1,2,6,3312]{3,1,2,0:T(2,128)S(1)}, f32[1,2,6,3312]{3,1,2,0:T(2,128)}, u32[]{:S(2)}) %copy-start.7) | copy-done | bytes 159000
  13.4 0.0 copy-start.8
  13.4 0.9 %copy-done.8 = bf16[192,192]{1,0:T(8,128)(2,1)S(1)} copy-done((bf16[192,192]{1,0:T(8,128)(2,1)S(1)}, bf16[192,192]{1,0:T(8,128)(2,1)}, u32[]{:S(2)}) %copy-start.8) | copy-done | bytes 73752
  14.3 0.0 copy-start.10
  14.3 0.7 copy-done.10
  14.9 0.0 copy-start.9
  15.0 3.0 %prepare.1 = (f32[12,144,128]{2,1,0:T(8,128)S(1)}, f32[2,144,128]{2,1,0:T(8,128)S(1)}, bf16[3,192,192]{2,1,0:T(8,128)(2,1)S(1)}, bf16[768,192]{1,0:T(8,128)(2,1)...) custom-call(f32[6,2,3312]{2,1,0:T(2,128)S(1)} %bitcast.47, ...), custom_call_target="tpu_custom_call" | custom-call | flops 4000000000 | bytes 4000000 | tf_op jit(solution)/shard_map/prepare/pallas_call | solution.py:164
  18.0 0.0 collective-permute-done.1.lon_ref
  18.0 0.0 collective-permute-done.2.corner_ref
  18.0 0.0 collective-permute-done.lat_ref
  18.0 0.0 copy-done.9
  18.0 12.5 %window_grads.1 = (bf16[864,192]{1,0:T(8,128)(2,1)S(1)}, bf16[32,16,384]{2,1,0:T(8,128)(2,1)}) custom-call(bf16[2,3,120,192]{3,2,1,0:T(8,128)(2,1)S(1)} %get-tuple-element.29.own_ref, bf16[2,3,30,4,192]{4,3,2,1,0:T(4,128)(2,1)S(1)} %collective-permute-done.lat_ref, bf16[2,3,6,4,192]{4,3,2,1,0:T(4,128)(2,1)S(1)} %collective-permute-done.1.lon_ref, ...), custom_call_target="tpu_custom_call" | custom-call | flops 20000000000 | bytes 4000000 | tf_op jit(solution)/shard_map/window_grads/pallas_call | solution.py:392
  30.6 6.0 %all-to-all-start = ((bf16[32,16,384]{2,1,0:T(8,128)(2,1)}), bf16[32,16,384]{2,1,0:T(8,128)(2,1)S(1)}, u32[]{:S(2)}, u32[]{:S(2)}) async-start(bf16[32,16,384]{2,1,0:T(8,128)(2,1)} %get-tuple-element.41), calls=%async_computation | async-start | bytes 786432 | tf_op jit(solution)/shard_map/all_to_all | solution.py:543
  36.6 0.3 pieces.1
  36.9 0.0 copy-start.2
  36.9 0.0 copy-start.5
  36.9 3.0 %collective-permute-start.3 = (bf16[6,24,192]{2,1,0:T(8,128)(2,1)S(1)}, bf16[6,24,192]{2,1,0:T(8,128)(2,1)S(1)}, u32[]{:S(2)}, u32[]{:S(2)}) collective-permute-start(bf16[6,24,192]{2,1,0:T(8,128)(2,1)S(1)} %get-tuple-element.42), channel_id=1, source_target_pairs={{0,4},{4,0},{8,12},{12,8},{16,20},{20,16},{24,28},{28,24},{32,36},... | collective-permute-start | bytes 165896 | tf_op jit(solution)/shard_map/ppermute | solution.py:624
  39.9 7.0 %all-to-all-done = bf16[32,16,384]{2,1,0:T(8,128)(2,1)S(1)} async-done(((bf16[32,16,384]{2,1,0:T(8,128)(2,1)}), bf16[32,16,384]{2,1,0:T(8,128)(2,1)S(1)}, u32[]{:S(2)}, u32[]{:S(2)}) %all-to-all-start) | async-done | bytes 393248 | tf_op jit(solution)/shard_map/all_to_all | solution.py:543
  46.8 0.1 bitcast_convert_fusion
  47.0 0.0 collective-permute-done.3.tail_ref
  47.0 0.7 broadcast_in_dim.6
  47.7 8.2 %all-to-all-start.1 = ((bf16[8,16,768]{2,1,0:T(8,128)(2,1)}), bf16[8,16,768]{2,1,0:T(8,128)(2,1)S(1)}, u32[]{:S(2)}, u32[]{:S(2)}) async-start(bf16[8,16,768]{2,1,0:T(8,128)(2,1)} %broadcast_in_dim.6), calls=%async_computation.1 | async-start | bytes 393216 | tf_op jit(solution)/shard_map/all_to_all | solution.py:552
  56.0 0.8 collective-permute-start.4
  56.8 8.7 %all-to-all-done.1 = bf16[8,16,768]{2,1,0:T(8,128)(2,1)S(1)} async-done(((bf16[8,16,768]{2,1,0:T(8,128)(2,1)}), bf16[8,16,768]{2,1,0:T(8,128)(2,1)S(1)}, u32[]{:S(2)}, u32[]{:S(2)}) %all-to-all-start.1) | async-done | bytes 196640 | tf_op jit(solution)/shard_map/all_to_all | solution.py:552
  65.6 0.0 collective-permute-done.4.lat_ref
  65.6 0.8 broadcast_in_dim.7
  66.3 6.0 %all-to-all-start.2 = ((bf16[32,16,384]{2,1,0:T(8,128)(2,1)}), bf16[32,16,384]{2,1,0:T(8,128)(2,1)S(1)}, u32[]{:S(2)}, u32[]{:S(2)}) async-start(bf16[32,16,384]{2,1,0:T(8,128)(2,1)} %bitcast.16), calls=%async_computation.2 | async-start | bytes 786432 | tf_op jit(solution)/shard_map/all_to_all | solution.py:628
  72.3 0.0 copy-done.2
  72.3 0.0 copy-done.5
  72.3 1.9 %norm_grads.1 = bf16[6,36,4,192]{3,2,1,0:T(4,128)(2,1)} custom-call(bf16[6,36,4,192]{3,2,1,0:T(4,128)(2,1)S(1)} %bitcast.43, bf16[6,36,4,192]{3,2,1,0:T(4,128)(2,1)S(1)} %bitcast.46, f32[1,192]{1,0:T(1,128)S(1)} %get-tuple-element.28.gain_ref, bf16[6,120,192]{2,1,0:T(8,128)(2,1)S(1)} %get-tuple-element.40.body_ref, ...), custom_call_target="tpu_custom_call" | custom-call | flops 10000000 | bytes 1500000 | tf_op jit(solution)/shard_map/norm_grads/pallas_call | solution.py:484
  74.2 8.3 %all-to-all-done.2.parts_ref = bf16[32,16,384]{2,1,0:T(8,128)(2,1)S(1)} async-done(((bf16[32,16,384]{2,1,0:T(8,128)(2,1)}), bf16[32,16,384]{2,1,0:T(8,128)(2,1)S(1)}, u32[]{:S(2)}, u32[]{:S(2)}) %all-to-all-start.2) | async-done | bytes 393248 | tf_op jit(solution)/shard_map/all_to_all | solution.py:628
  82.5 0.9 %unpack.1 = (f32[1,192]{1,0:T(1,128)}, f32[192,576]{1,0:T(8,128)}, f32[192,192]{1,0:T(8,128)}, f32[6,2,3312]{2,1,0:T(2,128)}) custom-call(bf16[32,16,384]{2,1,0:T(8,128)(2,1)S(1)} %all-to-all-done.2.parts_ref), custom_call_target="tpu_custom_call" | custom-call | tf_op jit(solution)/shard_map/unpack/pallas_call | solution.py:526
  (15 shorter events, 0.2 us)
Async XLA Ops:
  0.6 1.0 %copy-start = (bf16[4,6,36,192]{3,0,2,1:T(4,128)(2,1)S(1)}, bf16[4,6,36,192]{3,0,2,1:T(4,128)(2,1)}, u32[]{:S(2)}) copy-start(bf16[4,6,36,192]{3,0,2,1:T(4,128)(2,1)} %param.6) | copy-start | bytes 995332
  1.6 1.0 %copy-start.3 = (bf16[4,6,36,192]{3,0,2,1:T(4,128)(2,1)S(1)}, bf16[4,6,36,192]{3,0,2,1:T(4,128)(2,1)}, u32[]{:S(2)}) copy-start(bf16[4,6,36,192]{3,0,2,1:T(4,128)(2,1)} %param.7) | copy-start | bytes 995332
  2.9 15.1 %collective-permute-start = (bf16[2,3,30,4,192]{4,3,2,1,0:T(4,128)(2,1)S(1)}, bf16[2,3,30,4,192]{4,3,2,1,0:T(4,128)(2,1)S(1)}, u32[]{:S(2)}, u32[]{:S(2)}) collective-permute-start(bf16[2,3,30,4,192]{4,3,2,1,0:T(4,128)(2,1)S(1)} %get-tuple-element.30), channel_id=1, source_target_pairs={{0,3},{1,0},{2,1},{3,2},{4,7},{5,4},{6,5},{7,6},{8,11},{9,8},{10,9... | collective-permute-start | bytes 829448 | tf_op jit(solution)/shard_map/ppermute | solution.py:616
  6.3 11.7 %collective-permute-start.1 = (bf16[2,3,6,4,192]{4,3,2,1,0:T(4,128)(2,1)S(1)}, bf16[2,3,6,4,192]{4,3,2,1,0:T(4,128)(2,1)S(1)}, u32[]{:S(2)}, u32[]{:S(2)}) collective-permute-start(bf16[2,3,6,4,192]{4,3,2,1,0:T(4,128)(2,1)S(1)} %get-tuple-element.31), channel_id=1, source_target_pairs={{0,4},{4,0},{8,12},{12,8},{16,20},{20,16},{24,28},{28,24},{32,36},... | collective-permute-start | bytes 165896 | tf_op jit(solution)/shard_map/ppermute | solution.py:615
  7.3 10.7 %collective-permute-start.2 = (bf16[2,3,6,4,192]{4,3,2,1,0:T(4,128)(2,1)S(1)}, bf16[2,3,6,4,192]{4,3,2,1,0:T(4,128)(2,1)S(1)}, u32[]{:S(2)}, u32[]{:S(2)}) collective-permute-start(bf16[2,3,6,4,192]{4,3,2,1,0:T(4,128)(2,1)S(1)} %get-tuple-element.32), channel_id=1, source_target_pairs={{0,7},{1,4},{2,5},{3,6},{4,3},{5,0},{6,1},{7,2},{8,15},{9,12},{10,... | collective-permute-start | bytes 165896 | tf_op jit(solution)/shard_map/ppermute | solution.py:614
  9.5 1.0 %copy-start.1 = (bf16[4,6,36,192]{3,0,2,1:T(4,128)(2,1)S(1)}, bf16[4,6,36,192]{3,0,2,1:T(4,128)(2,1)}, u32[]{:S(2)}) copy-start(bf16[4,6,36,192]{3,0,2,1:T(4,128)(2,1)} %param.6) | copy-start | bytes 995332
  10.5 1.0 %copy-start.4 = (bf16[4,6,36,192]{3,0,2,1:T(4,128)(2,1)S(1)}, bf16[4,6,36,192]{3,0,2,1:T(4,128)(2,1)}, u32[]{:S(2)}) copy-start(bf16[4,6,36,192]{3,0,2,1:T(4,128)(2,1)} %param.7) | copy-start | bytes 995332
  11.5 0.9 %copy-start.6 = (bf16[192,576]{1,0:T(8,128)(2,1)S(1)}, bf16[192,576]{1,0:T(8,128)(2,1)}, u32[]{:S(2)}) copy-start(bf16[192,576]{1,0:T(8,128)(2,1)} %wqkv_ref.1) | copy-start | bytes 663556
  12.5 0.9 %copy-start.7 = (f32[1,2,6,3312]{3,1,2,0:T(2,128)S(1)}, f32[1,2,6,3312]{3,1,2,0:T(2,128)}, u32[]{:S(2)}) copy-start(f32[1,2,6,3312]{3,1,2,0:T(2,128)} %param.11) | copy-start | bytes 476932
  13.4 0.9 %copy-start.8 = (bf16[192,192]{1,0:T(8,128)(2,1)S(1)}, bf16[192,192]{1,0:T(8,128)(2,1)}, u32[]{:S(2)}) copy-start(bf16[192,192]{1,0:T(8,128)(2,1)} %wproj_ref.3) | copy-start | bytes 221188
  14.3 0.7 copy-start.10
  14.9 3.1 %copy-start.9 = (bf16[192,192]{1,0:T(8,128)(2,1)S(1)}, bf16[192,192]{1,0:T(8,128)(2,1)}, u32[]{:S(2)}) copy-start(bf16[192,192]{1,0:T(8,128)(2,1)} %wproj_ref.3) | copy-start | bytes 221188
  30.6 16.3 %all-to-all-start = ((bf16[32,16,384]{2,1,0:T(8,128)(2,1)}), bf16[32,16,384]{2,1,0:T(8,128)(2,1)S(1)}, u32[]{:S(2)}, u32[]{:S(2)}) async-start(bf16[32,16,384]{2,1,0:T(8,128)(2,1)} %get-tuple-element.41), calls=%async_computation | async-start | bytes 786432 | tf_op jit(solution)/shard_map/all_to_all | solution.py:543
  36.9 35.5 %copy-start.2 = (bf16[4,6,36,192]{3,0,2,1:T(4,128)(2,1)S(1)}, bf16[4,6,36,192]{3,0,2,1:T(4,128)(2,1)}, u32[]{:S(2)}) copy-start(bf16[4,6,36,192]{3,0,2,1:T(4,128)(2,1)} %param.6) | copy-start | bytes 995332
  36.9 35.5 %copy-start.5 = (bf16[4,6,36,192]{3,0,2,1:T(4,128)(2,1)S(1)}, bf16[4,6,36,192]{3,0,2,1:T(4,128)(2,1)}, u32[]{:S(2)}) copy-start(bf16[4,6,36,192]{3,0,2,1:T(4,128)(2,1)} %param.7) | copy-start | bytes 995332
  36.9 10.2 %collective-permute-start.3 = (bf16[6,24,192]{2,1,0:T(8,128)(2,1)S(1)}, bf16[6,24,192]{2,1,0:T(8,128)(2,1)S(1)}, u32[]{:S(2)}, u32[]{:S(2)}) collective-permute-start(bf16[6,24,192]{2,1,0:T(8,128)(2,1)S(1)} %get-tuple-element.42), channel_id=1, source_target_pairs={{0,4},{4,0},{8,12},{12,8},{16,20},{20,16},{24,28},{28,24},{32,36},... | collective-permute-start | bytes 165896 | tf_op jit(solution)/shard_map/ppermute | solution.py:624
  47.7 17.7 %all-to-all-start.1 = ((bf16[8,16,768]{2,1,0:T(8,128)(2,1)}), bf16[8,16,768]{2,1,0:T(8,128)(2,1)S(1)}, u32[]{:S(2)}, u32[]{:S(2)}) async-start(bf16[8,16,768]{2,1,0:T(8,128)(2,1)} %broadcast_in_dim.6), calls=%async_computation.1 | async-start | bytes 393216 | tf_op jit(solution)/shard_map/all_to_all | solution.py:552
  56.0 9.6 %collective-permute-start.4 = (bf16[3,144,192]{2,1,0:T(8,128)(2,1)S(1)}, bf16[3,144,192]{2,1,0:T(8,128)(2,1)S(1)}, u32[]{:S(2)}, u32[]{:S(2)}) collective-permute-start(bf16[3,144,192]{2,1,0:T(8,128)(2,1)S(1)} %pad_maximum_fusion), channel_id=1, source_target_pairs={{0,1},{1,2},{2,3},{3,0},{4,5},{5,6},{6,7},{7,4},{8,9},{9,10},{10,1... | collective-permute-start | bytes 497672 | tf_op jit(solution)/shard_map/ppermute | solution.py:626
  66.3 16.1 %all-to-all-start.2 = ((bf16[32,16,384]{2,1,0:T(8,128)(2,1)}), bf16[32,16,384]{2,1,0:T(8,128)(2,1)S(1)}, u32[]{:S(2)}, u32[]{:S(2)}) async-start(bf16[32,16,384]{2,1,0:T(8,128)(2,1)} %bitcast.16), calls=%async_computation.2 | async-start | bytes 786432 | tf_op jit(solution)/shard_map/all_to_all | solution.py:628

commit v5 on v4

--- a/solution.py
+++ b/solution.py
@@ -90,10 +90,26 @@
 
 
 def prepare_kernel(
-    table_ref, wqkv_ref, wproj_ref, gain_ref, x_ref, g_ref,
-    main_ref, left_ref, w3_ref, w3t_ref, wprojt_ref, own_ref, match_ref, gain_out, wide, pairs,
+    table_hbm, wqkv_hbm, wproj_hbm, gain_hbm, x_hbm, g_hbm,
+    main_ref, left_ref, w3_ref, w3t_ref, wproj_ref, wprojt_ref, own_ref, match_ref, gain_out,
+    wide, pairs, table_ref, wqkv_ref, mine, sems,
 ):
-    gain_out[...] = gain_ref[...]
+    kept = pl.ds(3, 3), pl.ds(6, 30)
+    moves = (
+        (table_hbm, table_ref),
+        (wqkv_hbm, wqkv_ref),
+        (wproj_hbm, wproj_ref),
+        (gain_hbm, gain_out),
+        (x_hbm.at[kept], mine.at[0]),
+        (g_hbm.at[kept], mine.at[1]),
+    )
+    copies = [pltpu.make_async_copy(a, b, sems.at[n]) for n, (a, b) in enumerate(moves)]
+    for copy in copies:
+        copy.start()
+    for oj in range(WLON):
+        match_ref[oj] = offset_match(oj, True)
+    for copy in copies:
+        copy.wait()
     for k in range(3):
         part = wqkv_ref[:, k * C : (k + 1) * C]
         w3_ref[k] = part
@@ -101,8 +117,8 @@
         w3t_ref[k * WIDTH + C : (k + 1) * WIDTH] = jnp.zeros((WIDTH - C, C), bf16)
     wprojt_ref[...] = wproj_ref[...].T
     for a in range(3):
-        own_ref[0, a] = x_ref[a + 3, 6:36].reshape(BODY, C)
-        own_ref[1, a] = g_ref[a + 3, 6:36].reshape(BODY, C)
+        for k in range(2):
+            own_ref[k, a] = mine[k, a].reshape(BODY, C)
     wide[...] = jnp.zeros_like(wide)
     for h in range(HEADS):
         for lz in range(2):
@@ -130,7 +146,6 @@
     low = (rest - middle.astype(f32)).astype(bf16)
     lane_head = iota((PAIRS, MAIN), 1) // LEFT
     for oj in range(WLON):
-        match_ref[oj] = offset_match(oj, True)
         match = offset_match(oj, False)
         dense = dot(high, match) + (dot(middle, match) + dot(low, match))
         for lz in range(2):
@@ -159,6 +174,10 @@
         left_ref[lz] = jnp.where(allowed, left_ref[lz], -1e30)
 
 
+def in_hbm(array):
+    return pltpu.with_memory_space_constraint(array, pltpu.HBM)
+
+
 def prepare(table, wqkv, wproj, gain, x, g):
     vmem = pl.BlockSpec(memory_space=pltpu.VMEM)
     return pl.pallas_call(
@@ -169,19 +188,27 @@
             jax.ShapeDtypeStruct((3, C, C), bf16),
             jax.ShapeDtypeStruct((3 * WIDTH, C), bf16),
             jax.ShapeDtypeStruct((C, C), bf16),
+            jax.ShapeDtypeStruct((C, C), bf16),
             jax.ShapeDtypeStruct((2, 3, BODY, C), bf16),
             jax.ShapeDtypeStruct((WLON, 2 * MAIN, PAIRS * 32), bf16),
             jax.ShapeDtypeStruct((1, C), f32),
         ),
-        in_specs=[vmem] * 6,
-        out_specs=(vmem,) * 8,
-        scratch_shapes=[pltpu.VMEM((16, WIDE), f32), pltpu.VMEM((3, TYPES * 16, 128), f32)],
+        in_specs=[pl.BlockSpec(memory_space=pltpu.HBM)] * 6,
+        out_specs=(vmem,) * 9,
+        scratch_shapes=[
+            pltpu.VMEM((16, WIDE), f32),
+            pltpu.VMEM((3, TYPES * 16, 128), f32),
+            pltpu.VMEM((HEADS, 2, TABLE), f32),
+            pltpu.VMEM((C, 3 * C), bf16),
+            pltpu.VMEM((2, 3, 30, 4, C), bf16),
+            pltpu.SemaphoreType.DMA((6,)),
+        ],
         compiler_params=pltpu.CompilerParams(vmem_limit_bytes=VMEM_LIMIT),
         cost_estimate=pl.CostEstimate(
             flops=4_000_000_000, bytes_accessed=4_000_000, transcendentals=0
         ),
         name="prepare",
-    )(table, wqkv, wproj, gain, x, g)
+    )(*(in_hbm(a) for a in (table, wqkv, wproj, gain, x, g)))
 
 
 def normalised(values):
@@ -597,7 +624,7 @@
         scratch_shapes=[pltpu.SemaphoreType.DMA((6,))],
         compiler_params=pltpu.CompilerParams(vmem_limit_bytes=VMEM_LIMIT),
         name="pack",
-    )(x, g)
+    )(in_hbm(x), in_hbm(g))
 
 
 def on_device(x, g, ln_gain, w_qkv, w_proj, bias_table):
@@ -614,11 +641,11 @@
     corner_in = lax.ppermute(to_corner, both, corner_down)
     lon_in = lax.ppermute(to_lon, lon_axes, lon_swap)
     lat_in = lax.ppermute(to_lat, lat_axes, lat_down)
-    bias, bias_left, w3, w3t, wproj_t, own, match, gain = prepare(
+    bias, bias_left, w3, w3t, wproj, wproj_t, own, match, gain = prepare(
         bias_table[0].transpose(1, 0, 2), w_qkv, w_proj, ln_gain.reshape(1, C), x, g
     )
     rows, send = main(
-        own, lat_in, lon_in, corner_in, gain, w3, w3t, w_proj, wproj_t, bias, bias_left, match
+        own, lat_in, lon_in, corner_in, gain, w3, w3t, wproj, wproj_t, bias, bias_left, match
     )
     body, tail = pieces(rows)
     tail = lax.ppermute(tail, lon_axes, lon_swap)

time: 84.1 us -> 79.6 us (0.946)
  local copies, waits for them, and re-layouts: 9.03 us -> 1.55 us
  Pallas kernels: 18.9 us -> 20.7 us
  starting transfers between devices: 30.5 us -> 31.9 us
    unnamed x26 -> x8, local copies, waits for them, and re-layouts: 7.52 us -> 0.04 us
    all_to_all x1, starting transfers between devices: 6 us -> 7.44 us  [scattered(): got = lax.all_to_all(send, GROUP, 0, 0, tiled=True)]
    pallas_call x1, Pallas kernels: 3.03 us -> 3.93 us  [prepare(): pl.pallas_call(prepare_kernel, out_shape=(jax.ShapeDtypeStruct((TYPES, WI...]
    pallas_call x1, Pallas kernels: 0.27 us -> 1.15 us  [pack(): pl.pallas_call(pack_kernel, out_shape=(jax.ShapeDtypeStruct((2, 3, 6, 4,...]
  transfers between devices with their start and end apart: 8 -> 8, of which waited for: 3 -> 3; matrix products, arithmetic and copies ran while one was open for 0% -> 0% of each run, Pallas kernels for 6% -> 8%
where the time goes in v5:
time: 79.6 us; the launch traced here: 79.2 us
  starting transfers between devices  31.9 us (40%)
  waiting for transfers between devices  23.9 us (30%)
  Pallas kernels  20.7 us (26%)
  local copies, waits for them, and re-layouts  1.55 us (2%)
  between operations  0.83 us (1%)
    pallas_call x1, Pallas kernels, main(): pl.pallas_call(main_kernel, out_shape=(jax.ShapeDtypeStruct((WINDOWS * WI...  12.5 us
    all_to_all x1, waiting for transfers between devices, exchanged(): lax.all_to_all(jnp.broadcast_to(mixed[None], (count,) + mixed.shape), RES...  8.65 us
    all_to_all x1, waiting for transfers between devices, on_device(): parts = lax.all_to_all(spread, GROUP, 0, 0, tiled=True)  8.29 us
    all_to_all x1, starting transfers between devices, exchanged(): lax.all_to_all(jnp.broadcast_to(mixed[None], (count,) + mixed.shape), RES...  8.18 us
    all_to_all x1, starting transfers between devices, scattered(): got = lax.all_to_all(send, GROUP, 0, 0, tiled=True)  7.44 us
    all_to_all x1, waiting for transfers between devices, scattered(): got = lax.all_to_all(send, GROUP, 0, 0, tiled=True)  6.97 us
    all_to_all x1, starting transfers between devices, on_device(): parts = lax.all_to_all(spread, GROUP, 0, 0, tiled=True)  5.97 us
    pallas_call x1, Pallas kernels, prepare(): pl.pallas_call(prepare_kernel, out_shape=(jax.ShapeDtypeStruct((TYPES, WI...  3.93 us
  transfers between devices with their start and end apart: 8, of which 3 were waited for; matrix products, arithmetic and copies ran while one was open for 0% of the time, Pallas kernels for 8%

profile of v5, /device:TPU:1, one launch (start us, length us, event | category | flops | bytes accessed | tf_op | source)
XLA Modules:
  0.0 79.2 jit_solution(12590668722114852960)
XLA Ops:
  0.6 1.1 %pack.1 = (bf16[2,3,6,4,192]{4,3,2,1,0:T(4,128)(2,1)S(1)}, bf16[2,3,6,4,192]{4,3,2,1,0:T(4,128)(2,1)S(1)}, bf16[2,3,30,4,192]{4,3,2,1,0:T(4,128)(2,1)S(1)}) custom-call(bf16[6,36,4,192]{3,2,1,0:T(4,128)(2,1)} %bitcast.41, bf16[6,36,4,192]{3,2,1,0:T(4,128)(2,1)} %bitcast.44), custom_call_target="tpu_custom_call" | custom-call | tf_op jit(solution)/shard_map/pack/pallas_call | solution.py:615
  1.8 3.3 %collective-permute-start = (bf16[2,3,30,4,192]{4,3,2,1,0:T(4,128)(2,1)S(1)}, bf16[2,3,30,4,192]{4,3,2,1,0:T(4,128)(2,1)S(1)}, u32[]{:S(2)}, u32[]{:S(2)}) collective-permute-start(bf16[2,3,30,4,192]{4,3,2,1,0:T(4,128)(2,1)S(1)} %get-tuple-element.31), channel_id=1, source_target_pairs={{0,3},{1,0},{2,1},{3,2},{4,7},{5,4},{6,5},{7,6},{8,11},{9,8},{10,9... | collective-permute-start | bytes 829448 | tf_op jit(solution)/shard_map/ppermute | solution.py:643
  5.1 1.0 %collective-permute-start.1 = (bf16[2,3,6,4,192]{4,3,2,1,0:T(4,128)(2,1)S(1)}, bf16[2,3,6,4,192]{4,3,2,1,0:T(4,128)(2,1)S(1)}, u32[]{:S(2)}, u32[]{:S(2)}) collective-permute-start(bf16[2,3,6,4,192]{4,3,2,1,0:T(4,128)(2,1)S(1)} %get-tuple-element.32), channel_id=1, source_target_pairs={{0,4},{4,0},{8,12},{12,8},{16,20},{20,16},{24,28},{28,24},{32,36},... | collective-permute-start | bytes 165896 | tf_op jit(solution)/shard_map/ppermute | solution.py:642
  6.1 2.2 %collective-permute-start.2 = (bf16[2,3,6,4,192]{4,3,2,1,0:T(4,128)(2,1)S(1)}, bf16[2,3,6,4,192]{4,3,2,1,0:T(4,128)(2,1)S(1)}, u32[]{:S(2)}, u32[]{:S(2)}) collective-permute-start(bf16[2,3,6,4,192]{4,3,2,1,0:T(4,128)(2,1)S(1)} %get-tuple-element.33), channel_id=1, source_target_pairs={{0,7},{1,4},{2,5},{3,6},{4,3},{5,0},{6,1},{7,2},{8,15},{9,12},{10,... | collective-permute-start | bytes 165896 | tf_op jit(solution)/shard_map/ppermute | solution.py:641
  8.3 3.9 %prepare.1 = (f32[12,144,128]{2,1,0:T(8,128)S(1)}, f32[2,144,128]{2,1,0:T(8,128)S(1)}, bf16[3,192,192]{2,1,0:T(8,128)(2,1)S(1)}, bf16[768,192]{1,0:T(8,128)(2,1)...) custom-call(f32[6,2,3312]{2,1,0:T(2,128)} %bitcast.48, ...), custom_call_target="tpu_custom_call" | custom-call | flops 4000000000 | bytes 4000000 | tf_op jit(solution)/shard_map/prepare/pallas_call | solution.py:183
  12.3 0.0 collective-permute-done.1.lon_ref
  12.3 0.0 collective-permute-done.2.corner_ref
  12.3 0.0 collective-permute-done.lat_ref
  12.3 12.5 %window_grads.1 = (bf16[864,192]{1,0:T(8,128)(2,1)S(1)}, bf16[32,16,384]{2,1,0:T(8,128)(2,1)}) custom-call(bf16[2,3,120,192]{3,2,1,0:T(8,128)(2,1)S(1)} %get-tuple-element.30.own_ref, bf16[2,3,30,4,192]{4,3,2,1,0:T(4,128)(2,1)S(1)} %collective-permute-done.lat_ref, bf16[2,3,6,4,192]{4,3,2,1,0:T(4,128)(2,1)S(1)} %collective-permute-done.1.lon_ref, ...), custom_call_target="tpu_custom_call" | custom-call | flops 20000000000 | bytes 4000000 | tf_op jit(solution)/shard_map/window_grads/pallas_call | solution.py:419
  24.8 7.4 %all-to-all-start = ((bf16[32,16,384]{2,1,0:T(8,128)(2,1)}), bf16[32,16,384]{2,1,0:T(8,128)(2,1)S(1)}, u32[]{:S(2)}, u32[]{:S(2)}) async-start(bf16[32,16,384]{2,1,0:T(8,128)(2,1)} %get-tuple-element.43), calls=%async_computation | async-start | bytes 786432 | tf_op jit(solution)/shard_map/all_to_all | solution.py:570
  32.3 0.3 pieces.1
  32.6 0.0 copy-start
  32.6 0.0 copy-start.1
  32.6 3.0 %collective-permute-start.3 = (bf16[6,24,192]{2,1,0:T(8,128)(2,1)S(1)}, bf16[6,24,192]{2,1,0:T(8,128)(2,1)S(1)}, u32[]{:S(2)}, u32[]{:S(2)}) collective-permute-start(bf16[6,24,192]{2,1,0:T(8,128)(2,1)S(1)} %get-tuple-element.44), channel_id=1, source_target_pairs={{0,4},{4,0},{8,12},{12,8},{16,20},{20,16},{24,28},{28,24},{32,36},... | collective-permute-start | bytes 165896 | tf_op jit(solution)/shard_map/ppermute | solution.py:651
  35.6 7.0 %all-to-all-done = bf16[32,16,384]{2,1,0:T(8,128)(2,1)S(1)} async-done(((bf16[32,16,384]{2,1,0:T(8,128)(2,1)}), bf16[32,16,384]{2,1,0:T(8,128)(2,1)S(1)}, u32[]{:S(2)}, u32[]{:S(2)}) %all-to-all-start) | async-done | bytes 393248 | tf_op jit(solution)/shard_map/all_to_all | solution.py:570
  42.5 0.1 bitcast_convert_fusion
  42.7 0.0 collective-permute-done.3.tail_ref
  42.8 0.7 broadcast_in_dim.6
  43.4 8.2 %all-to-all-start.1 = ((bf16[8,16,768]{2,1,0:T(8,128)(2,1)}), bf16[8,16,768]{2,1,0:T(8,128)(2,1)S(1)}, u32[]{:S(2)}, u32[]{:S(2)}) async-start(bf16[8,16,768]{2,1,0:T(8,128)(2,1)} %broadcast_in_dim.6), calls=%async_computation.1 | async-start | bytes 393216 | tf_op jit(solution)/shard_map/all_to_all | solution.py:579
  51.7 0.8 %collective-permute-start.4 = (bf16[3,144,192]{2,1,0:T(8,128)(2,1)S(1)}, bf16[3,144,192]{2,1,0:T(8,128)(2,1)S(1)}, u32[]{:S(2)}, u32[]{:S(2)}) collective-permute-start(bf16[3,144,192]{2,1,0:T(8,128)(2,1)S(1)} %pad_maximum_fusion), channel_id=1, source_target_pairs={{0,1},{1,2},{2,3},{3,0},{4,5},{5,6},{6,7},{7,4},{8,9},{9,10},{10,1... | collective-permute-start | bytes 497672 | tf_op jit(solution)/shard_map/ppermute | solution.py:653
  52.5 8.7 %all-to-all-done.1 = bf16[8,16,768]{2,1,0:T(8,128)(2,1)S(1)} async-done(((bf16[8,16,768]{2,1,0:T(8,128)(2,1)}), bf16[8,16,768]{2,1,0:T(8,128)(2,1)S(1)}, u32[]{:S(2)}, u32[]{:S(2)}) %all-to-all-start.1) | async-done | bytes 196640 | tf_op jit(solution)/shard_map/all_to_all | solution.py:579
  61.3 0.0 collective-permute-done.4.lat_ref
  61.3 0.8 broadcast_in_dim.7
  62.1 6.0 %all-to-all-start.2 = ((bf16[32,16,384]{2,1,0:T(8,128)(2,1)}), bf16[32,16,384]{2,1,0:T(8,128)(2,1)S(1)}, u32[]{:S(2)}, u32[]{:S(2)}) async-start(bf16[32,16,384]{2,1,0:T(8,128)(2,1)} %bitcast.16), calls=%async_computation.2 | async-start | bytes 786432 | tf_op jit(solution)/shard_map/all_to_all | solution.py:655
  68.0 0.0 copy-done
  68.1 0.0 copy-done.1
  68.1 1.9 %norm_grads.1 = bf16[6,36,4,192]{3,2,1,0:T(4,128)(2,1)} custom-call(bf16[6,36,4,192]{3,2,1,0:T(4,128)(2,1)S(1)} %bitcast.43, bf16[6,36,4,192]{3,2,1,0:T(4,128)(2,1)S(1)} %bitcast.46, f32[1,192]{1,0:T(1,128)S(1)} %get-tuple-element.29.gain_ref, bf16[6,120,192]{2,1,0:T(8,128)(2,1)S(1)} %get-tuple-element.42.body_ref, ...), custom_call_target="tpu_custom_call" | custom-call | flops 10000000 | bytes 1500000 | tf_op jit(solution)/shard_map/norm_grads/pallas_call | solution.py:511
  69.9 8.3 %all-to-all-done.2.parts_ref = bf16[32,16,384]{2,1,0:T(8,128)(2,1)S(1)} async-done(((bf16[32,16,384]{2,1,0:T(8,128)(2,1)}), bf16[32,16,384]{2,1,0:T(8,128)(2,1)S(1)}, u32[]{:S(2)}, u32[]{:S(2)}) %all-to-all-start.2) | async-done | bytes 393248 | tf_op jit(solution)/shard_map/all_to_all | solution.py:655
  78.2 0.9 %unpack.1 = (f32[1,192]{1,0:T(1,128)}, f32[192,576]{1,0:T(8,128)}, f32[192,192]{1,0:T(8,128)}, f32[6,2,3312]{2,1,0:T(2,128)}) custom-call(bf16[32,16,384]{2,1,0:T(8,128)(2,1)S(1)} %all-to-all-done.2.parts_ref), custom_call_target="tpu_custom_call" | custom-call | tf_op jit(solution)/shard_map/unpack/pallas_call | solution.py:553
  (15 shorter events, 0.2 us)
Async XLA Ops:
  1.8 10.5 %collective-permute-start = (bf16[2,3,30,4,192]{4,3,2,1,0:T(4,128)(2,1)S(1)}, bf16[2,3,30,4,192]{4,3,2,1,0:T(4,128)(2,1)S(1)}, u32[]{:S(2)}, u32[]{:S(2)}) collective-permute-start(bf16[2,3,30,4,192]{4,3,2,1,0:T(4,128)(2,1)S(1)} %get-tuple-element.31), channel_id=1, source_target_pairs={{0,3},{1,0},{2,1},{3,2},{4,7},{5,4},{6,5},{7,6},{8,11},{9,8},{10,9... | collective-permute-start | bytes 829448 | tf_op jit(solution)/shard_map/ppermute | solution.py:643
  5.1 7.2 %collective-permute-start.1 = (bf16[2,3,6,4,192]{4,3,2,1,0:T(4,128)(2,1)S(1)}, bf16[2,3,6,4,192]{4,3,2,1,0:T(4,128)(2,1)S(1)}, u32[]{:S(2)}, u32[]{:S(2)}) collective-permute-start(bf16[2,3,6,4,192]{4,3,2,1,0:T(4,128)(2,1)S(1)} %get-tuple-element.32), channel_id=1, source_target_pairs={{0,4},{4,0},{8,12},{12,8},{16,20},{20,16},{24,28},{28,24},{32,36},... | collective-permute-start | bytes 165896 | tf_op jit(solution)/shard_map/ppermute | solution.py:642
  6.1 6.2 %collective-permute-start.2 = (bf16[2,3,6,4,192]{4,3,2,1,0:T(4,128)(2,1)S(1)}, bf16[2,3,6,4,192]{4,3,2,1,0:T(4,128)(2,1)S(1)}, u32[]{:S(2)}, u32[]{:S(2)}) collective-permute-start(bf16[2,3,6,4,192]{4,3,2,1,0:T(4,128)(2,1)S(1)} %get-tuple-element.33), channel_id=1, source_target_pairs={{0,7},{1,4},{2,5},{3,6},{4,3},{5,0},{6,1},{7,2},{8,15},{9,12},{10,... | collective-permute-start | bytes 165896 | tf_op jit(solution)/shard_map/ppermute | solution.py:641
  24.8 17.7 %all-to-all-start = ((bf16[32,16,384]{2,1,0:T(8,128)(2,1)}), bf16[32,16,384]{2,1,0:T(8,128)(2,1)S(1)}, u32[]{:S(2)}, u32[]{:S(2)}) async-start(bf16[32,16,384]{2,1,0:T(8,128)(2,1)} %get-tuple-element.43), calls=%async_computation | async-start | bytes 786432 | tf_op jit(solution)/shard_map/all_to_all | solution.py:570
  32.6 35.5 %copy-start = (bf16[4,6,36,192]{3,0,2,1:T(4,128)(2,1)S(1)}, bf16[4,6,36,192]{3,0,2,1:T(4,128)(2,1)}, u32[]{:S(2)}) copy-start(bf16[4,6,36,192]{3,0,2,1:T(4,128)(2,1)} %param.6) | copy-start | bytes 995332
  32.6 35.5 %copy-start.1 = (bf16[4,6,36,192]{3,0,2,1:T(4,128)(2,1)S(1)}, bf16[4,6,36,192]{3,0,2,1:T(4,128)(2,1)}, u32[]{:S(2)}) copy-start(bf16[4,6,36,192]{3,0,2,1:T(4,128)(2,1)} %param.7) | copy-start | bytes 995332
  32.6 10.2 %collective-permute-start.3 = (bf16[6,24,192]{2,1,0:T(8,128)(2,1)S(1)}, bf16[6,24,192]{2,1,0:T(8,128)(2,1)S(1)}, u32[]{:S(2)}, u32[]{:S(2)}) collective-permute-start(bf16[6,24,192]{2,1,0:T(8,128)(2,1)S(1)} %get-tuple-element.44), channel_id=1, source_target_pairs={{0,4},{4,0},{8,12},{12,8},{16,20},{20,16},{24,28},{28,24},{32,36},... | collective-permute-start | bytes 165896 | tf_op jit(solution)/shard_map/ppermute | solution.py:651
  43.4 17.7 %all-to-all-start.1 = ((bf16[8,16,768]{2,1,0:T(8,128)(2,1)}), bf16[8,16,768]{2,1,0:T(8,128)(2,1)S(1)}, u32[]{:S(2)}, u32[]{:S(2)}) async-start(bf16[8,16,768]{2,1,0:T(8,128)(2,1)} %broadcast_in_dim.6), calls=%async_computation.1 | async-start | bytes 393216 | tf_op jit(solution)/shard_map/all_to_all | solution.py:579
  51.7 9.6 %collective-permute-start.4 = (bf16[3,144,192]{2,1,0:T(8,128)(2,1)S(1)}, bf16[3,144,192]{2,1,0:T(8,128)(2,1)S(1)}, u32[]{:S(2)}, u32[]{:S(2)}) collective-permute-start(bf16[3,144,192]{2,1,0:T(8,128)(2,1)S(1)} %pad_maximum_fusion), channel_id=1, source_target_pairs={{0,1},{1,2},{2,3},{3,0},{4,5},{5,6},{6,7},{7,4},{8,9},{9,10},{10,1... | collective-permute-start | bytes 497672 | tf_op jit(solution)/shard_map/ppermute | solution.py:653
  62.1 16.1 %all-to-all-start.2 = ((bf16[32,16,384]{2,1,0:T(8,128)(2,1)}), bf16[32,16,384]{2,1,0:T(8,128)(2,1)S(1)}, u32[]{:S(2)}, u32[]{:S(2)}) async-start(bf16[32,16,384]{2,1,0:T(8,128)(2,1)} %bitcast.16), calls=%async_computation.2 | async-start | bytes 786432 | tf_op jit(solution)/shard_map/all_to_all | solution.py:655

commit v6 on v5

--- a/solution.py
+++ b/solution.py
@@ -43,7 +43,7 @@
 VMEM_LIMIT = 40 * 1024 * 1024
 
 NN = (((1,), (0,)), ((), ()))
-NT = (((1,), (1,)), ((), ()))
+TN = (((0,), (0,)), ((), ()))
 
 
 def dot(a, b, dims=NN):
@@ -91,8 +91,8 @@
 
 def prepare_kernel(
     table_hbm, wqkv_hbm, wproj_hbm, gain_hbm, x_hbm, g_hbm,
-    main_ref, left_ref, w3_ref, w3t_ref, wproj_ref, wprojt_ref, own_ref, match_ref, gain_out,
-    wide, pairs, table_ref, wqkv_ref, mine, sems,
+    main_ref, left_ref, w3_ref, w3t_ref, wprojt_ref, own_ref, match_ref, gain_out,
+    wide, pairs, table_ref, wqkv_ref, wproj_ref, mine, sems,
 ):
     kept = pl.ds(3, 3), pl.ds(6, 30)
     moves = (
@@ -188,18 +188,18 @@
             jax.ShapeDtypeStruct((3, C, C), bf16),
             jax.ShapeDtypeStruct((3 * WIDTH, C), bf16),
             jax.ShapeDtypeStruct((C, C), bf16),
-            jax.ShapeDtypeStruct((C, C), bf16),
             jax.ShapeDtypeStruct((2, 3, BODY, C), bf16),
             jax.ShapeDtypeStruct((WLON, 2 * MAIN, PAIRS * 32), bf16),
             jax.ShapeDtypeStruct((1, C), f32),
         ),
         in_specs=[pl.BlockSpec(memory_space=pltpu.HBM)] * 6,
-        out_specs=(vmem,) * 9,
+        out_specs=(vmem,) * 8,
         scratch_shapes=[
             pltpu.VMEM((16, WIDE), f32),
             pltpu.VMEM((3, TYPES * 16, 128), f32),
             pltpu.VMEM((HEADS, 2, TABLE), f32),
             pltpu.VMEM((C, 3 * C), bf16),
+            pltpu.VMEM((C, C), bf16),
             pltpu.VMEM((2, 3, 30, 4, C), bf16),
             pltpu.SemaphoreType.DMA((6,)),
         ],
@@ -225,11 +225,11 @@
 
 
 def main_kernel(
-    own_ref, lat_ref, lon_ref, corner_ref, gain_ref, w3_ref, w3t_ref, wproj_ref, wprojt_ref,
+    own_ref, lat_ref, lon_ref, corner_ref, gain_ref, w3_ref, w3t_ref, wprojt_ref,
     bias_ref, left_ref, match_ref, rows_out, send_out,
-    xw, gw, standard_ref, cot_ref, query_ref, key_ref, value_ref, mixed_ref, tokens_t_ref,
+    xw, gw, standard_ref, cot_ref, query_ref, key_ref, value_ref, mixed_ref, tokens_ref,
     qkv_t_ref, mixed_t_ref, scores_ref, grad_attend_ref, half_ref, grad_half_ref, dense, dense_left,
-    wsum, psum, gsum, spread, wide, grads, stack,
+    wsum, psum, gsum, spread, outputs_ref, cots_ref, wide, grads, stack,
 ):
     order = window_order(False)
     for a in range(6):
@@ -250,8 +250,6 @@
     lane_head = iota((WIN, C), 1) // HEAD_DIM
     shape = (WIN, MAIN)
     repeat = ones_where((iota(shape, 0) == MAIN + iota(shape, 1) % LEFT) & (iota(shape, 1) < SHARED))
-    shape = (MAIN, WIN)
-    repeat_t = ones_where((iota(shape, 1) == MAIN + iota(shape, 0) % LEFT) & (iota(shape, 0) < SHARED))
     shape = (LEFT, MAIN)
     gather = ones_where((iota(shape, 0) == iota(shape, 1) % LEFT) & (iota(shape, 1) < SHARED))
     own_head_t = iota((C, MAIN), 0) // HEAD_DIM == iota((C, MAIN), 1) // LEFT
@@ -260,16 +258,26 @@
     def of_head(value, h):
         return jnp.where(lane_head[: value.shape[0]] == h, value, jnp.zeros_like(value))
 
-    def stacked(value):
-        return jnp.concatenate([of_head(value, h) for h in range(HEADS)], axis=0)
+    def per_head(columns, left):
+        blocks = []
+        for h in range(HEADS):
+            above = jnp.zeros((h * HEAD_DIM, MAIN), bf16)
+            below = jnp.zeros((C - (h + 1) * HEAD_DIM, MAIN), bf16)
+            own = columns[h * HEAD_DIM : (h + 1) * HEAD_DIM, :MAIN]
+            blocks.append(jnp.concatenate([x for x in (above, own, below) if x.shape[0]], axis=0))
+        return jnp.concatenate(blocks + [only_head(own_head_t, left)], axis=1)
+
+    def repeated(rows):
+        zeros = jnp.zeros((MAIN - SHARED, C), bf16)
+        return jnp.concatenate([rows[MAIN:]] * HEADS + [zeros], axis=0)
 
     def only_head(mask, value):
         return jnp.where(mask, value, jnp.zeros_like(value)).astype(bf16)
 
     standard, _ = normalised(xw[...].reshape(WINDOWS * WIN, C))
     standard_ref[...] = standard
-    scaled = standard * gain
-    tokens = scaled.astype(bf16)
+    tokens = (standard * gain).astype(bf16)
+    tokens_ref[...] = tokens
     cots = gw[...].reshape(WINDOWS * WIN, C).astype(bf16)
     cot_ref[...] = cots
     query_ref[...] = dot(tokens, w3_ref[0]).astype(bf16)
@@ -277,32 +285,27 @@
     value_ref[...] = dot(tokens, w3_ref[2]).astype(bf16)
     mixed_ref[...] = dot(cots, wprojt_ref[...]).astype(bf16)
     for w in range(WINDOWS):
-        tokens_t = scaled[w * WIN : (w + 1) * WIN].T.astype(bf16)
-        tokens_t_ref[w] = tokens_t
-        for k in range(3):
-            part = dot(w3t_ref[k * WIDTH : k * WIDTH + C], tokens_t)
-            qkv_t_ref[w, k * C : (k + 1) * C] = part.astype(bf16)
-        mixed_t_ref[w] = dot(wproj_ref[...], gw[w].T.astype(bf16)).astype(bf16)
+        span = slice(w * WIN, (w + 1) * WIN)
+        for k, ref in enumerate((query_ref, key_ref, value_ref)):
+            qkv_t_ref[w, k * C : (k + 1) * C] = ref[span].T
+        mixed_t_ref[w] = mixed_ref[span].T
 
     for w in range(WINDOWS):
         lz = w // STRIPS
         span = slice(w * WIN, (w + 1) * WIN)
         query_t, mixed_t = qkv_t_ref[w, 0:C], mixed_t_ref[w]
         key, value = key_ref[span], value_ref[span]
-        scores_ref[w, : HEADS * WIN] = dot(stacked(key), query_t[:, :MAIN])
-        scores_ref[w, HEADS * WIN :] = dot(key, only_head(own_head_t, dot(query_t, repeat)))
-        grad_attend_ref[w, : HEADS * WIN] = dot(stacked(value), mixed_t[:, :MAIN])
-        grad_attend_ref[w, HEADS * WIN :] = dot(value, only_head(own_head_t, dot(mixed_t, repeat)))
+        scores_ref[w] = dot(key, per_head(query_t, dot(query_t, repeat)))
+        grad_attend_ref[w] = dot(value, per_head(mixed_t, dot(mixed_t, repeat)))
         for t in range(HEADS + 1):
-            lines = slice(t * WIN, (t + 1) * WIN)
             columns = slice(t * MAIN, (t + 1) * MAIN)
             bias = bias_ref[lz * HEADS + t] if t < HEADS else left_ref[lz]
-            scores = scores_ref[w, lines] * (SCALE * LOG2E) + bias
+            scores = scores_ref[w, :, columns] * (SCALE * LOG2E) + bias
             top = jnp.max(scores, axis=0, keepdims=True)
             powers = jnp.exp2(scores - top)
             attend = powers * (1.0 / jnp.sum(powers, axis=0, keepdims=True))
             half_ref[w, :, columns] = attend.astype(bf16)
-            grad_attend = grad_attend_ref[w, lines]
+            grad_attend = grad_attend_ref[w, :, columns]
             total = jnp.sum(attend * grad_attend, axis=0, keepdims=True)
             grad_scores = attend * (grad_attend - total)
             grad_half_ref[w, :, columns] = grad_scores.astype(bf16)
@@ -327,14 +330,15 @@
 
         def per_key(left_ref, right):
             parts = [of_head(right[:MAIN], h) for h in range(HEADS)]
-            parts.append(only_head(own_head, dot(repeat_t, right)))
+            parts.append(only_head(own_head, repeated(right)))
             return dot(left_ref[w], jnp.concatenate(parts, axis=0))
 
         cot = cot_ref[span]
         out_t, out_left = per_query(qkv_t_ref[w, 2 * C :], half_ref)
-        both = jnp.concatenate([out_t.astype(bf16), out_left.astype(bf16)], axis=1)
-        added = dot(both, jnp.concatenate([cot[:MAIN], dot(repeat_t, cot).astype(bf16)], axis=0))
-        psum[...] = added if w == 0 else psum[...] + added
+        outputs_ref[:, 2 * w * MAIN : (2 * w + 1) * MAIN] = out_t.astype(bf16)
+        outputs_ref[:, (2 * w + 1) * MAIN : 2 * (w + 1) * MAIN] = out_left.astype(bf16)
+        cots_ref[2 * w * MAIN : (2 * w + 1) * MAIN] = cot[:MAIN]
+        cots_ref[(2 * w + 1) * MAIN : 2 * (w + 1) * MAIN] = repeated(cot)
         query_grad, query_left = per_query(qkv_t_ref[w, C : 2 * C], grad_half_ref)
         first = slice(w * WIN, w * WIN + MAIN)
         last = slice(w * WIN + MAIN, (w + 1) * WIN)
@@ -348,9 +352,8 @@
     back = dot(grad_projected, w3t_ref[...]).astype(bf16)
     rows_out[...] = back
     gsum[0:1, :] = jnp.sum(back.astype(f32) * standard_ref[...], axis=0, keepdims=True)
-    for w in range(WINDOWS):
-        added = dot(tokens_t_ref[w], spread[w * WIN : (w + 1) * WIN])
-        wsum[...] = added if w == 0 else wsum[...] + added
+    wsum[...] = dot(tokens_ref[...], grad_projected, TN)
+    psum[...] = dot(outputs_ref[...], cots_ref[...])
 
     total = jnp.zeros((TYPES * 16, PAIRS * 32), f32)
     lane_left = iota((PAIRS, MAIN), 1) // LEFT
@@ -364,9 +367,8 @@
                 picked += [both, jnp.zeros((4, 2 * MAIN), f32)]
         picked = jnp.concatenate(picked, axis=0)
         high = picked.astype(bf16)
-        low = (picked - high.astype(f32)).astype(bf16)
         match = match_ref[oj]
-        total += dot(high, match) + dot(low, match)
+        total += dot(high, match)
     for v in range(3):
         grads[v] = total[:, 128 * v : 128 * (v + 1)]
     wide[...] = jnp.zeros_like(wide)
@@ -414,7 +416,7 @@
             send_out[p, :, last] = jnp.zeros((16, 128), bf16)
 
 
-def main(own, lat_in, lon_in, corner_in, gain, w3, w3t, wproj, wproj_t, bias, bias_left, match):
+def main(own, lat_in, lon_in, corner_in, gain, w3, w3t, wproj_t, bias, bias_left, match):
     vmem = pl.BlockSpec(memory_space=pltpu.VMEM)
     return pl.pallas_call(
         main_kernel,
@@ -422,7 +424,7 @@
             jax.ShapeDtypeStruct((WINDOWS * WIN, C), bf16),
             jax.ShapeDtypeStruct((PARTS, 16, SLOTS * 128), bf16),
         ),
-        in_specs=[vmem] * 12,
+        in_specs=[vmem] * 11,
         out_specs=(vmem,) * 2,
         scratch_shapes=[
             pltpu.VMEM((WINDOWS, WIN, C), f32),
@@ -433,11 +435,11 @@
             pltpu.VMEM((WINDOWS * WIN, C), bf16),
             pltpu.VMEM((WINDOWS * WIN, C), bf16),
             pltpu.VMEM((WINDOWS * WIN, C), bf16),
-            pltpu.VMEM((WINDOWS, C, WIN), bf16),
+            pltpu.VMEM((WINDOWS * WIN, C), bf16),
             pltpu.VMEM((WINDOWS, 3 * C, WIN), bf16),
             pltpu.VMEM((WINDOWS, C, WIN), bf16),
-            pltpu.VMEM((WINDOWS, (HEADS + 1) * WIN, MAIN), f32),
-            pltpu.VMEM((WINDOWS, (HEADS + 1) * WIN, MAIN), f32),
+            pltpu.VMEM((WINDOWS, WIN, (HEADS + 1) * MAIN), f32),
+            pltpu.VMEM((WINDOWS, WIN, (HEADS + 1) * MAIN), f32),
             pltpu.VMEM((WINDOWS, WIN, (HEADS + 1) * MAIN), bf16),
             pltpu.VMEM((WINDOWS, WIN, (HEADS + 1) * MAIN), bf16),
             pltpu.VMEM((TYPES, WIN, MAIN), f32),
@@ -446,6 +448,8 @@
             pltpu.VMEM((C, C), f32),
             pltpu.VMEM((8, C), f32),
             pltpu.VMEM((WINDOWS * WIN, 3 * WIDTH), bf16),
+            pltpu.VMEM((C, 2 * WINDOWS * MAIN), bf16),
+            pltpu.VMEM((2 * WINDOWS * MAIN, C), bf16),
             pltpu.VMEM((16, WIDE), f32),
             pltpu.VMEM((3, TYPES * 16, 128), f32),
             pltpu.VMEM((B_TILES * 16, 128), f32),
@@ -455,7 +459,7 @@
             flops=20_000_000_000, bytes_accessed=4_000_000, transcendentals=750_000
         ),
         name="window_grads",
-    )(own, lat_in, lon_in, corner_in, gain, w3, w3t, wproj, wproj_t, bias, bias_left, match)
+    )(own, lat_in, lon_in, corner_in, gain, w3, w3t, wproj_t, bias, bias_left, match)
 
 
 def pieces_kernel(rows_ref, body_out, tail_out):
@@ -566,31 +570,43 @@
     )(parts)
 
 
-def scattered(send):
-    got = lax.all_to_all(send, GROUP, 0, 0, tiled=True)
-    got = got.reshape((PARTS // LATS, LATS, 16, SLOTS * 128)).astype(f32)
-    shared = jnp.sum(got[..., : 128 * W_SLOTS], axis=(0, 1))
-    last = jnp.sum(got[..., 128 * W_SLOTS :], axis=0)
-    return jnp.concatenate([shared] + [last[n] for n in range(LATS)], axis=1).astype(bf16)
-
-
-def exchanged(mixed):
-    count = lax.axis_size(REST)
-    got = lax.all_to_all(
-        jnp.broadcast_to(mixed[None], (count,) + mixed.shape), REST, 0, 0, tiled=True
-    )
-    total = jnp.sum(got.astype(f32), axis=0)
-    shared = total[:, : 128 * W_SLOTS]
+def fold_kernel(got_ref, out_ref):
+    shared = jnp.zeros((16, 128 * W_SLOTS), f32)
+    last = [jnp.zeros((16, 128), f32)] * LATS
+    for p in range(PARTS):
+        shared += got_ref[p, :, : 128 * W_SLOTS].astype(f32)
+        last[p % LATS] += got_ref[p, :, 128 * W_SLOTS :].astype(f32)
+    total = jnp.concatenate([shared] + last, axis=1).astype(bf16)
+    for n in range(out_ref.shape[0]):
+        out_ref[n] = total
+
+
+def share_kernel(got_ref, out_ref):
+    total = jnp.zeros(got_ref.shape[1:], f32)
+    for n in range(got_ref.shape[0]):
+        total += got_ref[n].astype(f32)
+    shared = total[:, : 128 * W_SLOTS].astype(bf16)
     last = [total[:, 128 * (W_SLOTS + n) : 128 * (W_SLOTS + n + 1)] for n in range(LATS)]
     everywhere = last[0] + last[1] + last[2] + last[3]
     part = lax.axis_index(GROUP)
     per_lat = (part >= B_FIRST) & (part < GAIN_PART)
-    rows = [
-        jnp.concatenate([shared, jnp.where(per_lat, last[n], everywhere)], axis=1).astype(bf16)
-        for n in range(LATS)
-    ]
-    spread = jnp.broadcast_to(jnp.stack(rows)[None], (PARTS // LATS, LATS, 16, SLOTS * 128))
-    return spread.reshape(PARTS, 16, SLOTS * 128)
+    last = [jnp.where(per_lat, one, everywhere).astype(bf16) for one in last]
+    for p in range(PARTS):
+        out_ref[p, :, : 128 * W_SLOTS] = shared
+        out_ref[p, :, 128 * W_SLOTS :] = last[p % LATS]
+
+
+def on_chip(kernel, shape, name):
+    vmem = pl.BlockSpec(memory_space=pltpu.VMEM)
+    return pl.pallas_call(
+        kernel,
+        out_shape=jax.ShapeDtypeStruct(shape, bf16),
+        in_specs=[vmem],
+        out_specs=vmem,
+        compiler_params=pltpu.CompilerParams(vmem_limit_bytes=VMEM_LIMIT),
+        cost_estimate=pl.CostEstimate(flops=1_000_000, bytes_accessed=600_000, transcendentals=0),
+        name=name,
+    )
 
 
 def pack_kernel(x_ref, g_ref, corner_out, lon_out, lat_out, sems):
@@ -641,17 +657,21 @@
     corner_in = lax.ppermute(to_corner, both, corner_down)
     lon_in = lax.ppermute(to_lon, lon_axes, lon_swap)
     lat_in = lax.ppermute(to_lat, lat_axes, lat_down)
-    bias, bias_left, w3, w3t, wproj, wproj_t, own, match, gain = prepare(
+    bias, bias_left, w3, w3t, wproj_t, own, match, gain = prepare(
         bias_table[0].transpose(1, 0, 2), w_qkv, w_proj, ln_gain.reshape(1, C), x, g
     )
     rows, send = main(
-        own, lat_in, lon_in, corner_in, gain, w3, w3t, wproj, wproj_t, bias, bias_left, match
+        own, lat_in, lon_in, corner_in, gain, w3, w3t, wproj_t, bias, bias_left, match
     )
     body, tail = pieces(rows)
     tail = lax.ppermute(tail, lon_axes, lon_swap)
-    mixed, tail = lax.optimization_barrier((scattered(send), tail))
+    got = lax.all_to_all(send, GROUP, 0, 0, tiled=True)
+    mixed = on_chip(fold_kernel, (lax.axis_size(REST), 16, 128 * (W_SLOTS + LATS)), "fold")(got)
+    mixed, tail = lax.optimization_barrier((mixed, tail))
     lat_rows = lax.ppermute(jnp.concatenate([tail[3:], body[3:]], axis=1), lat_axes, lat_up)
-    spread, lat_rows = lax.optimization_barrier((exchanged(mixed), lat_rows))
+    got = lax.all_to_all(mixed, REST, 0, 0, tiled=True)
+    spread = on_chip(share_kernel, send.shape, "share")(got)
+    spread, lat_rows = lax.optimization_barrier((spread, lat_rows))
     parts = lax.all_to_all(spread, GROUP, 0, 0, tiled=True)
     grad_gain, grad_wqkv, grad_wproj, grad_bias = unpack(parts)
     grad_x = norm_grads(x, g, gain, body, tail, lat_rows)

time: 79.6 us -> 76.3 us (0.959)
  waiting for transfers between devices: 23.9 us -> 26.9 us
  Pallas kernels: 20.7 us -> 18.4 us
  starting transfers between devices: 31.9 us -> 29.8 us
  local copies, waits for them, and re-layouts: 1.55 us -> 0.03 us
    pallas_call x1, Pallas kernels: 12.5 us -> 8.74 us  [main(): pl.pallas_call(main_kernel, out_shape=(jax.ShapeDtypeStruct((WINDOWS * WI...]
    ppermute x1, starting transfers between devices: 3.32 us -> 0.01 us  [on_device(): lat_in = lax.ppermute(to_lat, lat_axes, lat_down)]
    ppermute x1, waiting for transfers between devices: 0.01 us -> 2.98 us  [on_device(): lat_in = lax.ppermute(to_lat, lat_axes, lat_down)]
    ppermute x1, starting transfers between devices: 1.01 us -> 3.66 us  [on_device(): lon_in = lax.ppermute(to_lon, lon_axes, lon_swap)]
    all_to_all x2, starting transfers between devices: 15.6 us -> 13.6 us  [the longest x1 8.18 us: on_device(): got = lax.all_to_all(mixed, REST, 0, 0, tiled=True)]
    pallas_call x0 -> x2, Pallas kernels: none -> 1.53 us  [the longest x1 0.79 us: on_device(): spread = on_chip(share_kernel, send.shape, 'share')(got)]
    broadcast_in_dim x2 -> x0, local copies, waits for them, and re-layouts: 1.47 us -> none  [the longest x1 0.78 us: exchanged(): jnp.broadcast_to(jnp.stack(rows)[None], (PARTS // LATS, LATS, 16, SLOTS *...]
  transfers between devices with their start and end apart: 8 -> 8, of which waited for: 3 -> 4; matrix products, arithmetic and copies ran while one was open for 0% -> 0% of each run, Pallas kernels for 8% -> 10%
where the time goes in v6:
time: 76.3 us; the launch traced here: 75.9 us
  starting transfers between devices  29.8 us (39%)
  waiting for transfers between devices  26.9 us (35%)
  Pallas kernels  18.4 us (24%)
    pallas_call x1, Pallas kernels, main(): pl.pallas_call(main_kernel, out_shape=(jax.ShapeDtypeStruct((WINDOWS * WI...  8.74 us
    all_to_all x1, waiting for transfers between devices, on_device(): got = lax.all_to_all(mixed, REST, 0, 0, tiled=True)  8.65 us
    all_to_all x1, waiting for transfers between devices, on_device(): parts = lax.all_to_all(spread, GROUP, 0, 0, tiled=True)  8.29 us
    all_to_all x1, starting transfers between devices, on_device(): got = lax.all_to_all(mixed, REST, 0, 0, tiled=True)  8.18 us
    all_to_all x1, waiting for transfers between devices, on_device(): got = lax.all_to_all(send, GROUP, 0, 0, tiled=True)  6.97 us
    all_to_all x1, starting transfers between devices, on_device(): parts = lax.all_to_all(spread, GROUP, 0, 0, tiled=True)  5.85 us
    all_to_all x1, starting transfers between devices, on_device(): got = lax.all_to_all(send, GROUP, 0, 0, tiled=True)  5.47 us
    pallas_call x1, Pallas kernels, prepare(): pl.pallas_call(prepare_kernel, out_shape=(jax.ShapeDtypeStruct((TYPES, WI...  3.92 us
  transfers between devices with their start and end apart: 8, of which 4 were waited for; matrix products, arithmetic and copies ran while one was open for 0% of the time, Pallas kernels for 10%

profile of v6, /device:TPU:1, one launch (start us, length us, event | category | flops | bytes accessed | tf_op | source)
XLA Modules:
  0.0 75.9 jit_solution(10076146321982901803)
XLA Ops:
  0.6 1.1 %pack.1 = (bf16[2,3,6,4,192]{4,3,2,1,0:T(4,128)(2,1)S(1)}, bf16[2,3,6,4,192]{4,3,2,1,0:T(4,128)(2,1)S(1)}, bf16[2,3,30,4,192]{4,3,2,1,0:T(4,128)(2,1)S(1)}) custom-call(bf16[6,36,4,192]{3,2,1,0:T(4,128)(2,1)} %bitcast.11, bf16[6,36,4,192]{3,2,1,0:T(4,128)(2,1)} %bitcast.14), custom_call_target="tpu_custom_call" | custom-call | tf_op jit(solution)/shard_map/pack/pallas_call | solution.py:631
  1.8 3.7 %collective-permute-start.1 = (bf16[2,3,6,4,192]{4,3,2,1,0:T(4,128)(2,1)S(1)}, bf16[2,3,6,4,192]{4,3,2,1,0:T(4,128)(2,1)S(1)}, u32[]{:S(2)}, u32[]{:S(2)}) collective-permute-start(bf16[2,3,6,4,192]{4,3,2,1,0:T(4,128)(2,1)S(1)} %get-tuple-element.31), channel_id=1, source_target_pairs={{0,4},{4,0},{8,12},{12,8},{16,20},{20,16},{24,28},{28,24},{32,36},... | collective-permute-start | bytes 165896 | tf_op jit(solution)/shard_map/ppermute | solution.py:658
  5.4 2.8 %collective-permute-start.2 = (bf16[2,3,6,4,192]{4,3,2,1,0:T(4,128)(2,1)S(1)}, bf16[2,3,6,4,192]{4,3,2,1,0:T(4,128)(2,1)S(1)}, u32[]{:S(2)}, u32[]{:S(2)}) collective-permute-start(bf16[2,3,6,4,192]{4,3,2,1,0:T(4,128)(2,1)S(1)} %get-tuple-element.32), channel_id=1, source_target_pairs={{0,7},{1,4},{2,5},{3,6},{4,3},{5,0},{6,1},{7,2},{8,15},{9,12},{10,... | collective-permute-start | bytes 165896 | tf_op jit(solution)/shard_map/ppermute | solution.py:657
  8.2 0.0 collective-permute-start
  8.3 3.9 %prepare.1 = (f32[12,144,128]{2,1,0:T(8,128)S(1)}, f32[2,144,128]{2,1,0:T(8,128)S(1)}, bf16[3,192,192]{2,1,0:T(8,128)(2,1)S(1)}, bf16[768,192]{1,0:T(8,128)(2,1)...) custom-call(f32[6,2,3312]{2,1,0:T(2,128)} %bitcast.18, ...), custom_call_target="tpu_custom_call" | custom-call | flops 4000000000 | bytes 4000000 | tf_op jit(solution)/shard_map/prepare/pallas_call | solution.py:183
  12.2 0.0 collective-permute-done.1.lon_ref
  12.2 0.0 collective-permute-done.2.corner_ref
  12.2 3.0 %collective-permute-done.lat_ref = bf16[2,3,30,4,192]{4,3,2,1,0:T(4,128)(2,1)S(1)} collective-permute-done((bf16[2,3,30,4,192]{4,3,2,1,0:T(4,128)(2,1)S(1)}, bf16[2,3,30,4,192]{4,3,2,1,0:T(4,128)(2,1)S(1)}, u32[]{:S(2)}, u32[]{:S(2)}) %collective-permute-start) | collective-permute-done | bytes 276512 | tf_op jit(solution)/shard_map/ppermute | solution.py:659
  15.2 8.7 %window_grads.1 = (bf16[864,192]{1,0:T(8,128)(2,1)S(1)}, bf16[32,16,384]{2,1,0:T(8,128)(2,1)}) custom-call(bf16[2,3,120,192]{3,2,1,0:T(8,128)(2,1)S(1)} %get-tuple-element.29.own_ref, bf16[2,3,30,4,192]{4,3,2,1,0:T(4,128)(2,1)S(1)} %collective-permute-done.lat_ref, bf16[2,3,6,4,192]{4,3,2,1,0:T(4,128)(2,1)S(1)} %collective-permute-done.1.lon_ref, ...), custom_call_target="tpu_custom_call" | custom-call | flops 20000000000 | bytes 4000000 | tf_op jit(solution)/shard_map/window_grads/pallas_call | solution.py:421
  23.9 5.5 %all-to-all-start = ((bf16[32,16,384]{2,1,0:T(8,128)(2,1)}), bf16[32,16,384]{2,1,0:T(8,128)(2,1)S(1)}, u32[]{:S(2)}, u32[]{:S(2)}) async-start(bf16[32,16,384]{2,1,0:T(8,128)(2,1)} %get-tuple-element.41), calls=%async_computation | async-start | bytes 786432 | tf_op jit(solution)/shard_map/all_to_all | solution.py:668
  29.4 0.0 copy-start
  29.4 0.0 copy-start.1
  29.4 0.3 pieces.1
  29.7 3.0 %collective-permute-start.3 = (bf16[6,24,192]{2,1,0:T(8,128)(2,1)S(1)}, bf16[6,24,192]{2,1,0:T(8,128)(2,1)S(1)}, u32[]{:S(2)}, u32[]{:S(2)}) collective-permute-start(bf16[6,24,192]{2,1,0:T(8,128)(2,1)S(1)} %get-tuple-element.42), channel_id=1, source_target_pairs={{0,4},{4,0},{8,12},{12,8},{16,20},{20,16},{24,28},{28,24},{32,36},... | collective-permute-start | bytes 165896 | tf_op jit(solution)/shard_map/ppermute | solution.py:667
  32.7 7.0 %all-to-all-done.got_ref = bf16[32,16,384]{2,1,0:T(8,128)(2,1)S(1)} async-done(((bf16[32,16,384]{2,1,0:T(8,128)(2,1)}), bf16[32,16,384]{2,1,0:T(8,128)(2,1)S(1)}, u32[]{:S(2)}, u32[]{:S(2)}) %all-to-all-start) | async-done | bytes 393248 | tf_op jit(solution)/shard_map/all_to_all | solution.py:668
  39.7 0.7 fold.1
  40.4 0.0 collective-permute-done.3.tail_ref
  40.4 8.2 %all-to-all-start.1 = ((bf16[8,16,768]{2,1,0:T(8,128)(2,1)}), bf16[8,16,768]{2,1,0:T(8,128)(2,1)S(1)}, u32[]{:S(2)}, u32[]{:S(2)}) async-start(bf16[8,16,768]{2,1,0:T(8,128)(2,1)} %fold.1), calls=%async_computation.1 | async-start | bytes 393216 | tf_op jit(solution)/shard_map/all_to_all | solution.py:672
  48.6 0.8 %collective-permute-start.4 = (bf16[3,144,192]{2,1,0:T(8,128)(2,1)S(1)}, bf16[3,144,192]{2,1,0:T(8,128)(2,1)S(1)}, u32[]{:S(2)}, u32[]{:S(2)}) collective-permute-start(bf16[3,144,192]{2,1,0:T(8,128)(2,1)S(1)} %pad_maximum_fusion), channel_id=1, source_target_pairs={{0,1},{1,2},{2,3},{3,0},{4,5},{5,6},{6,7},{7,4},{8,9},{9,10},{10,1... | collective-permute-start | bytes 497672 | tf_op jit(solution)/shard_map/ppermute | solution.py:671
  49.5 8.7 %all-to-all-done.1.got_ref = bf16[8,16,768]{2,1,0:T(8,128)(2,1)S(1)} async-done(((bf16[8,16,768]{2,1,0:T(8,128)(2,1)}), bf16[8,16,768]{2,1,0:T(8,128)(2,1)S(1)}, u32[]{:S(2)}, u32[]{:S(2)}) %all-to-all-start.1) | async-done | bytes 196640 | tf_op jit(solution)/shard_map/all_to_all | solution.py:672
  58.1 0.8 %share.1 = bf16[32,16,384]{2,1,0:T(8,128)(2,1)} custom-call(bf16[8,16,768]{2,1,0:T(8,128)(2,1)S(1)} %all-to-all-done.1.got_ref), custom_call_target="tpu_custom_call" | custom-call | flops 1000000 | bytes 600000 | tf_op jit(solution)/shard_map/share/pallas_call | solution.py:673
  58.9 0.0 collective-permute-done.4.lat_ref
  58.9 5.9 %all-to-all-start.2 = ((bf16[32,16,384]{2,1,0:T(8,128)(2,1)}), bf16[32,16,384]{2,1,0:T(8,128)(2,1)S(1)}, u32[]{:S(2)}, u32[]{:S(2)}) async-start(bf16[32,16,384]{2,1,0:T(8,128)(2,1)} %share.1), calls=%async_computation.2 | async-start | bytes 786432 | tf_op jit(solution)/shard_map/all_to_all | solution.py:675
  64.8 0.0 copy-done
  64.8 0.0 copy-done.1
  64.8 1.9 %norm_grads.1 = bf16[6,36,4,192]{3,2,1,0:T(4,128)(2,1)} custom-call(bf16[6,36,4,192]{3,2,1,0:T(4,128)(2,1)S(1)} %bitcast.13, bf16[6,36,4,192]{3,2,1,0:T(4,128)(2,1)S(1)} %bitcast.16, f32[1,192]{1,0:T(1,128)S(1)} %get-tuple-element.28.gain_ref, bf16[6,120,192]{2,1,0:T(8,128)(2,1)S(1)} %get-tuple-element.40.body_ref, ...), custom_call_target="tpu_custom_call" | custom-call | flops 10000000 | bytes 1500000 | tf_op jit(solution)/shard_map/norm_grads/pallas_call | solution.py:515
  66.7 8.3 %all-to-all-done.2.parts_ref = bf16[32,16,384]{2,1,0:T(8,128)(2,1)S(1)} async-done(((bf16[32,16,384]{2,1,0:T(8,128)(2,1)}), bf16[32,16,384]{2,1,0:T(8,128)(2,1)S(1)}, u32[]{:S(2)}, u32[]{:S(2)}) %all-to-all-start.2) | async-done | bytes 393248 | tf_op jit(solution)/shard_map/all_to_all | solution.py:675
  75.0 0.9 %unpack.1 = (f32[1,192]{1,0:T(1,128)}, f32[192,576]{1,0:T(8,128)}, f32[192,192]{1,0:T(8,128)}, f32[6,2,3312]{2,1,0:T(2,128)}) custom-call(bf16[32,16,384]{2,1,0:T(8,128)(2,1)S(1)} %all-to-all-done.2.parts_ref), custom_call_target="tpu_custom_call" | custom-call | tf_op jit(solution)/shard_map/unpack/pallas_call | solution.py:557
  (3 shorter events, 0.1 us)
Async XLA Ops:
  1.8 10.4 %collective-permute-start.1 = (bf16[2,3,6,4,192]{4,3,2,1,0:T(4,128)(2,1)S(1)}, bf16[2,3,6,4,192]{4,3,2,1,0:T(4,128)(2,1)S(1)}, u32[]{:S(2)}, u32[]{:S(2)}) collective-permute-start(bf16[2,3,6,4,192]{4,3,2,1,0:T(4,128)(2,1)S(1)} %get-tuple-element.31), channel_id=1, source_target_pairs={{0,4},{4,0},{8,12},{12,8},{16,20},{20,16},{24,28},{28,24},{32,36},... | collective-permute-start | bytes 165896 | tf_op jit(solution)/shard_map/ppermute | solution.py:658
  5.4 6.8 %collective-permute-start.2 = (bf16[2,3,6,4,192]{4,3,2,1,0:T(4,128)(2,1)S(1)}, bf16[2,3,6,4,192]{4,3,2,1,0:T(4,128)(2,1)S(1)}, u32[]{:S(2)}, u32[]{:S(2)}) collective-permute-start(bf16[2,3,6,4,192]{4,3,2,1,0:T(4,128)(2,1)S(1)} %get-tuple-element.32), channel_id=1, source_target_pairs={{0,7},{1,4},{2,5},{3,6},{4,3},{5,0},{6,1},{7,2},{8,15},{9,12},{10,... | collective-permute-start | bytes 165896 | tf_op jit(solution)/shard_map/ppermute | solution.py:657
  8.2 6.9 %collective-permute-start = (bf16[2,3,30,4,192]{4,3,2,1,0:T(4,128)(2,1)S(1)}, bf16[2,3,30,4,192]{4,3,2,1,0:T(4,128)(2,1)S(1)}, u32[]{:S(2)}, u32[]{:S(2)}) collective-permute-start(bf16[2,3,30,4,192]{4,3,2,1,0:T(4,128)(2,1)S(1)} %get-tuple-element.30), channel_id=1, source_target_pairs={{0,3},{1,0},{2,1},{3,2},{4,7},{5,4},{6,5},{7,6},{8,11},{9,8},{10,9... | collective-permute-start | bytes 829448 | tf_op jit(solution)/shard_map/ppermute | solution.py:659
  23.9 15.7 %all-to-all-start = ((bf16[32,16,384]{2,1,0:T(8,128)(2,1)}), bf16[32,16,384]{2,1,0:T(8,128)(2,1)S(1)}, u32[]{:S(2)}, u32[]{:S(2)}) async-start(bf16[32,16,384]{2,1,0:T(8,128)(2,1)} %get-tuple-element.41), calls=%async_computation | async-start | bytes 786432 | tf_op jit(solution)/shard_map/all_to_all | solution.py:668
  29.4 35.4 %copy-start = (bf16[4,6,36,192]{3,0,2,1:T(4,128)(2,1)S(1)}, bf16[4,6,36,192]{3,0,2,1:T(4,128)(2,1)}, u32[]{:S(2)}) copy-start(bf16[4,6,36,192]{3,0,2,1:T(4,128)(2,1)} %param.6) | copy-start | bytes 995332
  29.4 35.4 %copy-start.1 = (bf16[4,6,36,192]{3,0,2,1:T(4,128)(2,1)S(1)}, bf16[4,6,36,192]{3,0,2,1:T(4,128)(2,1)}, u32[]{:S(2)}) copy-start(bf16[4,6,36,192]{3,0,2,1:T(4,128)(2,1)} %param.7) | copy-start | bytes 995332
  29.7 10.7 %collective-permute-start.3 = (bf16[6,24,192]{2,1,0:T(8,128)(2,1)S(1)}, bf16[6,24,192]{2,1,0:T(8,128)(2,1)S(1)}, u32[]{:S(2)}, u32[]{:S(2)}) collective-permute-start(bf16[6,24,192]{2,1,0:T(8,128)(2,1)S(1)} %get-tuple-element.42), channel_id=1, source_target_pairs={{0,4},{4,0},{8,12},{12,8},{16,20},{20,16},{24,28},{28,24},{32,36},... | collective-permute-start | bytes 165896 | tf_op jit(solution)/shard_map/ppermute | solution.py:667
  40.4 17.7 %all-to-all-start.1 = ((bf16[8,16,768]{2,1,0:T(8,128)(2,1)}), bf16[8,16,768]{2,1,0:T(8,128)(2,1)S(1)}, u32[]{:S(2)}, u32[]{:S(2)}) async-start(bf16[8,16,768]{2,1,0:T(8,128)(2,1)} %fold.1), calls=%async_computation.1 | async-start | bytes 393216 | tf_op jit(solution)/shard_map/all_to_all | solution.py:672
  48.6 10.3 %collective-permute-start.4 = (bf16[3,144,192]{2,1,0:T(8,128)(2,1)S(1)}, bf16[3,144,192]{2,1,0:T(8,128)(2,1)S(1)}, u32[]{:S(2)}, u32[]{:S(2)}) collective-permute-start(bf16[3,144,192]{2,1,0:T(8,128)(2,1)S(1)} %pad_maximum_fusion), channel_id=1, source_target_pairs={{0,1},{1,2},{2,3},{3,0},{4,5},{5,6},{6,7},{7,4},{8,9},{9,10},{10,1... | collective-permute-start | bytes 497672 | tf_op jit(solution)/shard_map/ppermute | solution.py:671
  58.9 16.0 %all-to-all-start.2 = ((bf16[32,16,384]{2,1,0:T(8,128)(2,1)}), bf16[32,16,384]{2,1,0:T(8,128)(2,1)S(1)}, u32[]{:S(2)}, u32[]{:S(2)}) async-start(bf16[32,16,384]{2,1,0:T(8,128)(2,1)} %share.1), calls=%async_computation.2 | async-start | bytes 786432 | tf_op jit(solution)/shard_map/all_to_all | solution.py:675

commit v7 on v6

--- a/solution.py
+++ b/solution.py
@@ -117,8 +117,7 @@
         w3t_ref[k * WIDTH + C : (k + 1) * WIDTH] = jnp.zeros((WIDTH - C, C), bf16)
     wprojt_ref[...] = wproj_ref[...].T
     for a in range(3):
-        for k in range(2):
-            own_ref[k, a] = mine[k, a].reshape(BODY, C)
+        own_ref[a] = side_by_side(mine, a)
     wide[...] = jnp.zeros_like(wide)
     for h in range(HEADS):
         for lz in range(2):
@@ -188,7 +187,7 @@
             jax.ShapeDtypeStruct((3, C, C), bf16),
             jax.ShapeDtypeStruct((3 * WIDTH, C), bf16),
             jax.ShapeDtypeStruct((C, C), bf16),
-            jax.ShapeDtypeStruct((2, 3, BODY, C), bf16),
+            jax.ShapeDtypeStruct((3, BODY, 2 * C), bf16),
             jax.ShapeDtypeStruct((WLON, 2 * MAIN, PAIRS * 32), bf16),
             jax.ShapeDtypeStruct((1, C), f32),
         ),
@@ -226,22 +225,19 @@
 
 def main_kernel(
     own_ref, lat_ref, lon_ref, corner_ref, gain_ref, w3_ref, w3t_ref, wprojt_ref,
-    bias_ref, left_ref, match_ref, rows_out, send_out,
+    bias_ref, left_ref, match_ref, rows_out, send_hbm,
     xw, gw, standard_ref, cot_ref, query_ref, key_ref, value_ref, mixed_ref, tokens_ref,
     qkv_t_ref, mixed_t_ref, scores_ref, grad_attend_ref, half_ref, grad_half_ref, dense, dense_left,
     wsum, psum, gsum, spread, outputs_ref, cots_ref, wide, grads, stack,
+    send_shared, send_last, sems,
 ):
     order = window_order(False)
     for a in range(6):
-        for k, to in enumerate((xw, gw)):
-            if a < 3:
-                body, tail = own_ref[k, a], lon_ref[k, a].reshape(TAIL, C)
-            else:
-                body = lat_ref[k, a - 3].reshape(BODY, C)
-                tail = corner_ref[k, a - 3].reshape(TAIL, C)
-            line = dot(order[:, :BODY], body) + dot(order[:, BODY:], tail)
-            for w in range(WINDOWS):
-                to[w, 24 * a : 24 * a + 24, :] = line[24 * w : 24 * w + 24]
+        body, tail = (own_ref[a], lon_ref[a]) if a < 3 else (lat_ref[a - 3], corner_ref[a - 3])
+        line = dot(order[:, :BODY], body) + dot(order[:, BODY:], tail)
+        for w in range(WINDOWS):
+            xw[w, 24 * a : 24 * a + 24, :] = line[24 * w : 24 * w + 24, :C]
+            gw[w, 24 * a : 24 * a + 24, :] = line[24 * w : 24 * w + 24, C:]
     dense[...] = jnp.zeros_like(dense)
     dense_left[...] = jnp.zeros_like(dense_left)
     gsum[...] = jnp.zeros_like(gsum)
@@ -354,6 +350,22 @@
     gsum[0:1, :] = jnp.sum(back.astype(f32) * standard_ref[...], axis=0, keepdims=True)
     wsum[...] = dot(tokens_ref[...], grad_projected, TN)
     psum[...] = dot(outputs_ref[...], cots_ref[...])
+
+    weights = jnp.concatenate(
+        [wsum[:, k * WIDTH : k * WIDTH + C] for k in range(3)] + [psum[...]], axis=1
+    )
+    for t in range(W_TILES):
+        row, column = divmod(t, 6)
+        tile = weights[16 * row : 16 * row + 16, 128 * column : 128 * column + 128]
+        p, slot = w_place(t)
+        if slot < W_SLOTS:
+            send_shared[p, :, 128 * slot : 128 * slot + 128] = tile.astype(bf16)
+        else:
+            send_last[p] = tile.astype(bf16)
+    shared_copy = pltpu.make_async_copy(
+        send_shared, send_hbm.at[:, :, pl.ds(0, 128 * W_SLOTS)], sems.at[0]
+    )
+    shared_copy.start()
 
     total = jnp.zeros((TYPES * 16, PAIRS * 32), f32)
     lane_left = iota((PAIRS, MAIN), 1) // LEFT
@@ -391,29 +403,26 @@
                 target = (slice(0, TYPES), slice(base, base + width))
                 wide[target] = jnp.where(inside, piece, wide[target])
 
-    weights = jnp.concatenate(
-        [wsum[:, k * WIDTH : k * WIDTH + C] for k in range(3)] + [psum[...]], axis=1
-    )
-    for t in range(W_TILES):
-        row, column = divmod(t, 6)
-        tile = weights[16 * row : 16 * row + 16, 128 * column : 128 * column + 128]
-        p, slot = w_place(t)
-        send_out[p, :, 128 * slot : 128 * slot + 128] = tile.astype(bf16)
     stack[...] = jnp.zeros_like(stack)
     for n in range(B_COLUMNS):
         stack[TYPES * n : TYPES * (n + 1), :] = wide[:TYPES, 128 * n : 128 * (n + 1)]
-    last = slice(128 * W_SLOTS, 128 * SLOTS)
     for n in range(B_TILES):
-        send_out[B_FIRST + n, :, last] = stack[16 * n : 16 * n + 16, :].astype(bf16)
+        send_last[B_FIRST + n] = stack[16 * n : 16 * n + 16, :].astype(bf16)
     for p in range(GAIN_PART, PARTS):
         if p == GAIN_PART:
             line = gsum[0:1, :]
             gains = jnp.concatenate([line[:, :128], jnp.zeros((7, 128), f32)], axis=0)
             more = jnp.concatenate([line[:, 128:], jnp.zeros((1, 256 - C), f32)], axis=1)
             more = jnp.concatenate([more, jnp.zeros((7, 128), f32)], axis=0)
-            send_out[p, :, last] = jnp.concatenate([gains, more], axis=0).astype(bf16)
+            send_last[p] = jnp.concatenate([gains, more], axis=0).astype(bf16)
         else:
-            send_out[p, :, last] = jnp.zeros((16, 128), bf16)
+            send_last[p] = jnp.zeros((16, 128), bf16)
+    second = pltpu.make_async_copy(
+        send_last, send_hbm.at[:, :, pl.ds(128 * W_SLOTS, 128)], sems.at[1]
+    )
+    second.start()
+    shared_copy.wait()
+    second.wait()
 
 
 def main(own, lat_in, lon_in, corner_in, gain, w3, w3t, wproj_t, bias, bias_left, match):
@@ -425,7 +434,7 @@
             jax.ShapeDtypeStruct((PARTS, 16, SLOTS * 128), bf16),
         ),
         in_specs=[vmem] * 11,
-        out_specs=(vmem,) * 2,
+        out_specs=(vmem, pl.BlockSpec(memory_space=pltpu.HBM)),
         scratch_shapes=[
             pltpu.VMEM((WINDOWS, WIN, C), f32),
             pltpu.VMEM((WINDOWS, WIN, C), f32),
@@ -453,6 +462,9 @@
             pltpu.VMEM((16, WIDE), f32),
             pltpu.VMEM((3, TYPES * 16, 128), f32),
             pltpu.VMEM((B_TILES * 16, 128), f32),
+            pltpu.VMEM((PARTS, 16, 128 * W_SLOTS), bf16),
+            pltpu.VMEM((PARTS, 16, 128), bf16),
+            pltpu.SemaphoreType.DMA((2,)),
         ],
         compiler_params=pltpu.CompilerParams(vmem_limit_bytes=VMEM_LIMIT),
         cost_estimate=pl.CostEstimate(
@@ -462,15 +474,18 @@
     )(own, lat_in, lon_in, corner_in, gain, w3, w3t, wproj_t, bias, bias_left, match)
 
 
-def pieces_kernel(rows_ref, body_out, tail_out):
+def pieces_kernel(rows_ref, own_out, lat_out, lon_out, corner_out):
     order_t = window_order(True)
     for a in range(6):
         line = jnp.concatenate(
             [rows_ref[WIN * w + 24 * a : WIN * w + 24 * a + 24, :] for w in range(WINDOWS)], axis=0
         )
         line = dot(order_t, line)
-        body_out[a] = line[:BODY].astype(bf16)
-        tail_out[a] = line[BODY:].astype(bf16)
+        body, tail = line[:BODY].astype(bf16), line[BODY:].astype(bf16)
+        if a < 3:
+            own_out[a], lon_out[a] = body, tail
+        else:
+            lat_out[a - 3], corner_out[a - 3] = body, tail
 
 
 def pieces(rows):
@@ -478,11 +493,13 @@
     return pl.pallas_call(
         pieces_kernel,
         out_shape=(
-            jax.ShapeDtypeStruct((6, BODY, C), bf16),
-            jax.ShapeDtypeStruct((6, TAIL, C), bf16),
+            jax.ShapeDtypeStruct((3, BODY, C), bf16),
+            jax.ShapeDtypeStruct((3, BODY, C), bf16),
+            jax.ShapeDtypeStruct((3, TAIL, C), bf16),
+            jax.ShapeDtypeStruct((3, TAIL, C), bf16),
         ),
         in_specs=[vmem],
-        out_specs=(vmem,) * 2,
+        out_specs=(vmem,) * 4,
         compiler_params=pltpu.CompilerParams(vmem_limit_bytes=VMEM_LIMIT),
         cost_estimate=pl.CostEstimate(
             flops=500_000_000, bytes_accessed=700_000, transcendentals=0
@@ -491,14 +508,14 @@
     )(rows)
 
 
-def norm_kernel(x_ref, g_ref, gain_ref, body_ref, tail_ref, lat_ref, out_ref):
+def norm_kernel(x_ref, g_ref, gain_ref, own_ref, lat_ref, lon_ref, corner_ref, out_ref):
     gain = gain_ref[...]
     for a in range(6):
         if a < 3:
-            grad = lat_ref[a].astype(f32)
+            head, body = corner_ref[a], lat_ref[a]
         else:
-            grad = [tail_ref[a - 3].astype(f32), body_ref[a - 3].astype(f32)]
-            grad = jnp.concatenate(grad, axis=0)
+            head, body = lon_ref[a - 3], own_ref[a - 3]
+        grad = jnp.concatenate([head.astype(f32), body.astype(f32)], axis=0)
         standard, inverse = normalised(x_ref[a].reshape(WIN, C).astype(f32))
         scaled = grad * gain
         local = inverse * (
@@ -510,19 +527,19 @@
         out_ref[a] = total.reshape(36, 4, C)
 
 
-def norm_grads(x, g, gain, body, tail, lat_in):
+def norm_grads(x, g, gain, own, lat_in, lon_in, corner_in):
     vmem = pl.BlockSpec(memory_space=pltpu.VMEM)
     return pl.pallas_call(
         norm_kernel,
         out_shape=jax.ShapeDtypeStruct(x.shape, bf16),
-        in_specs=[vmem] * 6,
+        in_specs=[vmem] * 7,
         out_specs=vmem,
         compiler_params=pltpu.CompilerParams(vmem_limit_bytes=VMEM_LIMIT),
         cost_estimate=pl.CostEstimate(
             flops=10_000_000, bytes_accessed=1_500_000, transcendentals=1000
         ),
         name="norm_grads",
-    )(x, g, gain, body, tail, lat_in)
+    )(x, g, gain, own, lat_in, lon_in, corner_in)
 
 
 def unpack_kernel(parts_ref, gain_out, wqkv_out, wproj_out, bias_out, stack):
@@ -575,7 +592,7 @@
     last = [jnp.zeros((16, 128), f32)] * LATS
     for p in range(PARTS):
         shared += got_ref[p, :, : 128 * W_SLOTS].astype(f32)
-        last[p % LATS] += got_ref[p, :, 128 * W_SLOTS :].astype(f32)
+        last[LATS - 1 - p % LATS] += got_ref[p, :, 128 * W_SLOTS :].astype(f32)
     total = jnp.concatenate([shared] + last, axis=1).astype(bf16)
     for n in range(out_ref.shape[0]):
         out_ref[n] = total
@@ -588,12 +605,12 @@
     shared = total[:, : 128 * W_SLOTS].astype(bf16)
     last = [total[:, 128 * (W_SLOTS + n) : 128 * (W_SLOTS + n + 1)] for n in range(LATS)]
     everywhere = last[0] + last[1] + last[2] + last[3]
-    part = lax.axis_index(GROUP)
+    part = PARTS - 1 - lax.axis_index(GROUP)
     per_lat = (part >= B_FIRST) & (part < GAIN_PART)
     last = [jnp.where(per_lat, one, everywhere).astype(bf16) for one in last]
     for p in range(PARTS):
         out_ref[p, :, : 128 * W_SLOTS] = shared
-        out_ref[p, :, 128 * W_SLOTS :] = last[p % LATS]
+        out_ref[p, :, 128 * W_SLOTS :] = last[LATS - 1 - p % LATS]
 
 
 def on_chip(kernel, shape, name):
@@ -609,21 +626,28 @@
     )
 
 
-def pack_kernel(x_ref, g_ref, corner_out, lon_out, lat_out, sems):
+def pack_kernel(x_hbm, g_hbm, corner_out, lon_out, lat_out, corner, lon, lat, sems):
+    places = (
+        (pl.ds(0, 3), pl.ds(6, 30), lat, lat_out),
+        (pl.ds(0, 3), pl.ds(0, 6), corner, corner_out),
+        (pl.ds(3, 3), pl.ds(0, 6), lon, lon_out),
+    )
     copies = []
-    for k, ref in enumerate((x_ref, g_ref)):
-        for n, (source, to) in enumerate(
-            (
-                (ref.at[pl.ds(0, 3), pl.ds(0, 6)], corner_out),
-                (ref.at[pl.ds(3, 3), pl.ds(0, 6)], lon_out),
-                (ref.at[pl.ds(0, 3), pl.ds(6, 30)], lat_out),
-            )
-        ):
-            copies.append(pltpu.make_async_copy(source, to.at[k], sems.at[3 * k + n]))
+    for n, (a, b, to, _) in enumerate(places):
+        for k, array in enumerate((x_hbm, g_hbm)):
+            copies.append(pltpu.make_async_copy(array.at[a, b], to.at[k], sems.at[2 * n + k]))
     for copy in copies:
         copy.start()
-    for copy in copies:
-        copy.wait()
+    for n, (_, _, held, out) in enumerate(places):
+        copies[2 * n].wait()
+        copies[2 * n + 1].wait()
+        for a in range(3):
+            out[a] = side_by_side(held, a)
+
+
+def side_by_side(held, a):
+    rows = held.shape[2] * 4
+    return jnp.concatenate([held[k, a].reshape(rows, C) for k in range(2)], axis=1)
 
 
 def pack(x, g):
@@ -631,16 +655,26 @@
     return pl.pallas_call(
         pack_kernel,
         out_shape=(
-            jax.ShapeDtypeStruct((2, 3, 6, 4, C), bf16),
-            jax.ShapeDtypeStruct((2, 3, 6, 4, C), bf16),
-            jax.ShapeDtypeStruct((2, 3, 30, 4, C), bf16),
+            jax.ShapeDtypeStruct((3, TAIL, 2 * C), bf16),
+            jax.ShapeDtypeStruct((3, TAIL, 2 * C), bf16),
+            jax.ShapeDtypeStruct((3, BODY, 2 * C), bf16),
         ),
         in_specs=[pl.BlockSpec(memory_space=pltpu.HBM)] * 2,
         out_specs=(vmem,) * 3,
-        scratch_shapes=[pltpu.SemaphoreType.DMA((6,))],
+        scratch_shapes=[
+            pltpu.VMEM((2, 3, 6, 4, C), bf16),
+            pltpu.VMEM((2, 3, 6, 4, C), bf16),
+            pltpu.VMEM((2, 3, 30, 4, C), bf16),
+            pltpu.SemaphoreType.DMA((6,)),
+        ],
         compiler_params=pltpu.CompilerParams(vmem_limit_bytes=VMEM_LIMIT),
         name="pack",
     )(in_hbm(x), in_hbm(g))
+
+
+def exchange(blocks, axes):
+    order = [list(reversed(range(blocks.shape[0])))]
+    return lax.all_to_all(blocks, axes, 0, 0, tiled=True, axis_index_groups=order)
 
 
 def on_device(x, g, ln_gain, w_qkv, w_proj, bias_table):
@@ -650,6 +684,7 @@
     lon_swap = [(i, i ^ 1) for i in range(lons)]
     lat_down = [(i, (i - 1) % lats) for i in range(lats)]
     lat_up = [(i, (i + 1) % lats) for i in range(lats)]
+    corner_up = [(i * lats + a, (i ^ 1) * lats + b) for i in range(lons) for a, b in lat_up]
     corner_down = [(i * lats + a, (i ^ 1) * lats + b) for i in range(lons) for a, b in lat_down]
 
     x, g = x.transpose(1, 2, 0, 3), g.transpose(1, 2, 0, 3)
@@ -663,18 +698,20 @@
     rows, send = main(
         own, lat_in, lon_in, corner_in, gain, w3, w3t, wproj_t, bias, bias_left, match
     )
-    body, tail = pieces(rows)
-    tail = lax.ppermute(tail, lon_axes, lon_swap)
-    got = lax.all_to_all(send, GROUP, 0, 0, tiled=True)
+    own, to_lat, to_lon, to_corner = pieces(rows)
+    back = (
+        lax.ppermute(to_lat, lat_axes, lat_up),
+        lax.ppermute(to_lon, lon_axes, lon_swap),
+        lax.ppermute(to_corner, both, corner_up),
+    )
+    got = exchange(send, GROUP)
     mixed = on_chip(fold_kernel, (lax.axis_size(REST), 16, 128 * (W_SLOTS + LATS)), "fold")(got)
-    mixed, tail = lax.optimization_barrier((mixed, tail))
-    lat_rows = lax.ppermute(jnp.concatenate([tail[3:], body[3:]], axis=1), lat_axes, lat_up)
-    got = lax.all_to_all(mixed, REST, 0, 0, tiled=True)
+    got = exchange(mixed, REST)
     spread = on_chip(share_kernel, send.shape, "share")(got)
-    spread, lat_rows = lax.optimization_barrier((spread, lat_rows))
-    parts = lax.all_to_all(spread, GROUP, 0, 0, tiled=True)
+    spread, back = lax.optimization_barrier((spread, back))
+    parts = exchange(spread, GROUP)
     grad_gain, grad_wqkv, grad_wproj, grad_bias = unpack(parts)
-    grad_x = norm_grads(x, g, gain, body, tail, lat_rows)
+    grad_x = norm_grads(x, g, gain, own, *back)
     grad_x = grad_x.transpose(2, 0, 1, 3)
     grad_bias = grad_bias.transpose(1, 0, 2)[None]
     return grad_x, grad_gain.reshape(C), grad_wqkv, grad_wproj, grad_bias

time: 76.3 us -> 69.1 us (0.906)
  waiting for transfers between devices: 26.9 us -> 10.7 us
  blocking collectives: 0 us -> 13.1 us
  starting transfers between devices: 29.8 us -> 25.8 us
    all_to_all x3 -> x2, waiting for transfers between devices: 23.9 us -> 5.98 us  [exchange(): lax.all_to_all(blocks, axes, 0, 0, tiled=True, axis_index_groups=order)]
    all_to_all x0 -> x1, blocking collectives: none -> 13.1 us  [exchange(): lax.all_to_all(blocks, axes, 0, 0, tiled=True, axis_index_groups=order)]
    all_to_all x3 -> x2, starting transfers between devices: 19.5 us -> 15.5 us  [exchange(): lax.all_to_all(blocks, axes, 0, 0, tiled=True, axis_index_groups=order)]
    ppermute x2 -> x3, waiting for transfers between devices: 0.01 us -> 2.73 us  [the longest x1 1.65 us: on_device(): lax.ppermute(to_lon, lon_axes, lon_swap)]
    ppermute x1, waiting for transfers between devices: 2.98 us -> 2 us  [on_device(): lat_in = lax.ppermute(to_lat, lat_axes, lat_down)]
    ppermute x2 -> x3, starting transfers between devices: 3.81 us -> 3.84 us  [the longest x1 2.73 us: on_device(): lax.ppermute(to_lon, lon_axes, lon_swap)]
  transfers between devices with their start and end apart: 8 -> 8, of which waited for: 4 -> 5; matrix products, arithmetic and copies ran while one was open for 0% -> 0% of each run, Pallas kernels for 10% -> 10%
where the time goes in v7:
time: 69.1 us; the launch traced here: 68.7 us
  starting transfers between devices  25.8 us (37%)
  Pallas kernels  18.3 us (26%)
  blocking collectives  13.1 us (19%)
  waiting for transfers between devices  10.7 us (15%)
  between operations  0.73 us (1%)
    all_to_all x2, starting transfers between devices, exchange(): lax.all_to_all(blocks, axes, 0, 0, tiled=True, axis_index_groups=order)  15.5 us
    all_to_all x1, blocking collectives, exchange(): lax.all_to_all(blocks, axes, 0, 0, tiled=True, axis_index_groups=order)  13.1 us
    pallas_call x1, Pallas kernels, main(): pl.pallas_call(main_kernel, out_shape=(jax.ShapeDtypeStruct((WINDOWS * WI...  8.43 us
    all_to_all x2, waiting for transfers between devices, exchange(): lax.all_to_all(blocks, axes, 0, 0, tiled=True, axis_index_groups=order)  5.98 us
    pallas_call x1, Pallas kernels, prepare(): pl.pallas_call(prepare_kernel, out_shape=(jax.ShapeDtypeStruct((TYPES, WI...  3.92 us
    ppermute x1, starting transfers between devices, on_device(): lon_in = lax.ppermute(to_lon, lon_axes, lon_swap)  3.66 us
    ppermute x1, starting transfers between devices, on_device(): corner_in = lax.ppermute(to_corner, both, corner_down)  2.8 us
    ppermute x1, starting transfers between devices, on_device(): lax.ppermute(to_lon, lon_axes, lon_swap)  2.73 us
  transfers between devices with their start and end apart: 8, of which 5 were waited for; matrix products, arithmetic and copies ran while one was open for 0% of the time, Pallas kernels for 10%

profile of v7, /device:TPU:1, one launch (start us, length us, event | category | flops | bytes accessed | tf_op | source)
XLA Modules:
  0.0 68.7 jit_solution(17526196474741613156)
XLA Ops:
  0.6 1.4 %pack.1 = (bf16[3,24,384]{2,1,0:T(8,128)(2,1)S(1)}, bf16[3,24,384]{2,1,0:T(8,128)(2,1)S(1)}, bf16[3,120,384]{2,1,0:T(8,128)(2,1)S(1)}) custom-call(bf16[6,36,4,192]{3,2,1,0:T(4,128)(2,1)} %bitcast.11, bf16[6,36,4,192]{3,2,1,0:T(4,128)(2,1)} %bitcast.14), custom_call_target="tpu_custom_call" | custom-call | tf_op jit(solution)/shard_map/pack/pallas_call | solution.py:655
  2.0 3.7 %collective-permute-start.1 = (bf16[3,24,384]{2,1,0:T(8,128)(2,1)S(1)}, bf16[3,24,384]{2,1,0:T(8,128)(2,1)S(1)}, u32[]{:S(2)}, u32[]{:S(2)}) collective-permute-start(bf16[3,24,384]{2,1,0:T(8,128)(2,1)S(1)} %get-tuple-element.33), channel_id=1, source_target_pairs={{0,4},{4,0},{8,12},{12,8},{16,20},{20,16},{24,28},{28,24},{32,36},... | collective-permute-start | bytes 165896 | tf_op jit(solution)/shard_map/ppermute | solution.py:693
  5.7 2.8 %collective-permute-start.2 = (bf16[3,24,384]{2,1,0:T(8,128)(2,1)S(1)}, bf16[3,24,384]{2,1,0:T(8,128)(2,1)S(1)}, u32[]{:S(2)}, u32[]{:S(2)}) collective-permute-start(bf16[3,24,384]{2,1,0:T(8,128)(2,1)S(1)} %get-tuple-element.34), channel_id=1, source_target_pairs={{0,7},{1,4},{2,5},{3,6},{4,3},{5,0},{6,1},{7,2},{8,15},{9,12},{10,... | collective-permute-start | bytes 165896 | tf_op jit(solution)/shard_map/ppermute | solution.py:692
  8.5 0.0 collective-permute-start
  8.5 3.9 %prepare.1 = (f32[12,144,128]{2,1,0:T(8,128)S(1)}, f32[2,144,128]{2,1,0:T(8,128)S(1)}, bf16[3,192,192]{2,1,0:T(8,128)(2,1)S(1)}, bf16[768,192]{1,0:T(8,128)(2,1)...) custom-call(f32[6,2,3312]{2,1,0:T(2,128)} %bitcast.18, ...), custom_call_target="tpu_custom_call" | custom-call | flops 4000000000 | bytes 4000000 | tf_op jit(solution)/shard_map/prepare/pallas_call | solution.py:182
  12.4 0.0 collective-permute-done.1.lon_ref
  12.4 0.0 collective-permute-done.2.corner_ref
  12.4 2.0 %collective-permute-done.lat_ref = bf16[3,120,384]{2,1,0:T(8,128)(2,1)S(1)} collective-permute-done((bf16[3,120,384]{2,1,0:T(8,128)(2,1)S(1)}, bf16[3,120,384]{2,1,0:T(8,128)(2,1)S(1)}, u32[]{:S(2)}, u32[]{:S(2)}) %collective-permute-start) | collective-permute-done | bytes 276512 | tf_op jit(solution)/shard_map/ppermute | solution.py:694
  14.4 8.4 %window_grads.1 = (bf16[864,192]{1,0:T(8,128)(2,1)S(1)}, bf16[32,16,384]{2,1,0:T(8,128)(2,1)S(1)}) custom-call(bf16[3,120,384]{2,1,0:T(8,128)(2,1)S(1)} %get-tuple-element.31.own_ref, bf16[3,120,384]{2,1,0:T(8,128)(2,1)S(1)} %collective-permute-done.lat_ref, bf16[3,24,384]{2,1,0:T(8,128)(2,1)S(1)} %collective-permute-done.1.lon_ref, ...), custom_call_target="tpu_custom_call" | custom-call | flops 20000000000 | bytes 4000000 | tf_op jit(solution)/shard_map/window_grads/pallas_call | solution.py:430
  22.8 0.0 copy-start
  22.9 0.0 copy-start.1
  22.9 13.1 %all_to_all.15.got_ref = bf16[32,16,384]{2,1,0:T(8,128)(2,1)S(1)} all-to-all(bf16[32,16,384]{2,1,0:T(8,128)(2,1)S(1)} %get-tuple-element.43), channel_id=1, replica_groups={{31,30,29,28,27,26,25,24,23,22,21,20,19,18,17,16,15,14,13,12,11,10,9,8,..., dimensions={0} | all-to-all | bytes 786432 | tf_op jit(solution)/shard_map/all_to_all | solution.py:677
  36.0 0.7 %fold.1 = bf16[8,16,768]{2,1,0:T(8,128)(2,1)} custom-call(bf16[32,16,384]{2,1,0:T(8,128)(2,1)S(1)} %all_to_all.15.got_ref), custom_call_target="tpu_custom_call" | custom-call | flops 1000000 | bytes 600000 | tf_op jit(solution)/shard_map/fold/pallas_call | solution.py:708
  36.8 8.9 %all-to-all-start.1 = ((bf16[8,16,768]{2,1,0:T(8,128)(2,1)}), bf16[8,16,768]{2,1,0:T(8,128)(2,1)S(1)}, u32[]{:S(2)}, u32[]{:S(2)}) async-start(bf16[8,16,768]{2,1,0:T(8,128)(2,1)} %fold.1), calls=%async_computation.1 | async-start | bytes 393216 | tf_op jit(solution)/shard_map/all_to_all | solution.py:677
  45.7 0.3 pieces.1
  46.0 0.9 %collective-permute-start.3 = (bf16[3,120,192]{2,1,0:T(8,128)(2,1)S(1)}, bf16[3,120,192]{2,1,0:T(8,128)(2,1)S(1)}, u32[]{:S(2)}, u32[]{:S(2)}) collective-permute-start(bf16[3,120,192]{2,1,0:T(8,128)(2,1)S(1)} %get-tuple-element.44), channel_id=1, source_target_pairs={{0,1},{1,2},{2,3},{3,0},{4,5},{5,6},{6,7},{7,4},{8,9},{9,10},{10,1... | collective-permute-start | bytes 414728 | tf_op jit(solution)/shard_map/ppermute | solution.py:703
  46.8 2.7 %collective-permute-start.4 = (bf16[3,24,192]{2,1,0:T(8,128)(2,1)S(1)}, bf16[3,24,192]{2,1,0:T(8,128)(2,1)S(1)}, u32[]{:S(2)}, u32[]{:S(2)}) collective-permute-start(bf16[3,24,192]{2,1,0:T(8,128)(2,1)S(1)} %get-tuple-element.45), channel_id=1, source_target_pairs={{0,4},{4,0},{8,12},{12,8},{16,20},{20,16},{24,28},{28,24},{32,36},... | collective-permute-start | bytes 82952 | tf_op jit(solution)/shard_map/ppermute | solution.py:704
  49.6 0.2 collective-permute-start.5
  49.8 1.1 %all-to-all-done.1.got_ref = bf16[8,16,768]{2,1,0:T(8,128)(2,1)S(1)} async-done(((bf16[8,16,768]{2,1,0:T(8,128)(2,1)}), bf16[8,16,768]{2,1,0:T(8,128)(2,1)S(1)}, u32[]{:S(2)}, u32[]{:S(2)}) %all-to-all-start.1) | async-done | bytes 196640 | tf_op jit(solution)/shard_map/all_to_all | solution.py:677
  50.9 0.8 %share.1 = bf16[32,16,384]{2,1,0:T(8,128)(2,1)} custom-call(bf16[8,16,768]{2,1,0:T(8,128)(2,1)S(1)} %all-to-all-done.1.got_ref), custom_call_target="tpu_custom_call" | custom-call | flops 1000000 | bytes 600000 | tf_op jit(solution)/shard_map/share/pallas_call | solution.py:710
  51.7 1.7 %collective-permute-done.4.lon_ref = bf16[3,24,192]{2,1,0:T(8,128)(2,1)S(1)} collective-permute-done((bf16[3,24,192]{2,1,0:T(8,128)(2,1)S(1)}, bf16[3,24,192]{2,1,0:T(8,128)(2,1)S(1)}, u32[]{:S(2)}, u32[]{:S(2)}) %collective-permute-start.4) | collective-permute-done | bytes 27680 | tf_op jit(solution)/shard_map/ppermute | solution.py:704
  53.4 1.1 %collective-permute-done.5.corner_ref = bf16[3,24,192]{2,1,0:T(8,128)(2,1)S(1)} collective-permute-done((bf16[3,24,192]{2,1,0:T(8,128)(2,1)S(1)}, bf16[3,24,192]{2,1,0:T(8,128)(2,1)S(1)}, u32[]{:S(2)}, u32[]{:S(2)}) %collective-permute-start.5) | collective-permute-done | bytes 27680 | tf_op jit(solution)/shard_map/ppermute | solution.py:705
  54.5 0.0 collective-permute-done.3.lat_ref
  54.5 6.6 %all-to-all-start.2 = ((bf16[32,16,384]{2,1,0:T(8,128)(2,1)}), bf16[32,16,384]{2,1,0:T(8,128)(2,1)S(1)}, u32[]{:S(2)}, u32[]{:S(2)}) async-start(bf16[32,16,384]{2,1,0:T(8,128)(2,1)} %share.1), calls=%async_computation.2 | async-start | bytes 786432 | tf_op jit(solution)/shard_map/all_to_all | solution.py:677
  61.1 0.0 copy-done
  61.1 0.0 copy-done.1
  61.1 1.9 %norm_grads.1 = bf16[6,36,4,192]{3,2,1,0:T(4,128)(2,1)} custom-call(bf16[6,36,4,192]{3,2,1,0:T(4,128)(2,1)S(1)} %bitcast.13, bf16[6,36,4,192]{3,2,1,0:T(4,128)(2,1)S(1)} %bitcast.16, f32[1,192]{1,0:T(1,128)S(1)} %get-tuple-element.30.gain_ref, bf16[3,120,192]{2,1,0:T(8,128)(2,1)S(1)} %get-tuple-element.42.own_ref, ...), custom_call_target="tpu_custom_call" | custom-call | flops 10000000 | bytes 1500000 | tf_op jit(solution)/shard_map/norm_grads/pallas_call | solution.py:532
  63.0 4.8 %all-to-all-done.2.parts_ref = bf16[32,16,384]{2,1,0:T(8,128)(2,1)S(1)} async-done(((bf16[32,16,384]{2,1,0:T(8,128)(2,1)}), bf16[32,16,384]{2,1,0:T(8,128)(2,1)S(1)}, u32[]{:S(2)}, u32[]{:S(2)}) %all-to-all-start.2) | async-done | bytes 393248 | tf_op jit(solution)/shard_map/all_to_all | solution.py:677
  67.8 0.9 %unpack.1 = (f32[1,192]{1,0:T(1,128)}, f32[192,576]{1,0:T(8,128)}, f32[192,192]{1,0:T(8,128)}, f32[6,2,3312]{2,1,0:T(2,128)}) custom-call(bf16[32,16,384]{2,1,0:T(8,128)(2,1)S(1)} %all-to-all-done.2.parts_ref), custom_call_target="tpu_custom_call" | custom-call | tf_op jit(solution)/shard_map/unpack/pallas_call | solution.py:574
Async XLA Ops:
  2.0 10.4 %collective-permute-start.1 = (bf16[3,24,384]{2,1,0:T(8,128)(2,1)S(1)}, bf16[3,24,384]{2,1,0:T(8,128)(2,1)S(1)}, u32[]{:S(2)}, u32[]{:S(2)}) collective-permute-start(bf16[3,24,384]{2,1,0:T(8,128)(2,1)S(1)} %get-tuple-element.33), channel_id=1, source_target_pairs={{0,4},{4,0},{8,12},{12,8},{16,20},{20,16},{24,28},{28,24},{32,36},... | collective-permute-start | bytes 165896 | tf_op jit(solution)/shard_map/ppermute | solution.py:693
  5.7 6.7 %collective-permute-start.2 = (bf16[3,24,384]{2,1,0:T(8,128)(2,1)S(1)}, bf16[3,24,384]{2,1,0:T(8,128)(2,1)S(1)}, u32[]{:S(2)}, u32[]{:S(2)}) collective-permute-start(bf16[3,24,384]{2,1,0:T(8,128)(2,1)S(1)} %get-tuple-element.34), channel_id=1, source_target_pairs={{0,7},{1,4},{2,5},{3,6},{4,3},{5,0},{6,1},{7,2},{8,15},{9,12},{10,... | collective-permute-start | bytes 165896 | tf_op jit(solution)/shard_map/ppermute | solution.py:692
  8.5 6.0 %collective-permute-start = (bf16[3,120,384]{2,1,0:T(8,128)(2,1)S(1)}, bf16[3,120,384]{2,1,0:T(8,128)(2,1)S(1)}, u32[]{:S(2)}, u32[]{:S(2)}) collective-permute-start(bf16[3,120,384]{2,1,0:T(8,128)(2,1)S(1)} %get-tuple-element.32), channel_id=1, source_target_pairs={{0,3},{1,0},{2,1},{3,2},{4,7},{5,4},{6,5},{7,6},{8,11},{9,8},{10,9... | collective-permute-start | bytes 829448 | tf_op jit(solution)/shard_map/ppermute | solution.py:694
  22.8 38.2 %copy-start = (bf16[4,6,36,192]{3,0,2,1:T(4,128)(2,1)S(1)}, bf16[4,6,36,192]{3,0,2,1:T(4,128)(2,1)}, u32[]{:S(2)}) copy-start(bf16[4,6,36,192]{3,0,2,1:T(4,128)(2,1)} %param.6) | copy-start | bytes 995332
  22.9 38.2 %copy-start.1 = (bf16[4,6,36,192]{3,0,2,1:T(4,128)(2,1)S(1)}, bf16[4,6,36,192]{3,0,2,1:T(4,128)(2,1)}, u32[]{:S(2)}) copy-start(bf16[4,6,36,192]{3,0,2,1:T(4,128)(2,1)} %param.7) | copy-start | bytes 995332
  36.8 14.2 %all-to-all-start.1 = ((bf16[8,16,768]{2,1,0:T(8,128)(2,1)}), bf16[8,16,768]{2,1,0:T(8,128)(2,1)S(1)}, u32[]{:S(2)}, u32[]{:S(2)}) async-start(bf16[8,16,768]{2,1,0:T(8,128)(2,1)} %fold.1), calls=%async_computation.1 | async-start | bytes 393216 | tf_op jit(solution)/shard_map/all_to_all | solution.py:677
  46.0 8.5 %collective-permute-start.3 = (bf16[3,120,192]{2,1,0:T(8,128)(2,1)S(1)}, bf16[3,120,192]{2,1,0:T(8,128)(2,1)S(1)}, u32[]{:S(2)}, u32[]{:S(2)}) collective-permute-start(bf16[3,120,192]{2,1,0:T(8,128)(2,1)S(1)} %get-tuple-element.44), channel_id=1, source_target_pairs={{0,1},{1,2},{2,3},{3,0},{4,5},{5,6},{6,7},{7,4},{8,9},{9,10},{10,1... | collective-permute-start | bytes 414728 | tf_op jit(solution)/shard_map/ppermute | solution.py:703
  46.8 6.5 %collective-permute-start.4 = (bf16[3,24,192]{2,1,0:T(8,128)(2,1)S(1)}, bf16[3,24,192]{2,1,0:T(8,128)(2,1)S(1)}, u32[]{:S(2)}, u32[]{:S(2)}) collective-permute-start(bf16[3,24,192]{2,1,0:T(8,128)(2,1)S(1)} %get-tuple-element.45), channel_id=1, source_target_pairs={{0,4},{4,0},{8,12},{12,8},{16,20},{20,16},{24,28},{28,24},{32,36},... | collective-permute-start | bytes 82952 | tf_op jit(solution)/shard_map/ppermute | solution.py:704
  49.6 4.9 %collective-permute-start.5 = (bf16[3,24,192]{2,1,0:T(8,128)(2,1)S(1)}, bf16[3,24,192]{2,1,0:T(8,128)(2,1)S(1)}, u32[]{:S(2)}, u32[]{:S(2)}) collective-permute-start(bf16[3,24,192]{2,1,0:T(8,128)(2,1)S(1)} %get-tuple-element.46), channel_id=1, source_target_pairs={{0,5},{1,6},{2,7},{3,4},{4,1},{5,2},{6,3},{7,0},{8,13},{9,14},{10,... | collective-permute-start | bytes 82952 | tf_op jit(solution)/shard_map/ppermute | solution.py:705
  54.5 13.3 %all-to-all-start.2 = ((bf16[32,16,384]{2,1,0:T(8,128)(2,1)}), bf16[32,16,384]{2,1,0:T(8,128)(2,1)S(1)}, u32[]{:S(2)}, u32[]{:S(2)}) async-start(bf16[32,16,384]{2,1,0:T(8,128)(2,1)} %share.1), calls=%async_computation.2 | async-start | bytes 786432 | tf_op jit(solution)/shard_map/all_to_all | solution.py:677

commit v8 on v7

--- a/solution.py
+++ b/solution.py
@@ -28,6 +28,7 @@
 GROUP = ("y", "xh", "xl", "c")
 REST = "z"
 PARTS = 32
+ORDER = [31 - (y * 8 + xh * 4 + xl * 2 + c) for c in range(2) for xl in range(2) for xh in range(2) for y in range(4)]
 SLOTS = 3
 W_TILES = 72
 W_SLOTS = 2
@@ -204,7 +205,7 @@
         ],
         compiler_params=pltpu.CompilerParams(vmem_limit_bytes=VMEM_LIMIT),
         cost_estimate=pl.CostEstimate(
-            flops=4_000_000_000, bytes_accessed=4_000_000, transcendentals=0
+            flops=400_000_000, bytes_accessed=400_000, transcendentals=0
         ),
         name="prepare",
     )(*(in_hbm(a) for a in (table, wqkv, wproj, gain, x, g)))
@@ -592,7 +593,7 @@
     last = [jnp.zeros((16, 128), f32)] * LATS
     for p in range(PARTS):
         shared += got_ref[p, :, : 128 * W_SLOTS].astype(f32)
-        last[LATS - 1 - p % LATS] += got_ref[p, :, 128 * W_SLOTS :].astype(f32)
+        last[ORDER[p] % LATS] += got_ref[p, :, 128 * W_SLOTS :].astype(f32)
     total = jnp.concatenate([shared] + last, axis=1).astype(bf16)
     for n in range(out_ref.shape[0]):
         out_ref[n] = total
@@ -605,12 +606,14 @@
     shared = total[:, : 128 * W_SLOTS].astype(bf16)
     last = [total[:, 128 * (W_SLOTS + n) : 128 * (W_SLOTS + n + 1)] for n in range(LATS)]
     everywhere = last[0] + last[1] + last[2] + last[3]
-    part = PARTS - 1 - lax.axis_index(GROUP)
-    per_lat = (part >= B_FIRST) & (part < GAIN_PART)
+    place = lax.axis_index(GROUP)
+    per_lat = place == ORDER[B_FIRST]
+    for p in range(B_FIRST + 1, GAIN_PART):
+        per_lat |= place == ORDER[p]
     last = [jnp.where(per_lat, one, everywhere).astype(bf16) for one in last]
     for p in range(PARTS):
         out_ref[p, :, : 128 * W_SLOTS] = shared
-        out_ref[p, :, 128 * W_SLOTS :] = last[LATS - 1 - p % LATS]
+        out_ref[p, :, 128 * W_SLOTS :] = last[ORDER[p] % LATS]
 
 
 def on_chip(kernel, shape, name):
@@ -672,9 +675,8 @@
     )(in_hbm(x), in_hbm(g))
 
 
-def exchange(blocks, axes):
-    order = [list(reversed(range(blocks.shape[0])))]
-    return lax.all_to_all(blocks, axes, 0, 0, tiled=True, axis_index_groups=order)
+def exchange(blocks, axes, order):
+    return lax.all_to_all(blocks, axes, 0, 0, tiled=True, axis_index_groups=[order])
 
 
 def on_device(x, g, ln_gain, w_qkv, w_proj, bias_table):
@@ -704,12 +706,12 @@
         lax.ppermute(to_lon, lon_axes, lon_swap),
         lax.ppermute(to_corner, both, corner_up),
     )
-    got = exchange(send, GROUP)
+    got = exchange(send, GROUP, ORDER)
     mixed = on_chip(fold_kernel, (lax.axis_size(REST), 16, 128 * (W_SLOTS + LATS)), "fold")(got)
-    got = exchange(mixed, REST)
+    got = exchange(mixed, REST, list(reversed(range(mixed.shape[0]))))
     spread = on_chip(share_kernel, send.shape, "share")(got)
     spread, back = lax.optimization_barrier((spread, back))
-    parts = exchange(spread, GROUP)
+    parts = exchange(spread, GROUP, ORDER)
     grad_gain, grad_wqkv, grad_wproj, grad_bias = unpack(parts)
     grad_x = norm_grads(x, g, gain, own, *back)
     grad_x = grad_x.transpose(2, 0, 1, 3)

time: 69.1 us -> 68.4 us (0.990)
  waiting for transfers between devices: 10.7 us -> 7.43 us
  starting transfers between devices: 25.8 us -> 27.2 us
  blocking collectives: 13.1 us -> 14.4 us
    ppermute x1, starting transfers between devices: 0.01 us -> 3.32 us  [on_device(): lat_in = lax.ppermute(to_lat, lat_axes, lat_down)]
    ppermute x1, starting transfers between devices: 3.66 us -> 1.01 us  [on_device(): lon_in = lax.ppermute(to_lon, lon_axes, lon_swap)]
    ppermute x1, waiting for transfers between devices: 2 us -> 0.01 us  [on_device(): lat_in = lax.ppermute(to_lat, lat_axes, lat_down)]
    all_to_all x1, blocking collectives: 13.1 us -> 14.4 us  [exchange(): lax.all_to_all(blocks, axes, 0, 0, tiled=True, axis_index_groups=[order])]
    ppermute x1, starting transfers between devices: 0.22 us -> 1.43 us  [on_device(): lax.ppermute(to_corner, both, corner_up)]
    ppermute x1, starting transfers between devices: 2.73 us -> 1.52 us  [on_device(): lax.ppermute(to_lon, lon_axes, lon_swap)]
    ppermute x1, starting transfers between devices: 0.89 us -> 1.78 us  [on_device(): lax.ppermute(to_lat, lat_axes, lat_up)]
  transfers between devices with their start and end apart: 8 -> 8, of which waited for: 5 -> 4; matrix products, arithmetic and copies ran while one was open for 0% -> 0% of each run, Pallas kernels for 10% -> 10%
where the time goes in v8:
time: 68.4 us; the launch traced here: 68 us
  starting transfers between devices  27.2 us (40%)
  Pallas kernels  18.3 us (27%)
  blocking collectives  14.4 us (21%)
  waiting for transfers between devices  7.43 us (11%)
  between operations  0.73 us (1%)
    all_to_all x2, starting transfers between devices, exchange(): lax.all_to_all(blocks, axes, 0, 0, tiled=True, axis_index_groups=[order])  15.9 us
    all_to_all x1, blocking collectives, exchange(): lax.all_to_all(blocks, axes, 0, 0, tiled=True, axis_index_groups=[order])  14.4 us
    pallas_call x1, Pallas kernels, main(): pl.pallas_call(main_kernel, out_shape=(jax.ShapeDtypeStruct((WINDOWS * WI...  8.44 us
    all_to_all x2, waiting for transfers between devices, exchange(): lax.all_to_all(blocks, axes, 0, 0, tiled=True, axis_index_groups=[order])  5.3 us
    pallas_call x1, Pallas kernels, prepare(): pl.pallas_call(prepare_kernel, out_shape=(jax.ShapeDtypeStruct((TYPES, WI...  3.91 us
    ppermute x1, starting transfers between devices, on_device(): lat_in = lax.ppermute(to_lat, lat_axes, lat_down)  3.32 us
    ppermute x1, starting transfers between devices, on_device(): corner_in = lax.ppermute(to_corner, both, corner_down)  2.23 us
    pallas_call x1, Pallas kernels, norm_grads(): pl.pallas_call(norm_kernel, out_shape=jax.ShapeDtypeStruct(x.shape, bf16)...  1.86 us
  transfers between devices with their start and end apart: 8, of which 4 were waited for; matrix products, arithmetic and copies ran while one was open for 0% of the time, Pallas kernels for 10%

profile of v8, /device:TPU:1, one launch (start us, length us, event | category | flops | bytes accessed | tf_op | source)
XLA Modules:
  0.0 68.0 jit_solution(18271348648411991236)
XLA Ops:
  0.6 1.4 %pack.1 = (bf16[3,24,384]{2,1,0:T(8,128)(2,1)S(1)}, bf16[3,24,384]{2,1,0:T(8,128)(2,1)S(1)}, bf16[3,120,384]{2,1,0:T(8,128)(2,1)S(1)}) custom-call(bf16[6,36,4,192]{3,2,1,0:T(4,128)(2,1)} %bitcast.11, bf16[6,36,4,192]{3,2,1,0:T(4,128)(2,1)} %bitcast.14), custom_call_target="tpu_custom_call" | custom-call | tf_op jit(solution)/shard_map/pack/pallas_call | solution.py:658
  2.0 3.3 %collective-permute-start = (bf16[3,120,384]{2,1,0:T(8,128)(2,1)S(1)}, bf16[3,120,384]{2,1,0:T(8,128)(2,1)S(1)}, u32[]{:S(2)}, u32[]{:S(2)}) collective-permute-start(bf16[3,120,384]{2,1,0:T(8,128)(2,1)S(1)} %get-tuple-element.32), channel_id=1, source_target_pairs={{0,3},{1,0},{2,1},{3,2},{4,7},{5,4},{6,5},{7,6},{8,11},{9,8},{10,9... | collective-permute-start | bytes 829448 | tf_op jit(solution)/shard_map/ppermute | solution.py:696
  5.3 1.0 %collective-permute-start.1 = (bf16[3,24,384]{2,1,0:T(8,128)(2,1)S(1)}, bf16[3,24,384]{2,1,0:T(8,128)(2,1)S(1)}, u32[]{:S(2)}, u32[]{:S(2)}) collective-permute-start(bf16[3,24,384]{2,1,0:T(8,128)(2,1)S(1)} %get-tuple-element.33), channel_id=1, source_target_pairs={{0,4},{4,0},{8,12},{12,8},{16,20},{20,16},{24,28},{28,24},{32,36},... | collective-permute-start | bytes 165896 | tf_op jit(solution)/shard_map/ppermute | solution.py:695
  6.3 2.2 %collective-permute-start.2 = (bf16[3,24,384]{2,1,0:T(8,128)(2,1)S(1)}, bf16[3,24,384]{2,1,0:T(8,128)(2,1)S(1)}, u32[]{:S(2)}, u32[]{:S(2)}) collective-permute-start(bf16[3,24,384]{2,1,0:T(8,128)(2,1)S(1)} %get-tuple-element.34), channel_id=1, source_target_pairs={{0,7},{1,4},{2,5},{3,6},{4,3},{5,0},{6,1},{7,2},{8,15},{9,12},{10,... | collective-permute-start | bytes 165896 | tf_op jit(solution)/shard_map/ppermute | solution.py:694
  8.5 3.9 %prepare.1 = (f32[12,144,128]{2,1,0:T(8,128)S(1)}, f32[2,144,128]{2,1,0:T(8,128)S(1)}, bf16[3,192,192]{2,1,0:T(8,128)(2,1)S(1)}, bf16[768,192]{1,0:T(8,128)(2,1)...) custom-call(f32[6,2,3312]{2,1,0:T(2,128)} %bitcast.18, ...), custom_call_target="tpu_custom_call" | custom-call | flops 400000000 | bytes 400000 | tf_op jit(solution)/shard_map/prepare/pallas_call | solution.py:183
  12.5 0.0 collective-permute-done.1.lon_ref
  12.5 0.0 collective-permute-done.2.corner_ref
  12.5 0.0 collective-permute-done.lat_ref
  12.5 8.4 %window_grads.1 = (bf16[864,192]{1,0:T(8,128)(2,1)S(1)}, bf16[32,16,384]{2,1,0:T(8,128)(2,1)S(1)}) custom-call(bf16[3,120,384]{2,1,0:T(8,128)(2,1)S(1)} %get-tuple-element.31.own_ref, bf16[3,120,384]{2,1,0:T(8,128)(2,1)S(1)} %collective-permute-done.lat_ref, bf16[3,24,384]{2,1,0:T(8,128)(2,1)S(1)} %collective-permute-done.1.lon_ref, ...), custom_call_target="tpu_custom_call" | custom-call | flops 20000000000 | bytes 4000000 | tf_op jit(solution)/shard_map/window_grads/pallas_call | solution.py:431
  20.9 0.0 copy-start
  21.0 0.0 copy-start.1
  21.0 14.4 %all_to_all.15.got_ref = bf16[32,16,384]{2,1,0:T(8,128)(2,1)S(1)} all-to-all(bf16[32,16,384]{2,1,0:T(8,128)(2,1)S(1)} %get-tuple-element.43), channel_id=1, replica_groups={{31,23,15,7,27,19,11,3,29,21,13,5,25,17,9,1,30,22,14,6,26,18,10,2,28,20..., dimensions={0} | all-to-all | bytes 786432 | tf_op jit(solution)/shard_map/all_to_all | solution.py:679
  35.3 0.7 %fold.1 = bf16[8,16,768]{2,1,0:T(8,128)(2,1)} custom-call(bf16[32,16,384]{2,1,0:T(8,128)(2,1)S(1)} %all_to_all.15.got_ref), custom_call_target="tpu_custom_call" | custom-call | flops 1000000 | bytes 600000 | tf_op jit(solution)/shard_map/fold/pallas_call | solution.py:710
  36.1 8.9 %all-to-all-start.1 = ((bf16[8,16,768]{2,1,0:T(8,128)(2,1)}), bf16[8,16,768]{2,1,0:T(8,128)(2,1)S(1)}, u32[]{:S(2)}, u32[]{:S(2)}) async-start(bf16[8,16,768]{2,1,0:T(8,128)(2,1)} %fold.1), calls=%async_computation.1 | async-start | bytes 393216 | tf_op jit(solution)/shard_map/all_to_all | solution.py:679
  45.0 0.3 pieces.1
  45.3 1.8 %collective-permute-start.3 = (bf16[3,120,192]{2,1,0:T(8,128)(2,1)S(1)}, bf16[3,120,192]{2,1,0:T(8,128)(2,1)S(1)}, u32[]{:S(2)}, u32[]{:S(2)}) collective-permute-start(bf16[3,120,192]{2,1,0:T(8,128)(2,1)S(1)} %get-tuple-element.44), channel_id=1, source_target_pairs={{0,1},{1,2},{2,3},{3,0},{4,5},{5,6},{6,7},{7,4},{8,9},{9,10},{10,1... | collective-permute-start | bytes 414728 | tf_op jit(solution)/shard_map/ppermute | solution.py:705
  47.0 1.5 %collective-permute-start.4 = (bf16[3,24,192]{2,1,0:T(8,128)(2,1)S(1)}, bf16[3,24,192]{2,1,0:T(8,128)(2,1)S(1)}, u32[]{:S(2)}, u32[]{:S(2)}) collective-permute-start(bf16[3,24,192]{2,1,0:T(8,128)(2,1)S(1)} %get-tuple-element.45), channel_id=1, source_target_pairs={{0,4},{4,0},{8,12},{12,8},{16,20},{20,16},{24,28},{28,24},{32,36},... | collective-permute-start | bytes 82952 | tf_op jit(solution)/shard_map/ppermute | solution.py:706
  48.6 1.4 %collective-permute-start.5 = (bf16[3,24,192]{2,1,0:T(8,128)(2,1)S(1)}, bf16[3,24,192]{2,1,0:T(8,128)(2,1)S(1)}, u32[]{:S(2)}, u32[]{:S(2)}) collective-permute-start(bf16[3,24,192]{2,1,0:T(8,128)(2,1)S(1)} %get-tuple-element.46), channel_id=1, source_target_pairs={{0,5},{1,6},{2,7},{3,4},{4,1},{5,2},{6,3},{7,0},{8,13},{9,14},{10,... | collective-permute-start | bytes 82952 | tf_op jit(solution)/shard_map/ppermute | solution.py:707
  50.0 0.5 all-to-all-done.1.got_ref
  50.5 0.8 %share.1 = bf16[32,16,384]{2,1,0:T(8,128)(2,1)} custom-call(bf16[8,16,768]{2,1,0:T(8,128)(2,1)S(1)} %all-to-all-done.1.got_ref), custom_call_target="tpu_custom_call" | custom-call | flops 1000000 | bytes 600000 | tf_op jit(solution)/shard_map/share/pallas_call | solution.py:712
  51.3 1.0 %collective-permute-done.4.lon_ref = bf16[3,24,192]{2,1,0:T(8,128)(2,1)S(1)} collective-permute-done((bf16[3,24,192]{2,1,0:T(8,128)(2,1)S(1)}, bf16[3,24,192]{2,1,0:T(8,128)(2,1)S(1)}, u32[]{:S(2)}, u32[]{:S(2)}) %collective-permute-start.4) | collective-permute-done | bytes 27680 | tf_op jit(solution)/shard_map/ppermute | solution.py:706
  52.4 1.1 %collective-permute-done.5.corner_ref = bf16[3,24,192]{2,1,0:T(8,128)(2,1)S(1)} collective-permute-done((bf16[3,24,192]{2,1,0:T(8,128)(2,1)S(1)}, bf16[3,24,192]{2,1,0:T(8,128)(2,1)S(1)}, u32[]{:S(2)}, u32[]{:S(2)}) %collective-permute-start.5) | collective-permute-done | bytes 27680 | tf_op jit(solution)/shard_map/ppermute | solution.py:707
  53.5 0.0 collective-permute-done.3.lat_ref
  53.5 7.0 %all-to-all-start.2 = ((bf16[32,16,384]{2,1,0:T(8,128)(2,1)}), bf16[32,16,384]{2,1,0:T(8,128)(2,1)S(1)}, u32[]{:S(2)}, u32[]{:S(2)}) async-start(bf16[32,16,384]{2,1,0:T(8,128)(2,1)} %share.1), calls=%async_computation.2 | async-start | bytes 786432 | tf_op jit(solution)/shard_map/all_to_all | solution.py:679
  60.4 0.0 copy-done
  60.4 0.0 copy-done.1
  60.4 1.9 %norm_grads.1 = bf16[6,36,4,192]{3,2,1,0:T(4,128)(2,1)} custom-call(bf16[6,36,4,192]{3,2,1,0:T(4,128)(2,1)S(1)} %bitcast.13, bf16[6,36,4,192]{3,2,1,0:T(4,128)(2,1)S(1)} %bitcast.16, f32[1,192]{1,0:T(1,128)S(1)} %get-tuple-element.30.gain_ref, bf16[3,120,192]{2,1,0:T(8,128)(2,1)S(1)} %get-tuple-element.42.own_ref, ...), custom_call_target="tpu_custom_call" | custom-call | flops 10000000 | bytes 1500000 | tf_op jit(solution)/shard_map/norm_grads/pallas_call | solution.py:533
  62.3 4.8 %all-to-all-done.2.parts_ref = bf16[32,16,384]{2,1,0:T(8,128)(2,1)S(1)} async-done(((bf16[32,16,384]{2,1,0:T(8,128)(2,1)}), bf16[32,16,384]{2,1,0:T(8,128)(2,1)S(1)}, u32[]{:S(2)}, u32[]{:S(2)}) %all-to-all-start.2) | async-done | bytes 393248 | tf_op jit(solution)/shard_map/all_to_all | solution.py:679
  67.1 0.9 %unpack.1 = (f32[1,192]{1,0:T(1,128)}, f32[192,576]{1,0:T(8,128)}, f32[192,192]{1,0:T(8,128)}, f32[6,2,3312]{2,1,0:T(2,128)}) custom-call(bf16[32,16,384]{2,1,0:T(8,128)(2,1)S(1)} %all-to-all-done.2.parts_ref), custom_call_target="tpu_custom_call" | custom-call | tf_op jit(solution)/shard_map/unpack/pallas_call | solution.py:575
Async XLA Ops:
  2.0 10.5 %collective-permute-start = (bf16[3,120,384]{2,1,0:T(8,128)(2,1)S(1)}, bf16[3,120,384]{2,1,0:T(8,128)(2,1)S(1)}, u32[]{:S(2)}, u32[]{:S(2)}) collective-permute-start(bf16[3,120,384]{2,1,0:T(8,128)(2,1)S(1)} %get-tuple-element.32), channel_id=1, source_target_pairs={{0,3},{1,0},{2,1},{3,2},{4,7},{5,4},{6,5},{7,6},{8,11},{9,8},{10,9... | collective-permute-start | bytes 829448 | tf_op jit(solution)/shard_map/ppermute | solution.py:696
  5.3 7.2 %collective-permute-start.1 = (bf16[3,24,384]{2,1,0:T(8,128)(2,1)S(1)}, bf16[3,24,384]{2,1,0:T(8,128)(2,1)S(1)}, u32[]{:S(2)}, u32[]{:S(2)}) collective-permute-start(bf16[3,24,384]{2,1,0:T(8,128)(2,1)S(1)} %get-tuple-element.33), channel_id=1, source_target_pairs={{0,4},{4,0},{8,12},{12,8},{16,20},{20,16},{24,28},{28,24},{32,36},... | collective-permute-start | bytes 165896 | tf_op jit(solution)/shard_map/ppermute | solution.py:695
  6.3 6.2 %collective-permute-start.2 = (bf16[3,24,384]{2,1,0:T(8,128)(2,1)S(1)}, bf16[3,24,384]{2,1,0:T(8,128)(2,1)S(1)}, u32[]{:S(2)}, u32[]{:S(2)}) collective-permute-start(bf16[3,24,384]{2,1,0:T(8,128)(2,1)S(1)} %get-tuple-element.34), channel_id=1, source_target_pairs={{0,7},{1,4},{2,5},{3,6},{4,3},{5,0},{6,1},{7,2},{8,15},{9,12},{10,... | collective-permute-start | bytes 165896 | tf_op jit(solution)/shard_map/ppermute | solution.py:694
  20.9 39.5 %copy-start = (bf16[4,6,36,192]{3,0,2,1:T(4,128)(2,1)S(1)}, bf16[4,6,36,192]{3,0,2,1:T(4,128)(2,1)}, u32[]{:S(2)}) copy-start(bf16[4,6,36,192]{3,0,2,1:T(4,128)(2,1)} %param.6) | copy-start | bytes 995332
  21.0 39.5 %copy-start.1 = (bf16[4,6,36,192]{3,0,2,1:T(4,128)(2,1)S(1)}, bf16[4,6,36,192]{3,0,2,1:T(4,128)(2,1)}, u32[]{:S(2)}) copy-start(bf16[4,6,36,192]{3,0,2,1:T(4,128)(2,1)} %param.7) | copy-start | bytes 995332
  36.1 14.5 %all-to-all-start.1 = ((bf16[8,16,768]{2,1,0:T(8,128)(2,1)}), bf16[8,16,768]{2,1,0:T(8,128)(2,1)S(1)}, u32[]{:S(2)}, u32[]{:S(2)}) async-start(bf16[8,16,768]{2,1,0:T(8,128)(2,1)} %fold.1), calls=%async_computation.1 | async-start | bytes 393216 | tf_op jit(solution)/shard_map/all_to_all | solution.py:679
  45.3 8.2 %collective-permute-start.3 = (bf16[3,120,192]{2,1,0:T(8,128)(2,1)S(1)}, bf16[3,120,192]{2,1,0:T(8,128)(2,1)S(1)}, u32[]{:S(2)}, u32[]{:S(2)}) collective-permute-start(bf16[3,120,192]{2,1,0:T(8,128)(2,1)S(1)} %get-tuple-element.44), channel_id=1, source_target_pairs={{0,1},{1,2},{2,3},{3,0},{4,5},{5,6},{6,7},{7,4},{8,9},{9,10},{10,1... | collective-permute-start | bytes 414728 | tf_op jit(solution)/shard_map/ppermute | solution.py:705
  47.0 5.3 %collective-permute-start.4 = (bf16[3,24,192]{2,1,0:T(8,128)(2,1)S(1)}, bf16[3,24,192]{2,1,0:T(8,128)(2,1)S(1)}, u32[]{:S(2)}, u32[]{:S(2)}) collective-permute-start(bf16[3,24,192]{2,1,0:T(8,128)(2,1)S(1)} %get-tuple-element.45), channel_id=1, source_target_pairs={{0,4},{4,0},{8,12},{12,8},{16,20},{20,16},{24,28},{28,24},{32,36},... | collective-permute-start | bytes 82952 | tf_op jit(solution)/shard_map/ppermute | solution.py:706
  48.6 4.9 %collective-permute-start.5 = (bf16[3,24,192]{2,1,0:T(8,128)(2,1)S(1)}, bf16[3,24,192]{2,1,0:T(8,128)(2,1)S(1)}, u32[]{:S(2)}, u32[]{:S(2)}) collective-permute-start(bf16[3,24,192]{2,1,0:T(8,128)(2,1)S(1)} %get-tuple-element.46), channel_id=1, source_target_pairs={{0,5},{1,6},{2,7},{3,4},{4,1},{5,2},{6,3},{7,0},{8,13},{9,14},{10,... | collective-permute-start | bytes 82952 | tf_op jit(solution)/shard_map/ppermute | solution.py:707
  53.5 13.6 %all-to-all-start.2 = ((bf16[32,16,384]{2,1,0:T(8,128)(2,1)}), bf16[32,16,384]{2,1,0:T(8,128)(2,1)S(1)}, u32[]{:S(2)}, u32[]{:S(2)}) async-start(bf16[32,16,384]{2,1,0:T(8,128)(2,1)} %share.1), calls=%async_computation.2 | async-start | bytes 786432 | tf_op jit(solution)/shard_map/all_to_all | solution.py:679

commit v9 on v8

--- a/solution.py
+++ b/solution.py
@@ -39,6 +39,8 @@
 WIDTH = 256
 LATS = 4
 WIDE = 3584
+TALL = 160
+TALLER = 208
 f32 = jnp.float32
 bf16 = jnp.bfloat16
 VMEM_LIMIT = 40 * 1024 * 1024
@@ -93,7 +95,7 @@
 def prepare_kernel(
     table_hbm, wqkv_hbm, wproj_hbm, gain_hbm, x_hbm, g_hbm,
     main_ref, left_ref, w3_ref, w3t_ref, wprojt_ref, own_ref, match_ref, gain_out,
-    wide, pairs, table_ref, wqkv_ref, wproj_ref, mine, sems,
+    wide, pairs, plain, plain_left, table_ref, wqkv_ref, wproj_ref, mine, sems,
 ):
     kept = pl.ds(3, 3), pl.ds(6, 30)
     moves = (
@@ -139,7 +141,7 @@
                 inside = (lane >= 32 * q) & (lane < 32 * q + OFFSETS)
                 total = jnp.where(inside, piece[:, :128], total)
             pairs[v, pl.ds(zl_j, TYPES, stride=16), :] = total[:TYPES]
-    full = jnp.concatenate([pairs[v] for v in range(3)], axis=1)
+    full = jnp.concatenate([pairs[v, : TYPES * 16] for v in range(3)], axis=1)
     high = full.astype(bf16)
     rest = full - high.astype(f32)
     middle = rest.astype(bf16)
@@ -153,9 +155,9 @@
             for h in range(HEADS):
                 t = lz * HEADS + h
                 block = dense[t * 16 : t * 16 + PAIRS]
-                main_ref[t, pl.ds(oj, PAIRS, stride=WLON), :] = block[:, :MAIN]
+                plain[t, pl.ds(oj, PAIRS, stride=WLON), :] = block[:, :MAIN]
                 left = jnp.where(lane_head == h, block[:, MAIN:], left)
-            left_ref[lz, pl.ds(oj, PAIRS, stride=WLON), :] = left
+            plain_left[lz, pl.ds(oj, PAIRS, stride=WLON), :] = left
     lat = lax.axis_index("xl") * 2 + lax.axis_index("c")
     last_band = (lat == LATS - 1).astype(jnp.int32)
 
@@ -169,9 +171,9 @@
         allowed = region(column, lz) == region(j, lz)
         for h in range(HEADS):
             t = lz * HEADS + h
-            main_ref[t] = jnp.where(allowed, main_ref[t], -1e30)
+            main_ref[t] = jnp.where(allowed, plain[t, :WIN], -1e30)
         allowed = region(query_index(column + MAIN), lz) == region(j, lz)
-        left_ref[lz] = jnp.where(allowed, left_ref[lz], -1e30)
+        left_ref[lz] = jnp.where(allowed, plain_left[lz, :WIN], -1e30)
 
 
 def in_hbm(array):
@@ -196,7 +198,9 @@
         out_specs=(vmem,) * 8,
         scratch_shapes=[
             pltpu.VMEM((16, WIDE), f32),
-            pltpu.VMEM((3, TYPES * 16, 128), f32),
+            pltpu.VMEM((3, TALLER, 128), f32),
+            pltpu.VMEM((TYPES, TALL, MAIN), f32),
+            pltpu.VMEM((2, TALL, MAIN), f32),
             pltpu.VMEM((HEADS, 2, TABLE), f32),
             pltpu.VMEM((C, 3 * C), bf16),
             pltpu.VMEM((C, C), bf16),
@@ -307,9 +311,9 @@
             grad_scores = attend * (grad_attend - total)
             grad_half_ref[w, :, columns] = grad_scores.astype(bf16)
             if t < HEADS:
-                dense[lz * HEADS + t] += grad_scores
+                dense[lz * HEADS + t, :WIN] += grad_scores
             else:
-                dense_left[lz] += grad_scores
+                dense_left[lz, :WIN] += grad_scores
 
     for w in range(WINDOWS):
         span = slice(w * WIN, (w + 1) * WIN)
@@ -383,7 +387,7 @@
         match = match_ref[oj]
         total += dot(high, match)
     for v in range(3):
-        grads[v] = total[:, 128 * v : 128 * (v + 1)]
+        grads[v, : TYPES * 16] = total[:, 128 * v : 128 * (v + 1)]
     wide[...] = jnp.zeros_like(wide)
     lane = iota((TYPES, 256), 1)
     for zl_j in range(PAIRS):
@@ -452,8 +456,8 @@
             pltpu.VMEM((WINDOWS, WIN, (HEADS + 1) * MAIN), f32),
             pltpu.VMEM((WINDOWS, WIN, (HEADS + 1) * MAIN), bf16),
             pltpu.VMEM((WINDOWS, WIN, (HEADS + 1) * MAIN), bf16),
-            pltpu.VMEM((TYPES, WIN, MAIN), f32),
-            pltpu.VMEM((2, WIN, MAIN), f32),
+            pltpu.VMEM((TYPES, TALL, MAIN), f32),
+            pltpu.VMEM((2, TALL, MAIN), f32),
             pltpu.VMEM((C, 3 * WIDTH), f32),
             pltpu.VMEM((C, C), f32),
             pltpu.VMEM((8, C), f32),
@@ -461,7 +465,7 @@
             pltpu.VMEM((C, 2 * WINDOWS * MAIN), bf16),
             pltpu.VMEM((2 * WINDOWS * MAIN, C), bf16),
             pltpu.VMEM((16, WIDE), f32),
-            pltpu.VMEM((3, TYPES * 16, 128), f32),
+            pltpu.VMEM((3, TALLER, 128), f32),
             pltpu.VMEM((B_TILES * 16, 128), f32),
             pltpu.VMEM((PARTS, 16, 128 * W_SLOTS), bf16),
             pltpu.VMEM((PARTS, 16, 128), bf16),

time: 68.4 us -> 68.4 us (level)
  no operation moved by 1% of the time
where the time goes in v9:
time: 68.4 us; the launch traced here: 68 us
  starting transfers between devices  27.2 us (40%)
  Pallas kernels  18.3 us (27%)
  blocking collectives  14.4 us (21%)
  waiting for transfers between devices  7.43 us (11%)
  between operations  0.73 us (1%)
    all_to_all x2, starting transfers between devices, exchange(): lax.all_to_all(blocks, axes, 0, 0, tiled=True, axis_index_groups=[order])  15.9 us
    all_to_all x1, blocking collectives, exchange(): lax.all_to_all(blocks, axes, 0, 0, tiled=True, axis_index_groups=[order])  14.4 us
    pallas_call x1, Pallas kernels, main(): pl.pallas_call(main_kernel, out_shape=(jax.ShapeDtypeStruct((WINDOWS * WI...  8.43 us
    all_to_all x2, waiting for transfers between devices, exchange(): lax.all_to_all(blocks, axes, 0, 0, tiled=True, axis_index_groups=[order])  5.3 us
    pallas_call x1, Pallas kernels, prepare(): pl.pallas_call(prepare_kernel, out_shape=(jax.ShapeDtypeStruct((TYPES, WI...  3.91 us
    ppermute x1, starting transfers between devices, on_device(): lat_in = lax.ppermute(to_lat, lat_axes, lat_down)  3.32 us
    ppermute x1, starting transfers between devices, on_device(): corner_in = lax.ppermute(to_corner, both, corner_down)  2.23 us
    pallas_call x1, Pallas kernels, norm_grads(): pl.pallas_call(norm_kernel, out_shape=jax.ShapeDtypeStruct(x.shape, bf16)...  1.86 us
  transfers between devices with their start and end apart: 8, of which 4 were waited for; matrix products, arithmetic and copies ran while one was open for 0% of the time, Pallas kernels for 10%

profile of v9, /device:TPU:1, one launch (start us, length us, event | category | flops | bytes accessed | tf_op | source)
XLA Modules:
  0.0 68.0 jit_solution(14047071429656312611)
XLA Ops:
  0.6 1.4 %pack.1 = (bf16[3,24,384]{2,1,0:T(8,128)(2,1)S(1)}, bf16[3,24,384]{2,1,0:T(8,128)(2,1)S(1)}, bf16[3,120,384]{2,1,0:T(8,128)(2,1)S(1)}) custom-call(bf16[6,36,4,192]{3,2,1,0:T(4,128)(2,1)} %bitcast.11, bf16[6,36,4,192]{3,2,1,0:T(4,128)(2,1)} %bitcast.14), custom_call_target="tpu_custom_call" | custom-call | tf_op jit(solution)/shard_map/pack/pallas_call | solution.py:662
  2.0 3.3 %collective-permute-start = (bf16[3,120,384]{2,1,0:T(8,128)(2,1)S(1)}, bf16[3,120,384]{2,1,0:T(8,128)(2,1)S(1)}, u32[]{:S(2)}, u32[]{:S(2)}) collective-permute-start(bf16[3,120,384]{2,1,0:T(8,128)(2,1)S(1)} %get-tuple-element.32), channel_id=1, source_target_pairs={{0,3},{1,0},{2,1},{3,2},{4,7},{5,4},{6,5},{7,6},{8,11},{9,8},{10,9... | collective-permute-start | bytes 829448 | tf_op jit(solution)/shard_map/ppermute | solution.py:700
  5.3 1.0 %collective-permute-start.1 = (bf16[3,24,384]{2,1,0:T(8,128)(2,1)S(1)}, bf16[3,24,384]{2,1,0:T(8,128)(2,1)S(1)}, u32[]{:S(2)}, u32[]{:S(2)}) collective-permute-start(bf16[3,24,384]{2,1,0:T(8,128)(2,1)S(1)} %get-tuple-element.33), channel_id=1, source_target_pairs={{0,4},{4,0},{8,12},{12,8},{16,20},{20,16},{24,28},{28,24},{32,36},... | collective-permute-start | bytes 165896 | tf_op jit(solution)/shard_map/ppermute | solution.py:699
  6.3 2.2 %collective-permute-start.2 = (bf16[3,24,384]{2,1,0:T(8,128)(2,1)S(1)}, bf16[3,24,384]{2,1,0:T(8,128)(2,1)S(1)}, u32[]{:S(2)}, u32[]{:S(2)}) collective-permute-start(bf16[3,24,384]{2,1,0:T(8,128)(2,1)S(1)} %get-tuple-element.34), channel_id=1, source_target_pairs={{0,7},{1,4},{2,5},{3,6},{4,3},{5,0},{6,1},{7,2},{8,15},{9,12},{10,... | collective-permute-start | bytes 165896 | tf_op jit(solution)/shard_map/ppermute | solution.py:698
  8.5 3.9 %prepare.1 = (f32[12,144,128]{2,1,0:T(8,128)S(1)}, f32[2,144,128]{2,1,0:T(8,128)S(1)}, bf16[3,192,192]{2,1,0:T(8,128)(2,1)S(1)}, bf16[768,192]{1,0:T(8,128)(2,1)...) custom-call(f32[6,2,3312]{2,1,0:T(2,128)} %bitcast.18, ...), custom_call_target="tpu_custom_call" | custom-call | flops 400000000 | bytes 400000 | tf_op jit(solution)/shard_map/prepare/pallas_call | solution.py:185
  12.5 0.0 collective-permute-done.1.lon_ref
  12.5 0.0 collective-permute-done.2.corner_ref
  12.5 0.0 collective-permute-done.lat_ref
  12.5 8.4 %window_grads.1 = (bf16[864,192]{1,0:T(8,128)(2,1)S(1)}, bf16[32,16,384]{2,1,0:T(8,128)(2,1)S(1)}) custom-call(bf16[3,120,384]{2,1,0:T(8,128)(2,1)S(1)} %get-tuple-element.31.own_ref, bf16[3,120,384]{2,1,0:T(8,128)(2,1)S(1)} %collective-permute-done.lat_ref, bf16[3,24,384]{2,1,0:T(8,128)(2,1)S(1)} %collective-permute-done.1.lon_ref, ...), custom_call_target="tpu_custom_call" | custom-call | flops 20000000000 | bytes 4000000 | tf_op jit(solution)/shard_map/window_grads/pallas_call | solution.py:435
  20.9 0.0 copy-start
  21.0 0.0 copy-start.1
  21.0 14.4 %all_to_all.15.got_ref = bf16[32,16,384]{2,1,0:T(8,128)(2,1)S(1)} all-to-all(bf16[32,16,384]{2,1,0:T(8,128)(2,1)S(1)} %get-tuple-element.43), channel_id=1, replica_groups={{31,23,15,7,27,19,11,3,29,21,13,5,25,17,9,1,30,22,14,6,26,18,10,2,28,20..., dimensions={0} | all-to-all | bytes 786432 | tf_op jit(solution)/shard_map/all_to_all | solution.py:683
  35.3 0.7 %fold.1 = bf16[8,16,768]{2,1,0:T(8,128)(2,1)} custom-call(bf16[32,16,384]{2,1,0:T(8,128)(2,1)S(1)} %all_to_all.15.got_ref), custom_call_target="tpu_custom_call" | custom-call | flops 1000000 | bytes 600000 | tf_op jit(solution)/shard_map/fold/pallas_call | solution.py:714
  36.1 8.9 %all-to-all-start.1 = ((bf16[8,16,768]{2,1,0:T(8,128)(2,1)}), bf16[8,16,768]{2,1,0:T(8,128)(2,1)S(1)}, u32[]{:S(2)}, u32[]{:S(2)}) async-start(bf16[8,16,768]{2,1,0:T(8,128)(2,1)} %fold.1), calls=%async_computation.1 | async-start | bytes 393216 | tf_op jit(solution)/shard_map/all_to_all | solution.py:683
  45.0 0.3 pieces.1
  45.3 1.8 %collective-permute-start.3 = (bf16[3,120,192]{2,1,0:T(8,128)(2,1)S(1)}, bf16[3,120,192]{2,1,0:T(8,128)(2,1)S(1)}, u32[]{:S(2)}, u32[]{:S(2)}) collective-permute-start(bf16[3,120,192]{2,1,0:T(8,128)(2,1)S(1)} %get-tuple-element.44), channel_id=1, source_target_pairs={{0,1},{1,2},{2,3},{3,0},{4,5},{5,6},{6,7},{7,4},{8,9},{9,10},{10,1... | collective-permute-start | bytes 414728 | tf_op jit(solution)/shard_map/ppermute | solution.py:709
  47.0 1.5 %collective-permute-start.4 = (bf16[3,24,192]{2,1,0:T(8,128)(2,1)S(1)}, bf16[3,24,192]{2,1,0:T(8,128)(2,1)S(1)}, u32[]{:S(2)}, u32[]{:S(2)}) collective-permute-start(bf16[3,24,192]{2,1,0:T(8,128)(2,1)S(1)} %get-tuple-element.45), channel_id=1, source_target_pairs={{0,4},{4,0},{8,12},{12,8},{16,20},{20,16},{24,28},{28,24},{32,36},... | collective-permute-start | bytes 82952 | tf_op jit(solution)/shard_map/ppermute | solution.py:710
  48.6 1.4 %collective-permute-start.5 = (bf16[3,24,192]{2,1,0:T(8,128)(2,1)S(1)}, bf16[3,24,192]{2,1,0:T(8,128)(2,1)S(1)}, u32[]{:S(2)}, u32[]{:S(2)}) collective-permute-start(bf16[3,24,192]{2,1,0:T(8,128)(2,1)S(1)} %get-tuple-element.46), channel_id=1, source_target_pairs={{0,5},{1,6},{2,7},{3,4},{4,1},{5,2},{6,3},{7,0},{8,13},{9,14},{10,... | collective-permute-start | bytes 82952 | tf_op jit(solution)/shard_map/ppermute | solution.py:711
  50.0 0.5 all-to-all-done.1.got_ref
  50.5 0.8 %share.1 = bf16[32,16,384]{2,1,0:T(8,128)(2,1)} custom-call(bf16[8,16,768]{2,1,0:T(8,128)(2,1)S(1)} %all-to-all-done.1.got_ref), custom_call_target="tpu_custom_call" | custom-call | flops 1000000 | bytes 600000 | tf_op jit(solution)/shard_map/share/pallas_call | solution.py:716
  51.3 1.0 %collective-permute-done.4.lon_ref = bf16[3,24,192]{2,1,0:T(8,128)(2,1)S(1)} collective-permute-done((bf16[3,24,192]{2,1,0:T(8,128)(2,1)S(1)}, bf16[3,24,192]{2,1,0:T(8,128)(2,1)S(1)}, u32[]{:S(2)}, u32[]{:S(2)}) %collective-permute-start.4) | collective-permute-done | bytes 27680 | tf_op jit(solution)/shard_map/ppermute | solution.py:710
  52.4 1.1 %collective-permute-done.5.corner_ref = bf16[3,24,192]{2,1,0:T(8,128)(2,1)S(1)} collective-permute-done((bf16[3,24,192]{2,1,0:T(8,128)(2,1)S(1)}, bf16[3,24,192]{2,1,0:T(8,128)(2,1)S(1)}, u32[]{:S(2)}, u32[]{:S(2)}) %collective-permute-start.5) | collective-permute-done | bytes 27680 | tf_op jit(solution)/shard_map/ppermute | solution.py:711
  53.5 0.0 collective-permute-done.3.lat_ref
  53.5 7.0 %all-to-all-start.2 = ((bf16[32,16,384]{2,1,0:T(8,128)(2,1)}), bf16[32,16,384]{2,1,0:T(8,128)(2,1)S(1)}, u32[]{:S(2)}, u32[]{:S(2)}) async-start(bf16[32,16,384]{2,1,0:T(8,128)(2,1)} %share.1), calls=%async_computation.2 | async-start | bytes 786432 | tf_op jit(solution)/shard_map/all_to_all | solution.py:683
  60.4 0.0 copy-done
  60.4 0.0 copy-done.1
  60.4 1.9 %norm_grads.1 = bf16[6,36,4,192]{3,2,1,0:T(4,128)(2,1)} custom-call(bf16[6,36,4,192]{3,2,1,0:T(4,128)(2,1)S(1)} %bitcast.13, bf16[6,36,4,192]{3,2,1,0:T(4,128)(2,1)S(1)} %bitcast.16, f32[1,192]{1,0:T(1,128)S(1)} %get-tuple-element.30.gain_ref, bf16[3,120,192]{2,1,0:T(8,128)(2,1)S(1)} %get-tuple-element.42.own_ref, ...), custom_call_target="tpu_custom_call" | custom-call | flops 10000000 | bytes 1500000 | tf_op jit(solution)/shard_map/norm_grads/pallas_call | solution.py:537
  62.3 4.8 %all-to-all-done.2.parts_ref = bf16[32,16,384]{2,1,0:T(8,128)(2,1)S(1)} async-done(((bf16[32,16,384]{2,1,0:T(8,128)(2,1)}), bf16[32,16,384]{2,1,0:T(8,128)(2,1)S(1)}, u32[]{:S(2)}, u32[]{:S(2)}) %all-to-all-start.2) | async-done | bytes 393248 | tf_op jit(solution)/shard_map/all_to_all | solution.py:683
  67.1 0.9 %unpack.1 = (f32[1,192]{1,0:T(1,128)}, f32[192,576]{1,0:T(8,128)}, f32[192,192]{1,0:T(8,128)}, f32[6,2,3312]{2,1,0:T(2,128)}) custom-call(bf16[32,16,384]{2,1,0:T(8,128)(2,1)S(1)} %all-to-all-done.2.parts_ref), custom_call_target="tpu_custom_call" | custom-call | tf_op jit(solution)/shard_map/unpack/pallas_call | solution.py:579
Async XLA Ops:
  2.0 10.5 %collective-permute-start = (bf16[3,120,384]{2,1,0:T(8,128)(2,1)S(1)}, bf16[3,120,384]{2,1,0:T(8,128)(2,1)S(1)}, u32[]{:S(2)}, u32[]{:S(2)}) collective-permute-start(bf16[3,120,384]{2,1,0:T(8,128)(2,1)S(1)} %get-tuple-element.32), channel_id=1, source_target_pairs={{0,3},{1,0},{2,1},{3,2},{4,7},{5,4},{6,5},{7,6},{8,11},{9,8},{10,9... | collective-permute-start | bytes 829448 | tf_op jit(solution)/shard_map/ppermute | solution.py:700
  5.3 7.2 %collective-permute-start.1 = (bf16[3,24,384]{2,1,0:T(8,128)(2,1)S(1)}, bf16[3,24,384]{2,1,0:T(8,128)(2,1)S(1)}, u32[]{:S(2)}, u32[]{:S(2)}) collective-permute-start(bf16[3,24,384]{2,1,0:T(8,128)(2,1)S(1)} %get-tuple-element.33), channel_id=1, source_target_pairs={{0,4},{4,0},{8,12},{12,8},{16,20},{20,16},{24,28},{28,24},{32,36},... | collective-permute-start | bytes 165896 | tf_op jit(solution)/shard_map/ppermute | solution.py:699
  6.3 6.2 %collective-permute-start.2 = (bf16[3,24,384]{2,1,0:T(8,128)(2,1)S(1)}, bf16[3,24,384]{2,1,0:T(8,128)(2,1)S(1)}, u32[]{:S(2)}, u32[]{:S(2)}) collective-permute-start(bf16[3,24,384]{2,1,0:T(8,128)(2,1)S(1)} %get-tuple-element.34), channel_id=1, source_target_pairs={{0,7},{1,4},{2,5},{3,6},{4,3},{5,0},{6,1},{7,2},{8,15},{9,12},{10,... | collective-permute-start | bytes 165896 | tf_op jit(solution)/shard_map/ppermute | solution.py:698
  20.9 39.5 %copy-start = (bf16[4,6,36,192]{3,0,2,1:T(4,128)(2,1)S(1)}, bf16[4,6,36,192]{3,0,2,1:T(4,128)(2,1)}, u32[]{:S(2)}) copy-start(bf16[4,6,36,192]{3,0,2,1:T(4,128)(2,1)} %param.6) | copy-start | bytes 995332
  21.0 39.5 %copy-start.1 = (bf16[4,6,36,192]{3,0,2,1:T(4,128)(2,1)S(1)}, bf16[4,6,36,192]{3,0,2,1:T(4,128)(2,1)}, u32[]{:S(2)}) copy-start(bf16[4,6,36,192]{3,0,2,1:T(4,128)(2,1)} %param.7) | copy-start | bytes 995332
  36.1 14.5 %all-to-all-start.1 = ((bf16[8,16,768]{2,1,0:T(8,128)(2,1)}), bf16[8,16,768]{2,1,0:T(8,128)(2,1)S(1)}, u32[]{:S(2)}, u32[]{:S(2)}) async-start(bf16[8,16,768]{2,1,0:T(8,128)(2,1)} %fold.1), calls=%async_computation.1 | async-start | bytes 393216 | tf_op jit(solution)/shard_map/all_to_all | solution.py:683
  45.3 8.2 %collective-permute-start.3 = (bf16[3,120,192]{2,1,0:T(8,128)(2,1)S(1)}, bf16[3,120,192]{2,1,0:T(8,128)(2,1)S(1)}, u32[]{:S(2)}, u32[]{:S(2)}) collective-permute-start(bf16[3,120,192]{2,1,0:T(8,128)(2,1)S(1)} %get-tuple-element.44), channel_id=1, source_target_pairs={{0,1},{1,2},{2,3},{3,0},{4,5},{5,6},{6,7},{7,4},{8,9},{9,10},{10,1... | collective-permute-start | bytes 414728 | tf_op jit(solution)/shard_map/ppermute | solution.py:709
  47.0 5.3 %collective-permute-start.4 = (bf16[3,24,192]{2,1,0:T(8,128)(2,1)S(1)}, bf16[3,24,192]{2,1,0:T(8,128)(2,1)S(1)}, u32[]{:S(2)}, u32[]{:S(2)}) collective-permute-start(bf16[3,24,192]{2,1,0:T(8,128)(2,1)S(1)} %get-tuple-element.45), channel_id=1, source_target_pairs={{0,4},{4,0},{8,12},{12,8},{16,20},{20,16},{24,28},{28,24},{32,36},... | collective-permute-start | bytes 82952 | tf_op jit(solution)/shard_map/ppermute | solution.py:710
  48.6 4.9 %collective-permute-start.5 = (bf16[3,24,192]{2,1,0:T(8,128)(2,1)S(1)}, bf16[3,24,192]{2,1,0:T(8,128)(2,1)S(1)}, u32[]{:S(2)}, u32[]{:S(2)}) collective-permute-start(bf16[3,24,192]{2,1,0:T(8,128)(2,1)S(1)} %get-tuple-element.46), channel_id=1, source_target_pairs={{0,5},{1,6},{2,7},{3,4},{4,1},{5,2},{6,3},{7,0},{8,13},{9,14},{10,... | collective-permute-start | bytes 82952 | tf_op jit(solution)/shard_map/ppermute | solution.py:711
  53.5 13.6 %all-to-all-start.2 = ((bf16[32,16,384]{2,1,0:T(8,128)(2,1)}), bf16[32,16,384]{2,1,0:T(8,128)(2,1)S(1)}, u32[]{:S(2)}, u32[]{:S(2)}) async-start(bf16[32,16,384]{2,1,0:T(8,128)(2,1)} %share.1), calls=%async_computation.2 | async-start | bytes 786432 | tf_op jit(solution)/shard_map/all_to_all | solution.py:683

commit v10 on v9

--- a/solution.py
+++ b/solution.py
@@ -28,7 +28,7 @@
 GROUP = ("y", "xh", "xl", "c")
 REST = "z"
 PARTS = 32
-ORDER = [31 - (y * 8 + xh * 4 + xl * 2 + c) for c in range(2) for xl in range(2) for xh in range(2) for y in range(4)]
+ORDER = [31 - (y * 8 + xh * 4 + xl * 2 + c) for c in range(2) for xh in range(2) for xl in range(2) for y in range(4)]
 SLOTS = 3
 W_TILES = 72
 W_SLOTS = 2

time: 68.4 us -> 69.1 us (1.010)
  waiting for transfers between devices: 7.43 us -> 9.42 us
  starting transfers between devices: 27.2 us -> 25.3 us
    ppermute x1, starting transfers between devices: 1.52 us -> 3.55 us  [on_device(): lax.ppermute(to_lon, lon_axes, lon_swap)]
    ppermute x1, starting transfers between devices: 1.78 us -> 0.08 us  [on_device(): lax.ppermute(to_lat, lat_axes, lat_up)]
    all_to_all x2, waiting for transfers between devices: 5.3 us -> 6.85 us  [exchange(): lax.all_to_all(blocks, axes, 0, 0, tiled=True, axis_index_groups=[order])]
    ppermute x1, starting transfers between devices: 1.43 us -> 0.01 us  [on_device(): lax.ppermute(to_corner, both, corner_up)]
    all_to_all x2, starting transfers between devices: 15.9 us -> 15.1 us  [exchange(): lax.all_to_all(blocks, axes, 0, 0, tiled=True, axis_index_groups=[order])]
where the time goes in v10:
time: 69.1 us; the launch traced here: 68.7 us
  starting transfers between devices  25.3 us (37%)
  Pallas kernels  18.3 us (26%)
  blocking collectives  14.9 us (22%)
  waiting for transfers between devices  9.42 us (14%)
  between operations  0.74 us (1%)
    all_to_all x2, starting transfers between devices, exchange(): lax.all_to_all(blocks, axes, 0, 0, tiled=True, axis_index_groups=[order])  15.1 us
    all_to_all x1, blocking collectives, exchange(): lax.all_to_all(blocks, axes, 0, 0, tiled=True, axis_index_groups=[order])  14.9 us
    pallas_call x1, Pallas kernels, main(): pl.pallas_call(main_kernel, out_shape=(jax.ShapeDtypeStruct((WINDOWS * WI...  8.43 us
    all_to_all x2, waiting for transfers between devices, exchange(): lax.all_to_all(blocks, axes, 0, 0, tiled=True, axis_index_groups=[order])  6.85 us
    pallas_call x1, Pallas kernels, prepare(): pl.pallas_call(prepare_kernel, out_shape=(jax.ShapeDtypeStruct((TYPES, WI...  3.91 us
    ppermute x1, starting transfers between devices, on_device(): lax.ppermute(to_lon, lon_axes, lon_swap)  3.55 us
    ppermute x1, starting transfers between devices, on_device(): lat_in = lax.ppermute(to_lat, lat_axes, lat_down)  3.32 us
    ppermute x1, starting transfers between devices, on_device(): corner_in = lax.ppermute(to_corner, both, corner_down)  2.23 us
  transfers between devices with their start and end apart: 8, of which 4 were waited for; matrix products, arithmetic and copies ran while one was open for 0% of the time, Pallas kernels for 10%

profile of v10, /device:TPU:1, one launch (start us, length us, event | category | flops | bytes accessed | tf_op | source)
XLA Modules:
  0.0 68.7 jit_solution(15523163857188765263)
XLA Ops:
  0.6 1.4 %pack.1 = (bf16[3,24,384]{2,1,0:T(8,128)(2,1)S(1)}, bf16[3,24,384]{2,1,0:T(8,128)(2,1)S(1)}, bf16[3,120,384]{2,1,0:T(8,128)(2,1)S(1)}) custom-call(bf16[6,36,4,192]{3,2,1,0:T(4,128)(2,1)} %bitcast.11, bf16[6,36,4,192]{3,2,1,0:T(4,128)(2,1)} %bitcast.14), custom_call_target="tpu_custom_call" | custom-call | tf_op jit(solution)/shard_map/pack/pallas_call | solution.py:662
  2.0 3.3 %collective-permute-start = (bf16[3,120,384]{2,1,0:T(8,128)(2,1)S(1)}, bf16[3,120,384]{2,1,0:T(8,128)(2,1)S(1)}, u32[]{:S(2)}, u32[]{:S(2)}) collective-permute-start(bf16[3,120,384]{2,1,0:T(8,128)(2,1)S(1)} %get-tuple-element.32), channel_id=1, source_target_pairs={{0,3},{1,0},{2,1},{3,2},{4,7},{5,4},{6,5},{7,6},{8,11},{9,8},{10,9... | collective-permute-start | bytes 829448 | tf_op jit(solution)/shard_map/ppermute | solution.py:700
  5.3 1.0 %collective-permute-start.1 = (bf16[3,24,384]{2,1,0:T(8,128)(2,1)S(1)}, bf16[3,24,384]{2,1,0:T(8,128)(2,1)S(1)}, u32[]{:S(2)}, u32[]{:S(2)}) collective-permute-start(bf16[3,24,384]{2,1,0:T(8,128)(2,1)S(1)} %get-tuple-element.33), channel_id=1, source_target_pairs={{0,4},{4,0},{8,12},{12,8},{16,20},{20,16},{24,28},{28,24},{32,36},... | collective-permute-start | bytes 165896 | tf_op jit(solution)/shard_map/ppermute | solution.py:699
  6.3 2.2 %collective-permute-start.2 = (bf16[3,24,384]{2,1,0:T(8,128)(2,1)S(1)}, bf16[3,24,384]{2,1,0:T(8,128)(2,1)S(1)}, u32[]{:S(2)}, u32[]{:S(2)}) collective-permute-start(bf16[3,24,384]{2,1,0:T(8,128)(2,1)S(1)} %get-tuple-element.34), channel_id=1, source_target_pairs={{0,7},{1,4},{2,5},{3,6},{4,3},{5,0},{6,1},{7,2},{8,15},{9,12},{10,... | collective-permute-start | bytes 165896 | tf_op jit(solution)/shard_map/ppermute | solution.py:698
  8.5 3.9 %prepare.1 = (f32[12,144,128]{2,1,0:T(8,128)S(1)}, f32[2,144,128]{2,1,0:T(8,128)S(1)}, bf16[3,192,192]{2,1,0:T(8,128)(2,1)S(1)}, bf16[768,192]{1,0:T(8,128)(2,1)...) custom-call(f32[6,2,3312]{2,1,0:T(2,128)} %bitcast.18, ...), custom_call_target="tpu_custom_call" | custom-call | flops 400000000 | bytes 400000 | tf_op jit(solution)/shard_map/prepare/pallas_call | solution.py:185
  12.5 0.0 collective-permute-done.1.lon_ref
  12.5 0.0 collective-permute-done.2.corner_ref
  12.5 0.0 collective-permute-done.lat_ref
  12.5 8.4 %window_grads.1 = (bf16[864,192]{1,0:T(8,128)(2,1)S(1)}, bf16[32,16,384]{2,1,0:T(8,128)(2,1)S(1)}) custom-call(bf16[3,120,384]{2,1,0:T(8,128)(2,1)S(1)} %get-tuple-element.31.own_ref, bf16[3,120,384]{2,1,0:T(8,128)(2,1)S(1)} %collective-permute-done.lat_ref, bf16[3,24,384]{2,1,0:T(8,128)(2,1)S(1)} %collective-permute-done.1.lon_ref, ...), custom_call_target="tpu_custom_call" | custom-call | flops 20000000000 | bytes 4000000 | tf_op jit(solution)/shard_map/window_grads/pallas_call | solution.py:435
  20.9 0.0 copy-start
  21.0 0.0 copy-start.1
  21.0 14.9 %all_to_all.15.got_ref = bf16[32,16,384]{2,1,0:T(8,128)(2,1)S(1)} all-to-all(bf16[32,16,384]{2,1,0:T(8,128)(2,1)S(1)} %get-tuple-element.43), channel_id=1, replica_groups={{31,23,15,7,29,21,13,5,27,19,11,3,25,17,9,1,30,22,14,6,28,20,12,4,26,18..., dimensions={0} | all-to-all | bytes 786432 | tf_op jit(solution)/shard_map/all_to_all | solution.py:683
  35.9 0.7 %fold.1 = bf16[8,16,768]{2,1,0:T(8,128)(2,1)} custom-call(bf16[32,16,384]{2,1,0:T(8,128)(2,1)S(1)} %all_to_all.15.got_ref), custom_call_target="tpu_custom_call" | custom-call | flops 1000000 | bytes 600000 | tf_op jit(solution)/shard_map/fold/pallas_call | solution.py:714
  36.6 8.9 %all-to-all-start.1 = ((bf16[8,16,768]{2,1,0:T(8,128)(2,1)}), bf16[8,16,768]{2,1,0:T(8,128)(2,1)S(1)}, u32[]{:S(2)}, u32[]{:S(2)}) async-start(bf16[8,16,768]{2,1,0:T(8,128)(2,1)} %fold.1), calls=%async_computation.1 | async-start | bytes 393216 | tf_op jit(solution)/shard_map/all_to_all | solution.py:683
  45.5 0.3 pieces.1
  45.8 0.1 collective-permute-start.3
  45.9 3.6 %collective-permute-start.4 = (bf16[3,24,192]{2,1,0:T(8,128)(2,1)S(1)}, bf16[3,24,192]{2,1,0:T(8,128)(2,1)S(1)}, u32[]{:S(2)}, u32[]{:S(2)}) collective-permute-start(bf16[3,24,192]{2,1,0:T(8,128)(2,1)S(1)} %get-tuple-element.45), channel_id=1, source_target_pairs={{0,4},{4,0},{8,12},{12,8},{16,20},{20,16},{24,28},{28,24},{32,36},... | collective-permute-start | bytes 82952 | tf_op jit(solution)/shard_map/ppermute | solution.py:710
  49.5 0.0 collective-permute-start.5
  49.5 1.5 %all-to-all-done.1.got_ref = bf16[8,16,768]{2,1,0:T(8,128)(2,1)S(1)} async-done(((bf16[8,16,768]{2,1,0:T(8,128)(2,1)}), bf16[8,16,768]{2,1,0:T(8,128)(2,1)S(1)}, u32[]{:S(2)}, u32[]{:S(2)}) %all-to-all-start.1) | async-done | bytes 196640 | tf_op jit(solution)/shard_map/all_to_all | solution.py:683
  51.0 0.8 %share.1 = bf16[32,16,384]{2,1,0:T(8,128)(2,1)} custom-call(bf16[8,16,768]{2,1,0:T(8,128)(2,1)S(1)} %all-to-all-done.1.got_ref), custom_call_target="tpu_custom_call" | custom-call | flops 1000000 | bytes 600000 | tf_op jit(solution)/shard_map/share/pallas_call | solution.py:716
  51.8 1.5 %collective-permute-done.4.lon_ref = bf16[3,24,192]{2,1,0:T(8,128)(2,1)S(1)} collective-permute-done((bf16[3,24,192]{2,1,0:T(8,128)(2,1)S(1)}, bf16[3,24,192]{2,1,0:T(8,128)(2,1)S(1)}, u32[]{:S(2)}, u32[]{:S(2)}) %collective-permute-start.4) | collective-permute-done | bytes 27680 | tf_op jit(solution)/shard_map/ppermute | solution.py:710
  53.3 1.1 %collective-permute-done.5.corner_ref = bf16[3,24,192]{2,1,0:T(8,128)(2,1)S(1)} collective-permute-done((bf16[3,24,192]{2,1,0:T(8,128)(2,1)S(1)}, bf16[3,24,192]{2,1,0:T(8,128)(2,1)S(1)}, u32[]{:S(2)}, u32[]{:S(2)}) %collective-permute-start.5) | collective-permute-done | bytes 27680 | tf_op jit(solution)/shard_map/ppermute | solution.py:711
  54.4 0.0 collective-permute-done.3.lat_ref
  54.4 6.2 %all-to-all-start.2 = ((bf16[32,16,384]{2,1,0:T(8,128)(2,1)}), bf16[32,16,384]{2,1,0:T(8,128)(2,1)S(1)}, u32[]{:S(2)}, u32[]{:S(2)}) async-start(bf16[32,16,384]{2,1,0:T(8,128)(2,1)} %share.1), calls=%async_computation.2 | async-start | bytes 786432 | tf_op jit(solution)/shard_map/all_to_all | solution.py:683
  60.6 0.0 copy-done
  60.6 0.0 copy-done.1
  60.6 1.9 %norm_grads.1 = bf16[6,36,4,192]{3,2,1,0:T(4,128)(2,1)} custom-call(bf16[6,36,4,192]{3,2,1,0:T(4,128)(2,1)S(1)} %bitcast.13, bf16[6,36,4,192]{3,2,1,0:T(4,128)(2,1)S(1)} %bitcast.16, f32[1,192]{1,0:T(1,128)S(1)} %get-tuple-element.30.gain_ref, bf16[3,120,192]{2,1,0:T(8,128)(2,1)S(1)} %get-tuple-element.42.own_ref, ...), custom_call_target="tpu_custom_call" | custom-call | flops 10000000 | bytes 1500000 | tf_op jit(solution)/shard_map/norm_grads/pallas_call | solution.py:537
  62.5 5.3 %all-to-all-done.2.parts_ref = bf16[32,16,384]{2,1,0:T(8,128)(2,1)S(1)} async-done(((bf16[32,16,384]{2,1,0:T(8,128)(2,1)}), bf16[32,16,384]{2,1,0:T(8,128)(2,1)S(1)}, u32[]{:S(2)}, u32[]{:S(2)}) %all-to-all-start.2) | async-done | bytes 393248 | tf_op jit(solution)/shard_map/all_to_all | solution.py:683
  67.8 0.9 %unpack.1 = (f32[1,192]{1,0:T(1,128)}, f32[192,576]{1,0:T(8,128)}, f32[192,192]{1,0:T(8,128)}, f32[6,2,3312]{2,1,0:T(2,128)}) custom-call(bf16[32,16,384]{2,1,0:T(8,128)(2,1)S(1)} %all-to-all-done.2.parts_ref), custom_call_target="tpu_custom_call" | custom-call | tf_op jit(solution)/shard_map/unpack/pallas_call | solution.py:579
Async XLA Ops:
  2.0 10.5 %collective-permute-start = (bf16[3,120,384]{2,1,0:T(8,128)(2,1)S(1)}, bf16[3,120,384]{2,1,0:T(8,128)(2,1)S(1)}, u32[]{:S(2)}, u32[]{:S(2)}) collective-permute-start(bf16[3,120,384]{2,1,0:T(8,128)(2,1)S(1)} %get-tuple-element.32), channel_id=1, source_target_pairs={{0,3},{1,0},{2,1},{3,2},{4,7},{5,4},{6,5},{7,6},{8,11},{9,8},{10,9... | collective-permute-start | bytes 829448 | tf_op jit(solution)/shard_map/ppermute | solution.py:700
  5.3 7.2 %collective-permute-start.1 = (bf16[3,24,384]{2,1,0:T(8,128)(2,1)S(1)}, bf16[3,24,384]{2,1,0:T(8,128)(2,1)S(1)}, u32[]{:S(2)}, u32[]{:S(2)}) collective-permute-start(bf16[3,24,384]{2,1,0:T(8,128)(2,1)S(1)} %get-tuple-element.33), channel_id=1, source_target_pairs={{0,4},{4,0},{8,12},{12,8},{16,20},{20,16},{24,28},{28,24},{32,36},... | collective-permute-start | bytes 165896 | tf_op jit(solution)/shard_map/ppermute | solution.py:699
  6.3 6.2 %collective-permute-start.2 = (bf16[3,24,384]{2,1,0:T(8,128)(2,1)S(1)}, bf16[3,24,384]{2,1,0:T(8,128)(2,1)S(1)}, u32[]{:S(2)}, u32[]{:S(2)}) collective-permute-start(bf16[3,24,384]{2,1,0:T(8,128)(2,1)S(1)} %get-tuple-element.34), channel_id=1, source_target_pairs={{0,7},{1,4},{2,5},{3,6},{4,3},{5,0},{6,1},{7,2},{8,15},{9,12},{10,... | collective-permute-start | bytes 165896 | tf_op jit(solution)/shard_map/ppermute | solution.py:698
  20.9 39.6 %copy-start = (bf16[4,6,36,192]{3,0,2,1:T(4,128)(2,1)S(1)}, bf16[4,6,36,192]{3,0,2,1:T(4,128)(2,1)}, u32[]{:S(2)}) copy-start(bf16[4,6,36,192]{3,0,2,1:T(4,128)(2,1)} %param.6) | copy-start | bytes 995332
  21.0 39.6 %copy-start.1 = (bf16[4,6,36,192]{3,0,2,1:T(4,128)(2,1)S(1)}, bf16[4,6,36,192]{3,0,2,1:T(4,128)(2,1)}, u32[]{:S(2)}) copy-start(bf16[4,6,36,192]{3,0,2,1:T(4,128)(2,1)} %param.7) | copy-start | bytes 995332
  36.6 14.4 %all-to-all-start.1 = ((bf16[8,16,768]{2,1,0:T(8,128)(2,1)}), bf16[8,16,768]{2,1,0:T(8,128)(2,1)S(1)}, u32[]{:S(2)}, u32[]{:S(2)}) async-start(bf16[8,16,768]{2,1,0:T(8,128)(2,1)} %fold.1), calls=%async_computation.1 | async-start | bytes 393216 | tf_op jit(solution)/shard_map/all_to_all | solution.py:683
  45.8 8.5 %collective-permute-start.3 = (bf16[3,120,192]{2,1,0:T(8,128)(2,1)S(1)}, bf16[3,120,192]{2,1,0:T(8,128)(2,1)S(1)}, u32[]{:S(2)}, u32[]{:S(2)}) collective-permute-start(bf16[3,120,192]{2,1,0:T(8,128)(2,1)S(1)} %get-tuple-element.44), channel_id=1, source_target_pairs={{0,1},{1,2},{2,3},{3,0},{4,5},{5,6},{6,7},{7,4},{8,9},{9,10},{10,1... | collective-permute-start | bytes 414728 | tf_op jit(solution)/shard_map/ppermute | solution.py:709
  45.9 7.4 %collective-permute-start.4 = (bf16[3,24,192]{2,1,0:T(8,128)(2,1)S(1)}, bf16[3,24,192]{2,1,0:T(8,128)(2,1)S(1)}, u32[]{:S(2)}, u32[]{:S(2)}) collective-permute-start(bf16[3,24,192]{2,1,0:T(8,128)(2,1)S(1)} %get-tuple-element.45), channel_id=1, source_target_pairs={{0,4},{4,0},{8,12},{12,8},{16,20},{20,16},{24,28},{28,24},{32,36},... | collective-permute-start | bytes 82952 | tf_op jit(solution)/shard_map/ppermute | solution.py:710
  49.5 4.9 %collective-permute-start.5 = (bf16[3,24,192]{2,1,0:T(8,128)(2,1)S(1)}, bf16[3,24,192]{2,1,0:T(8,128)(2,1)S(1)}, u32[]{:S(2)}, u32[]{:S(2)}) collective-permute-start(bf16[3,24,192]{2,1,0:T(8,128)(2,1)S(1)} %get-tuple-element.46), channel_id=1, source_target_pairs={{0,5},{1,6},{2,7},{3,4},{4,1},{5,2},{6,3},{7,0},{8,13},{9,14},{10,... | collective-permute-start | bytes 82952 | tf_op jit(solution)/shard_map/ppermute | solution.py:711
  54.4 13.4 %all-to-all-start.2 = ((bf16[32,16,384]{2,1,0:T(8,128)(2,1)}), bf16[32,16,384]{2,1,0:T(8,128)(2,1)S(1)}, u32[]{:S(2)}, u32[]{:S(2)}) async-start(bf16[32,16,384]{2,1,0:T(8,128)(2,1)} %share.1), calls=%async_computation.2 | async-start | bytes 786432 | tf_op jit(solution)/shard_map/all_to_all | solution.py:683
